TPU v7x, 128 devices: a whole 4x4x4 slice. The times are simulated.
128 devices in a mesh: dp: 8 (over z, core), cent: 16 (over y, x).
Axes of the slice: x: 4, y: 4, z: 4, core: 2. Of those that a mesh axis runs over, the one named last changes fastest.
Arguments:
- embeddings: bfloat16 [16384, 128], P(('dp', 'cent')), may hold values from -6 to 6
- centroids: bfloat16 [131072, 128], P('cent'), may hold values from -6 to 6
- col_mass: float32 [131072], P('cent'), may hold values from 0.3 to 3
- assignments: int32 [2, 16384], P(None, ('dp', 'cent')), may hold values from 0 to 131071, as said below
Outputs:
- new_centroids: bfloat16 [131072, 128], P('cent')
- assign_mass: float32 [2, 16384], P(None, ('dp', 'cent'))
- residuals: bfloat16 [16384, 128], P(('dp', 'cent'))
Inputs may be any that keep to these rules, and one draw needn't show every extreme that they name: `assignments`: centroid k is owned by the device at cent index k // 8192 and dp index (k % 8192) // 1024. In each iteration, the 128 tokens of one device name centroids of exactly 64 distinct owners, 2 tokens each; in each iteration some owner gets 2 tokens from every device.
All inputs are finite; a program needn't handle non-finite values.
Results may differ from a plain program's by a relative error of at most 0.025.
Values may be sent and summed in bfloat16 or wider, within the bound.
No kernel may reach another device: no remote copies, remote signals or barrier semaphores. Data moves between devices by JAX's collectives and lax.ppermute only.
A program may use at most 64 MiB of HBM per device.

v0:
```python
import jax
import jax.numpy as jnp
from jax import lax
from jax.sharding import PartitionSpec as P

softness_factor = 0.05
prior_weight = 1.0


def unit_rows(x):
    xf = x.astype(jnp.float32)
    return xf * lax.rsqrt(jnp.sum(xf * xf, axis=1, keepdims=True) + 1e-06)


def tile_scores(block, cents):
    unscaled_logits = lax.dot_general(
        block, cents, (((1,), (1,)), ((), ())), preferred_element_type=jnp.float32
    )
    return jnp.exp(unscaled_logits / softness_factor)


def marginals(rows_all, cents, column_potential, target):
    count = rows_all.shape[0]
    blocks = rows_all.reshape(count // 512, 512, rows_all.shape[1])

    def row_pass(blk):
        return jnp.sum(tile_scores(blk, cents) * column_potential, axis=1)

    row_part = lax.map(row_pass, blocks).reshape(count)
    row_potential = 1.0 / lax.psum(row_part, "cent")

    def column_step(carry, pair):
        blk, scale = pair
        return (carry + jnp.sum(tile_scores(blk, cents) * scale[:, None], axis=0), None)

    col_part, _ = lax.scan(
        column_step,
        jnp.zeros((cents.shape[0],), jnp.float32),
        (blocks, row_potential.reshape(count // 512, 512)),
    )
    v_cols = target / lax.psum(col_part.astype(jnp.bfloat16), "dp").astype(jnp.float32)
    return (row_potential, v_cols)


def on_device(embeddings, centroids, col_mass, assignments):
    tok_local, width = embeddings.shape
    cent_local = centroids.shape[0]
    iters = assignments.shape[0]
    n_dp = lax.axis_size("dp")
    n_cent = lax.axis_size("cent")
    owner_devices = n_dp * n_cent
    centroid_count = cent_local * n_cent
    target = col_mass * (tok_local * owner_devices / centroid_count)
    cent_index = lax.axis_index("cent")
    xn = unit_rows(embeddings).astype(jnp.bfloat16)
    cents = unit_rows(centroids).astype(jnp.bfloat16)
    column_potential = jnp.ones((cent_local,), jnp.float32)
    rows_all, group_picks = (
        lax.all_gather(xn, "cent", axis=0, tiled=True),
        lax.all_gather(assignments, "cent", axis=1, tiled=True),
    )
    rows_f32 = rows_all.astype(jnp.float32)
    parts = []
    for step in range(iters):
        row_potential, column_potential = marginals(rows_all, cents, column_potential, target)
        picked_centroids = group_picks[step]
        within_range = picked_centroids // cent_local == cent_index
        local_centroid = jnp.where(within_range, picked_centroids % cent_local, 0)
        picked = cents[local_centroid].astype(jnp.float32)
        affinity_value = jnp.sum(rows_f32 * picked, axis=1)
        transport_weight = jnp.where(
            within_range,
            centroid_count
            * jnp.exp(affinity_value / softness_factor)
            * row_potential
            * column_potential[local_centroid],
            0.0,
        )
        target_rows = jnp.where(within_range, local_centroid, cent_local)
        acc = (
            jnp.zeros((cent_local, width), jnp.float32)
            .at[target_rows]
            .add(transport_weight[:, None] * rows_f32, mode="drop")
        )
        acc = lax.psum(acc, "dp")
        cents = unit_rows(prior_weight * cents.astype(jnp.float32) + acc).astype(jnp.bfloat16)
        parts.append(transport_weight)
    res_part = jnp.where(
        within_range[:, None], rows_f32 - cents[local_centroid].astype(jnp.float32), 0.0
    )
    assign_mass, res_share = (
        lax.psum_scatter(
            jnp.stack(parts).astype(jnp.bfloat16), "cent", scatter_dimension=1, tiled=True
        ).astype(jnp.float32),
        lax.psum_scatter(
            res_part.astype(jnp.bfloat16), "cent", scatter_dimension=0, tiled=True
        ).astype(jnp.float32),
    )
    residuals = res_share.astype(jnp.bfloat16)
    return (cents, assign_mass, residuals)


def solution(mesh):
    in_specs = (P(("dp", "cent"), None), P("cent", None), P("cent"), P(None, ("dp", "cent")))
    out_specs = (P("cent", None), P(None, ("dp", "cent")), P(("dp", "cent"), None))
    return jax.shard_map(
        on_device, mesh=mesh, in_specs=in_specs, out_specs=out_specs, check_vma=False
    )
```

profile of v0, /device:TPU:0, one launch (start us, length us, event | category | flops | bytes accessed | tf_op | source)
XLA Modules:
  0.0 624.0 jit_solution(815603974245639700)
XLA Ops:
  7.2 0.0 all-reduce.3.cloned.1.call-start
  7.2 1.0 fusion.24
  8.3 23.7 %all_gather.6 = s32[2,2048]{1,0:T(2,128)S(1)} all-gather(s32[2,128]{1,0:T(2,128)} %param.15), channel_id=1, replica_groups=mesh['dp'=8,'cent'=16] {'cent'}, dimensions={1}, use_global_device_ids=true | all-gather | bytes 17408 | tf_op jit(solution)/shard_map/all_gather | solution.py:60
  32.0 0.8 fusion.25
  32.8 2.7 fusion.12
  35.6 0.1 compare_select_fusion.2
  35.7 23.4 %all_gather.7 = bf16[2048,128]{1,0:T(8,128)(2,1)S(1)} all-gather(bf16[128,128]{1,0:T(8,128)(2,1)S(1)} %fusion.25), channel_id=1, replica_groups=mesh['dp'=8,'cent'=16] {'cent'}, dimensions={0}, use_global_device_ids=true | all-gather | bytes 557056 | tf_op jit(solution)/shard_map/all_gather | solution.py:59
  59.1 2.2 fusion.13
  61.3 17.4 %while.42 = (s32[]{:T(128)}, f32[4,512]{1,0:T(4,128)S(1)}, bf16[4,512,128]{2,1,0:T(8,128)(2,1)S(1)}, bf16[8192,128]{1,0:T(8,128)(2,1)}, s32[]{:T(128)}, /*index=5*/s32[]{:T(128)}) while((s32[]{:T(128)}, f32[4,512]{1,0:T(4,128)S(1)}, bf16[4,512,128]{2,1,0:T(8,128)(2,1)S(1)}, bf16[8192,128]{1,0:T(8,128)(2,1)}, s32[]{:T(128)}, ...), condition=%wide.region_5.6_spmd, body=%wide.region_3.5_spmd.sunk | while | flops 1082129920 | bytes 2234453 | solution.py:29
  61.3 4.3 exponential_reduce_fusion.2
  65.5 0.1 dynamic_update_slice.9
  65.6 4.3 exponential_reduce_fusion.2
  69.9 0.1 dynamic_update_slice.9
  70.0 4.3 exponential_reduce_fusion.2
  74.2 0.1 dynamic_update_slice.9
  74.3 4.3 exponential_reduce_fusion.2
  78.6 0.1 dynamic_update_slice.9
  78.7 38.6 %psum.42 = f32[2048]{0:T(1024)S(1)} all-reduce(f32[2048]{0:T(1024)S(1)} %bitcast.96), channel_id=1, replica_groups=mesh['dp'=8,'cent'=16] {'cent'}, use_global_device_ids=true, to_apply=%region_6.7 | all-reduce | flops 2048 | bytes 16384 | tf_op jit(solution)/shard_map/psum | solution.py:30
  117.3 21.6 %while.44 = (s32[]{:T(128)}, f32[8192]{0:T(1024)S(1)}, bf16[4,512,128]{2,1,0:T(8,128)(2,1)S(1)}, bf16[8192,128]{1,0:T(8,128)(2,1)}, f32[4,512]{1,0:T(4,128)S(1)}, /*index=5*/s32[]{:T(128)}, s32[]{:T(128)}) while((s32[]{:T(128)}, f32[8192]{0:T(1024)S(1)}, bf16[4,512,128]{2,1,0:T(8,128)(2,1)S(1)}, bf16[8192,128]{1,0:T(8,128)(2,1)}, ...), condition=%wide.region_9.10_spmd.clone, body=%wide.region_7.9_spmd.clone.sunk | while | flops 1086332928 | bytes 2365543 | solution.py:36
  117.4 5.3 multiply_reduce_fusion.9
  122.8 5.3 multiply_reduce_fusion.9
  128.2 5.3 multiply_reduce_fusion.9
  133.6 5.3 multiply_reduce_fusion.9
  139.0 24.7 %psum.43 = bf16[8192]{0:T(1024)(128)(2,1)S(1)} all-reduce(bf16[8192]{0:T(1024)(128)(2,1)S(1)} %convert_element_type.64), channel_id=1, replica_groups=mesh['dp'=8,'cent'=16] {'dp'}, use_global_device_ids=true, to_apply=%region_10.11 | all-reduce | flops 8192 | bytes 32768 | tf_op jit(solution)/shard_map/psum | solution.py:41
  163.6 7.4 %gather_fusion = bf16[2048,128]{1,0:T(8,128)(2,1)S(1)} fusion(bf16[8192,128]{1,0:T(8,128)(2,1)} %get-tuple-element.404, s32[2048]{0:T(1024)S(1)} %broadcast_clamp_fusion.1), kind=kCustom, calls=%fused_computation | custom fusion | bytes 1056768 | tf_op jit(solution)/shard_map/gather | solution.py:69
  171.1 11.8 %gather_fusion.1 = f32[2048]{0:T(1024)S(1)} fusion(f32[8192]{0:T(1024)S(1)} %convert_divide_fusion.1, s32[2048]{0:T(1024)S(1)} %broadcast_clamp_fusion.1), kind=kCustom, calls=%fused_computation.1 | custom fusion | bytes 24576 | tf_op jit(solution)/shard_map/gather | solution.py:76
  182.9 0.3 fusion.18
  183.3 14.7 %scatter_custom_fusion = f32[8192,128]{1,0:T(8,128)} fusion(s32[2048]{0:T(1024)S(1)} %bitcast.102, f32[]{:T(128)} %constant.103.clone.1, bf16[2048,128]{1,0:T(8,128)(2,1)S(1)} %bitcast.83, f32[2048]{0:T(1024)S(1)} %get-tuple-element.185), kind=kCustom, calls=%fused_computation.44 | custom fusion | flops 786432 | bytes 4726788 | tf_op jit(solution)/shard_map/scatter-add | solution.py:83
  198.0 0.0 all-reduce.3.cloned.1.call-update
  198.0 0.2 all-reduce.5.cloned.1.call-start
  198.2 0.1 compare_select_fusion
  198.4 66.1 %all-reduce.3.cloned.1.call-done = f32[8192,128]{1,0:T(8,128)} async-done(((f32[8192,128]{1,0:T(8,128)}), f32[8192,128]{1,0:T(8,128)}) %all-reduce.3.cloned.1.call-update) | async-done | bytes 4194320 | tf_op jit(solution)/shard_map/psum | solution.py:85
  264.5 4.1 multiply_reduce_fusion.4
  268.6 4.5 multiply_convert_fusion.1
  273.2 14.3 %while.43 = (s32[]{:T(128)}, f32[4,512]{1,0:T(4,128)S(1)}, bf16[4,512,128]{2,1,0:T(8,128)(2,1)S(1)}, bf16[8192,128]{1,0:T(8,128)(2,1)S(1)}, f32[8192]{0:T(1024)S(1)}, /*index=5*/s32[]{:T(128)}, s32[]{:T(128)}) while((s32[]{:T(128)}, f32[4,512]{1,0:T(4,128)S(1)}, bf16[4,512,128]{2,1,0:T(8,128)(2,1)S(1)}, bf16[8192,128]{1,0:T(8,128)(2,1)S(1)}, ...), condition=%wide.region_17.18_spmd, body=%wide.region_15.17_spmd.sunk | while | flops 1086324224 | bytes 2267229 | solution.py:29
  273.2 3.5 multiply_reduce_fusion.8
  276.8 3.5 multiply_reduce_fusion.8
  280.4 3.5 multiply_reduce_fusion.8
  283.9 3.5 multiply_reduce_fusion.8
  287.5 40.9 %psum.45 = f32[2048]{0:T(1024)S(1)} all-reduce(f32[2048]{0:T(1024)S(1)} %bitcast.97), channel_id=1, replica_groups=mesh['dp'=8,'cent'=16] {'cent'}, use_global_device_ids=true, to_apply=%region_18.19 | all-reduce | flops 2048 | bytes 16384 | tf_op jit(solution)/shard_map/psum | solution.py:30
  328.4 15.2 %while.45 = (s32[]{:T(128)}, f32[8192]{0:T(1024)S(1)}, bf16[4,512,128]{2,1,0:T(8,128)(2,1)S(1)}, bf16[8192,128]{1,0:T(8,128)(2,1)S(1)}, f32[4,512]{1,0:T(4,128)S(1)}, /*index=5*/s32[]{:T(128)}, s32[]{:T(128)}) while((s32[]{:T(128)}, f32[8192]{0:T(1024)S(1)}, bf16[4,512,128]{2,1,0:T(8,128)(2,1)S(1)}, ...), condition=%wide.region_21.22_spmd.clone, body=%wide.region_19.21_spmd.clone.sunk | while | flops 1086332928 | bytes 2365543 | solution.py:36
  328.5 3.7 multiply_reduce_fusion.10
  332.3 3.7 multiply_reduce_fusion.10
  336.1 3.7 multiply_reduce_fusion.10
  339.9 3.7 multiply_reduce_fusion.10
  343.6 23.6 %psum.46 = bf16[8192]{0:T(1024)(128)(2,1)S(1)} all-reduce(bf16[8192]{0:T(1024)(128)(2,1)S(1)} %convert_element_type.69), channel_id=1, replica_groups=mesh['dp'=8,'cent'=16] {'dp'}, use_global_device_ids=true, to_apply=%region_22.23 | all-reduce | flops 8192 | bytes 32768 | tf_op jit(solution)/shard_map/psum | solution.py:41
  367.2 6.2 gather_fusion.2
  373.4 11.8 %gather_fusion.3 = f32[2048]{0:T(1024)S(1)} fusion(f32[8192]{0:T(1024)S(1)} %convert_divide_fusion, s32[2048]{0:T(1024)S(1)} %broadcast_clamp_fusion), kind=kCustom, calls=%fused_computation.3 | custom fusion | bytes 24576 | tf_op jit(solution)/shard_map/gather | solution.py:76
  385.2 0.3 fusion.19
  385.6 14.7 %scatter_custom_fusion.1 = f32[8192,128]{1,0:T(8,128)} fusion(s32[2048]{0:T(1024)S(1)} %bitcast.101, f32[]{:T(128)} %constant.103.clone.1, bf16[2048,128]{1,0:T(8,128)(2,1)S(1)} %bitcast.85, f32[2048]{0:T(1024)S(1)} %get-tuple-element.187), kind=kCustom, calls=%fused_computation.42 | custom fusion | flops 786432 | bytes 4726788 | tf_op jit(solution)/shard_map/scatter-add | solution.py:83
  400.3 0.0 all-reduce.5.cloned.1.call-update
  400.3 0.0 reduce-scatter.7.cloned.1.call-start
  400.4 1.1 copy.7
  401.5 0.0 reduce-scatter.7.cloned.1.call-update
  401.5 0.3 reduce-scatter.5.cloned.1.call-start
  401.8 64.9 %all-reduce.5.cloned.1.call-done = f32[8192,128]{1,0:T(8,128)} async-done(((f32[8192,128]{1,0:T(8,128)}), f32[8192,128]{1,0:T(8,128)}) %all-reduce.5.cloned.1.call-update) | async-done | bytes 4194320 | tf_op jit(solution)/shard_map/psum | solution.py:85
  466.7 3.5 multiply_reduce_fusion.3
  470.3 2.3 multiply_convert_fusion
  472.5 7.4 %gather_fusion.4 = bf16[2048,128]{1,0:T(8,128)(2,1)S(1)} fusion(bf16[8192,128]{1,0:T(8,128)(2,1)} %multiply_convert_fusion, s32[2048]{0:T(1024)S(1)} %broadcast_clamp_fusion), kind=kCustom, calls=%fused_computation.4 | custom fusion | bytes 1056768 | tf_op jit(solution)/shard_map/gather | solution.py:89
  480.0 1.1 fusion.21
  481.2 60.8 %reduce-scatter.7.cloned.1.call-done = bf16[128,2]{1,0:T(8,128)(2,1)} async-done(((bf16[2048,2]{1,0:T(8,128)(2,1)}), bf16[128,2]{1,0:T(8,128)(2,1)}) %reduce-scatter.7.cloned.1.call-update) | async-done | bytes 528
  542.0 0.8 copy.8
  542.8 0.6 convert_element_type.72
  543.4 74.1 %reduce-scatter.5.cloned.1.call-done = bf16[128,128]{1,0:T(8,128)(2,1)} async-done(((bf16[2048,128]{1,0:T(8,128)(2,1)}), bf16[128,128]{1,0:T(8,128)(2,1)}) %reduce-scatter.5.cloned.1.call-update) | async-done | bytes 32784 | tf_op jit(solution)/shard_map/reduce_scatter | solution.py:95
  (59 shorter events, 0.6 us)
Async XLA Ops:
  7.2 51.9 %copy-start = (bf16[8192,128]{1,0:T(8,128)(2,1)S(1)}, bf16[8192,128]{1,0:T(8,128)(2,1)}, u32[]{:S(2)}) copy-start(bf16[8192,128]{1,0:T(8,128)(2,1)} %param.13) | copy-start | bytes 6291460
  7.2 257.3 %all-reduce.3.cloned.1.call-start = ((), (), s32[]{:S(2)}) async-start(), calls=%async_computation.2 | async-start | bytes 8388608 | tf_op jit(solution)/shard_map/psum | solution.py:85
  138.9 32.1 %copy-start.4 = (f32[8192]{0:T(1024)S(1)}, f32[8192]{0:T(1024)}, u32[]{:S(2)}) copy-start(f32[8192]{0:T(1024)} %param.14) | copy-start | bytes 98308
  198.0 268.7 %all-reduce.5.cloned.1.call-start = ((), (), s32[]{:S(2)}) async-start(), calls=%async_computation.3 | async-start | bytes 8388608 | tf_op jit(solution)/shard_map/psum | solution.py:85
  264.5 4.1 copy-start.1
  264.5 4.1 copy-start.3
  400.3 141.7 %reduce-scatter.7.cloned.1.call-start = ((), (), s32[]{:S(2)}) async-start(), calls=%async_computation.5 | async-start | bytes 557056
  401.5 216.0 %reduce-scatter.5.cloned.1.call-start = ((), (), s32[]{:S(2)}) async-start(), calls=%async_computation.4 | async-start | bytes 557056 | tf_op jit(solution)/shard_map/reduce_scatter | solution.py:95
  466.7 3.5 copy-start.2
Sparse Core Ops, SparseCore 0:
  198.1 66.2 all-reduce.2
  400.4 66.2 all-reduce.4
  469.9 72.0 reduce-scatter.6
  545.9 71.5 reduce-scatter.4
where the time goes:
time: 625 us; the launch traced here: 624 us
  waiting for transfers between devices  266 us (43%)
  blocking collectives  175 us (28%)
  matrix products  67.5 us (11%)
  other arithmetic  53.4 us (9%)
  local copies, waits for them, and re-layouts  47.1 us (8%)
  between operations  14.2 us (2%)
    psum x2, waiting for transfers between devices, on_device(): acc = lax.psum(acc, 'dp')  131 us
    psum x2, blocking collectives, marginals(): row_potential = 1.0 / lax.psum(row_part, 'cent')  79.5 us
    reduce_scatter x1, waiting for transfers between devices, on_device(): lax.psum_scatter(res_part.astype(jnp.bfloat16), 'cent', scatter_dimension...  74.1 us
    dot_general x16, matrix products, tile_scores(): lax.dot_general(block, cents, (((1,), (1,)), ((), ())), preferred_element...  67.5 us
    unnamed x5, waiting for transfers between devices  60.9 us
    psum x2, blocking collectives, marginals(): lax.psum(col_part.astype(jnp.bfloat16), 'dp').astype(jnp.float32)  48.2 us
    scatter-add x2, other arithmetic, on_device(): acc = jnp.zeros((cent_local, width), jnp.float32).at[target_rows].add(tra...  29.3 us
    all_gather x1, blocking collectives, on_device(): lax.all_gather(assignments, 'cent', axis=1, tiled=True)  23.7 us
  transfers between devices with their start and end apart: 4, of which 4 were waited for; matrix products, arithmetic and copies ran while one was open for 3% of the time, Pallas kernels for 0%

commit v1 on v0

v1 whole, which is shorter than its diff:
```python
import math

import jax
import jax.numpy as jnp
from jax import lax
from jax.experimental import pallas as pl
from jax.experimental.pallas import tpu as pltpu
from jax.sharding import PartitionSpec as P

F32, BF16 = jnp.float32, jnp.bfloat16
D = 128
TOK = 128
NC, ND = 16, 8
T = TOK * NC
KC = 8192
NO, KO = 8, 1024
SL = 256
SCALE = 20.0 * math.log2(math.e)
TOKENS, CENTROIDS = 16384, 131072
TC = 256
MIB = 2**20

NN = (((1,), (0,)), ((), ()))
NT = (((1,), (1,)), ((), ()))


def mm(a, b, dims=NN):
    return lax.dot_general(a, b, dims, preferred_element_type=F32)


def iota(shape, dim):
    return lax.broadcasted_iota(jnp.int32, shape, dim)


def unit(z):
    return z * lax.rsqrt(jnp.sum(z * z, axis=1, keepdims=True) + 1e-06)


def split(z):
    hi = z.astype(BF16)
    return hi, (z - hi.astype(F32)).astype(BF16)


def column(row):
    return jnp.concatenate(
        [
            jnp.broadcast_to(row[:, i : i + 128], (128, 128)).T
            for i in range(0, row.shape[1], 128)
        ],
        axis=0,
    )


def call(body, outs, name, flops, limit, scratch=()):
    return pl.pallas_call(
        body,
        out_shape=outs,
        scratch_shapes=list(scratch),
        name=name,
        compiler_params=pltpu.CompilerParams(vmem_limit_bytes=limit * MIB),
        cost_estimate=pl.CostEstimate(
            flops=flops, bytes_accessed=2 * MIB, transcendentals=0
        ),
    )


def shape(*dims, dtype=F32):
    return jax.ShapeDtypeStruct(dims, dtype)


def pack_kernel(emb, asg, out):
    xn = unit(emb[...].astype(F32)).astype(BF16)
    rows = []
    for it in range(2):
        a = asg[it : it + 1, :]
        owner = a >> 10
        own_f = owner.astype(F32)
        same = jnp.broadcast_to(own_f, (TOK, TOK)).T == own_f
        before = iota((TOK, TOK), 0) < iota((TOK, TOK), 1)
        rank = jnp.sum(jnp.where(same & before, 1.0, 0.0), axis=0, keepdims=True)
        code = (a & (KO - 1)) + 1
        rows.append((a >> 13, code >> 5, code & 31, (owner & 7) * 2 + rank.astype(jnp.int32)))
    zero = jnp.zeros((5, TOK), jnp.int32)
    for c in range(NC):
        out[c, 0:TOK, :] = xn
        parts = []
        for shard, hi, lo, place in rows:
            mine = shard == c
            parts += [jnp.where(mine, hi, 0), jnp.where(mine, lo, 0), place, zero]
        out[c, TOK : TOK + 16, :] = jnp.concatenate(parts, axis=0).astype(F32).astype(BF16)


def unpack_kernel(asg, rec, mass_out, res_out):
    masses = []
    for it in range(2):
        a = asg[it : it + 1, :]
        owner = a >> 10
        own_f = owner.astype(F32)
        same = jnp.broadcast_to(own_f, (TOK, TOK)).T == own_f
        before = iota((TOK, TOK), 0) < iota((TOK, TOK), 1)
        rank = jnp.sum(jnp.where(same & before, 1.0, 0.0), axis=0, keepdims=True)
        place = (owner.astype(F32) * 2.0 + rank) * 1.0
        shard = a >> 13
        row = shard.astype(F32) * 16.0 + (owner & 7).astype(F32) * 2.0 + rank
        col = column(row)
        lane = iota((TOK, 128), 1).astype(F32)
        oh = jnp.concatenate(
            [jnp.where(col == lane + 128.0 * j, 1.0, 0.0) for j in range(2)], axis=1
        ).astype(BF16)
        mrows = jnp.concatenate([rec[s, 16:32, :] for s in range(NC)], axis=0)
        m = mm(oh, mrows)
        masses.append(m.T[it : it + 1, :])
        if it == 1:
            rrows = jnp.concatenate([rec[s, 0:16, :] for s in range(NC)], axis=0)
            res_out[...] = mm(oh, rrows).astype(BF16)
    mass_out[...] = jnp.concatenate(masses, axis=0)


def cent_kernel(cent, out):
    @pl.loop(0, KC // 256)
    def _(i):
        at = pl.ds(pl.multiple_of(i * 256, 256), 256)
        out[at, :] = unit(cent[at, :].astype(F32)).astype(BF16)


def score_block(x, cblk, g, acc, weight, first):
    @pl.loop(0, T // TC)
    def _(j):
        at = pl.ds(pl.multiple_of(j * TC, TC), TC)
        s = mm(x[at, :], cblk[...], NT)
        e = jnp.exp2(s * SCALE)
        g[at, :] = e.astype(BF16)
        if weight is not None:
            e = e * weight
        part = e[:, 0:128]
        for q in range(1, KO // 128):
            part = part + e[:, q * 128 : (q + 1) * 128]
        if first:
            acc[at, :] = part
        else:
            acc[at, :] += part


def finish_rows(acc, out):
    for s in range(NC):
        r = jnp.sum(acc[s * 128 : (s + 1) * 128, :].T, axis=0, keepdims=True)
        for c in range(NC):
            out[c, s : s + 1, :] = r


def first_kernel(rec, cents, *refs):
    gs, row_out, x, acc = refs[:NO], refs[NO], refs[NO + 1], refs[NO + 2]
    for s in range(NC):
        x[s * TOK : (s + 1) * TOK, :] = rec[s, 0:TOK, :]
    for o in range(NO):
        score_block(x, cents.at[o * KO : (o + 1) * KO], gs[o], acc, None, o == 0)
    finish_rows(acc, row_out)


def owner_onehot(idcol, o):
    ids = idcol[o * 32 : (o + 1) * 32, :]
    lane = iota((32, 128), 1).astype(F32)
    return jnp.concatenate(
        [jnp.where(ids == lane + (128.0 * j + 1.0), 1.0, 0.0) for j in range(KO // 128)],
        axis=1,
    ).astype(BF16)


def slot_kernel(rec, cents, p_out, xs_out, id_out, code_out, col_out, cs_out):
    me = lax.axis_index("dp")
    for it in range(2):
        base = TOK + 8 * it
        hi = jnp.concatenate([rec[s, base : base + 1, :] for s in range(NC)], axis=1)
        lo = jnp.concatenate([rec[s, base + 1 : base + 2, :] for s in range(NC)], axis=1)
        pl_ = jnp.concatenate([rec[s, base + 2 : base + 3, :] for s in range(NC)], axis=1)
        hi = hi.astype(F32).astype(jnp.int32)
        lo = lo.astype(F32).astype(jnp.int32)
        pl_ = pl_.astype(F32).astype(jnp.int32)
        src = iota((1, T), 1) >> 7
        valid = (hi + lo) > 0
        lane32 = src * 2 + (pl_ & 1)
        owner = pl_ >> 1
        slot = jnp.where(valid, owner * 32 + lane32, -1)
        p = jnp.where(iota((SL, T), 0) == slot, 1.0, 0.0).astype(BF16)
        p_out[it] = p
        x = jnp.concatenate([rec[s, 0:TOK, :] for s in range(NC)], axis=0)
        xs_out[it] = mm(p, x).astype(BF16)
        ohl = jnp.where(iota((SL, T), 0) == jnp.where(valid, me * 32 + lane32, -1), 1.0, 0.0).astype(BF16)
        own8 = iota((8, T), 0) == owner
        digits = jnp.concatenate(
            [jnp.where(own8 & valid, hi, 0), jnp.where(own8 & valid, lo, 0)], axis=0
        ).astype(F32).astype(BF16)
        ids = mm(digits, ohl, NT)
        id_out[it] = jnp.concatenate([ids[:, 0:128], ids[:, 128:256]], axis=0).astype(BF16)
        flat = jnp.concatenate(
            [hi.astype(F32), lo.astype(F32), jnp.zeros((6, T), F32)], axis=0
        ).astype(BF16)
        both = mm(flat, p, NT)
        code = both[0:1, :] * 32.0 + both[1:2, :]
        code_out[it] = jnp.broadcast_to(code, (8, SL))
        col = column(code)
        col_out[it] = col
        if it == 0:
            for o in range(NO):
                oh = owner_onehot(col, o)
                cs_out[o * 32 : (o + 1) * 32, :] = mm(
                    oh, cents[o * KO : (o + 1) * KO, :]
                ).astype(BF16)


def colsum_kernel(it, rowp, p_in, xs_in, ids_in, cs_in, *refs):
    gs, out, w_out, ucol = refs[:NO], refs[NO], refs[NO + 1], refs[NO + 2]
    u = 1.0 / jnp.sum(rowp[...], axis=0)
    for s in range(NC):
        ucol[s * 128 : (s + 1) * 128, :] = jnp.broadcast_to(u[s : s + 1, :], (128, 128)).T.astype(BF16)
    W = 512
    for o in range(NO):
        for h in range(KO // W):

            def body(j, acc):
                at = pl.ds(pl.multiple_of(j * 128, 128), 128)
                uu = ucol[at, :]
                prod = gs[o][at, h * W : (h + 1) * W] * jnp.concatenate([uu] * (W // 128), axis=1)
                prod = prod[0:64] + prod[64:128]
                prod = (prod[0:32] + prod[32:64]).astype(F32)
                return acc + ((prod[0:8] + prod[8:16]) + (prod[16:24] + prod[24:32]))

            acc = lax.fori_loop(0, T // 128, body, jnp.zeros((8, W), F32))
            tot = jnp.sum(acc, axis=0, keepdims=True)
            row = (o * KO + h * W) // 128
            rows = jnp.concatenate(
                [tot[:, q * 128 : (q + 1) * 128] for q in range(W // 128)], axis=0
            ).astype(BF16)
            for d in range(ND):
                out[d, row : row + W // 128, :] = rows
    uflat = jnp.concatenate([u[s : s + 1, :] for s in range(NC)], axis=1)
    uhi, ulo = split(uflat)
    us = mm(jnp.concatenate([uhi, ulo, jnp.zeros((6, T), BF16)], axis=0), p_in[it], NT)
    us = column(us[0:1, :] + us[1:2, :])
    xs = xs_in[it].astype(F32)
    aff = jnp.sum(xs * cs_in[...].astype(F32), axis=1, keepdims=True)
    w = (CENTROIDS * jnp.exp2(aff * SCALE)) * us
    w_out[...] = w
    rows = (w * xs).astype(BF16)
    for d in range(ND):
        out[d, 64:320, :] = rows
        out[d, 320:352, :] = ids_in[it]


def potentials(rec, target, vbuf):
    tot = rec[0, 0:64, :].astype(F32)
    for d in range(1, ND):
        tot = tot + rec[d, 0:64, :].astype(F32)
    v = target[...] * (TOKENS / CENTROIDS) / tot
    vbuf[...] = v
    ids = rec[0, 320:352, :].astype(F32)
    for d in range(1, ND):
        ids = ids + rec[d, 320:352, :].astype(F32)
    hi = jnp.concatenate([ids[0:8], ids[16:24]], axis=1)
    lo = jnp.concatenate([ids[8:16], ids[24:32]], axis=1)
    return hi * 32.0 + lo


def own_masses(vbuf, code_in, it, w):
    code = code_in[it][0:1, :]
    lid = (code - 1.0).astype(jnp.int32)
    lid = jnp.where(code > 0.0, lid, 0)
    owner = iota((1, SL), 1) >> 5
    row = owner * 8 + (lid >> 7)
    oh = jnp.where(iota((128, SL), 0) == (lid & 127), 1.0, 0.0).astype(BF16)
    vhi, vlo = split(vbuf[...])
    got = mm(vhi, oh) + mm(vlo, oh)
    got = jnp.sum(jnp.where(iota((64, SL), 0) == row, got, 0.0), axis=0, keepdims=True)
    return w * column(got)


def refine(o, rec, codes, vbuf, old, new):
    lid = codes[o : o + 1, :] - 1.0
    pos = lid.astype(jnp.int32)
    vhi, vlo = split(vbuf[o * 8 : (o + 1) * 8, :])
    oh = jnp.where(iota((128, 256), 0) == (pos & 127), 1.0, 0.0).astype(BF16)
    got = mm(vhi, oh) + mm(vlo, oh)
    vs = jnp.sum(jnp.where(iota((8, 256), 0) == (pos >> 7), got, 0.0), axis=0, keepdims=True)
    rows = jnp.concatenate([rec[d, 64 + o * 32 : 96 + o * 32, :] for d in range(ND)], axis=0)
    for q in range(KO // 256):
        oht = jnp.where(iota((256, 256), 0) + q * 256 == pos, vs, 0.0).astype(BF16)
        at = slice(o * KO + q * 256, o * KO + (q + 1) * 256)
        z = old[at, :].astype(F32) + mm(oht, rows)
        new[at, :] = unit(z).astype(BF16)


def second_kernel(rec, target, code_in, col_in, w_in, old, pay, *refs):
    new, gs, row_out, mass_out, cs_out = refs[0], refs[1 : 1 + NO], refs[1 + NO], refs[2 + NO], refs[3 + NO]
    x, acc, vbuf = refs[4 + NO :]
    for s in range(NC):
        x[s * TOK : (s + 1) * TOK, :] = pay[s, 0:TOK, :]
    codes = potentials(rec, target, vbuf)
    mass_out[...] = own_masses(vbuf, code_in, 0, w_in[...])
    col = col_in[1]
    for o in range(NO):
        refine(o, rec, codes, vbuf, old, new)
        cblk = new.at[o * KO : (o + 1) * KO]
        cs_out[o * 32 : (o + 1) * 32, :] = mm(owner_onehot(col, o), cblk[...]).astype(BF16)
        vrow = jnp.concatenate([vbuf[o * 8 + q : o * 8 + q + 1, :] for q in range(8)], axis=1)
        score_block(x, cblk, gs[o], acc, vrow, o == 0)
    finish_rows(acc, row_out)


def last_kernel(rec, target, code_in, col_in, xs_in, w_in, mass1, old, new, out, vbuf):
    codes = potentials(rec, target, vbuf)
    mass2 = own_masses(vbuf, code_in, 1, w_in[...])
    lane = iota((SL, 128), 1)
    m = jnp.where(lane == 0, mass1[...], jnp.where(lane == 1, mass2, 0.0))
    col = col_in[1]
    res = []
    for o in range(NO):
        refine(o, rec, codes, vbuf, old, new)
        res.append(mm(owner_onehot(col, o), new[o * KO : (o + 1) * KO, :]))
    r = xs_in[1].astype(F32) - jnp.concatenate(res, axis=0)
    i, j = iota((SL, SL), 0), iota((SL, SL), 1)
    want = ((i >> 1) & 7) * 32 + (i >> 4) * 2 + (i & 1)
    perm = jnp.where(j == want, 1.0, 0.0).astype(BF16)
    r = mm(perm, r.astype(BF16)).astype(BF16)
    m = mm(perm, m.astype(BF16)).astype(BF16)
    for s in range(NC):
        out[s, 0:16, :] = r[s * 16 : (s + 1) * 16]
        out[s, 16:32, :] = m[s * 16 : (s + 1) * 16]


def exchange(x, axis):
    return lax.all_to_all(x, axis, 0, 0, tiled=True)


def on_device(embeddings, centroids, col_mass, assignments):
    target = col_mass.reshape(KC // 128, 128)
    gshape = tuple(pltpu.VMEM((T, KO), BF16) for _ in range(NO))
    sums = shape(NC, NC, 128)
    xacc = (pltpu.VMEM((T, D), BF16), pltpu.VMEM((T, 128), F32))
    vbuf = (pltpu.VMEM((KC // 128, 128), F32),)
    pay = call(pack_kernel, shape(NC, TOK + 16, 128, dtype=BF16), "pack", 10**6, 8)(
        embeddings, assignments
    )
    rec = exchange(pay, "cent")
    c0 = call(cent_kernel, shape(KC, D, dtype=BF16), "cents", 10**9, 12)(centroids)
    *g, rows = call(first_kernel, gshape + (sums,), "first", 10**10, 12, xacc)(rec, c0)
    rows = exchange(rows, "cent")
    p, xs, ids, code, col, cs = call(
        slot_kernel,
        (
            shape(2, SL, T, dtype=BF16),
            shape(2, SL, D, dtype=BF16),
            shape(2, 32, 128, dtype=BF16),
            shape(2, 8, SL),
            shape(2, SL, 128),
            shape(SL, D, dtype=BF16),
        ),
        "slots",
        10**9,
        16,
    )(rec, c0)

    def columns(it, rows, cs, g):
        def body(*refs):
            colsum_kernel(it, *refs)

        out, w = call(
            body,
            (shape(ND, 352, 128, dtype=BF16), shape(SL, 128)),
            f"columns{it}",
            10**9,
            12,
            (pltpu.VMEM((T, 128), BF16),),
        )(rows, p, xs, ids, cs, *g)
        return exchange(out, "dp"), w

    got, w = columns(0, rows, cs, g)
    c1, *rest = call(
        second_kernel,
        (shape(KC, D, dtype=BF16),) + gshape + (sums, shape(SL, 128), shape(SL, D, dtype=BF16)),
        "second",
        10**10,
        14,
        xacc + vbuf,
    )(got, target, code, col, w, c0, rec)
    g, (rows, mass1, cs) = rest[:NO], rest[NO:]
    rows = exchange(rows, "cent")
    got, w = columns(1, rows, cs, g)
    c2, out = call(
        last_kernel,
        (shape(KC, D, dtype=BF16), shape(NC, 32, 128, dtype=BF16)),
        "last",
        10**9,
        14,
        vbuf,
    )(got, target, code, col, xs, w, mass1, c1)
    back = exchange(out, "cent")
    mass, res = call(unpack_kernel, (shape(2, TOK), shape(TOK, D, dtype=BF16)), "unpack", 10**6, 8)(
        assignments, back
    )
    return c2, mass, res


def solution(mesh):
    in_specs = (P(("dp", "cent"), None), P("cent", None), P("cent"), P(None, ("dp", "cent")))
    out_specs = (P("cent", None), P(None, ("dp", "cent")), P(("dp", "cent"), None))
    return jax.shard_map(
        on_device, mesh=mesh, in_specs=in_specs, out_specs=out_specs, check_vma=False
    )
```

time: 625 us -> 190 us (0.30)
  waiting for transfers between devices: 266 us -> 10.4 us
  blocking collectives: 175 us -> 55.1 us
  Pallas kernels: 0 us -> 74.5 us
  matrix products: 67.5 us -> 0 us
  other arithmetic: 53.4 us -> 0 us
  between operations: 14.2 us -> 0.74 us
  starting transfers between devices: 0.56 us -> 10.6 us
  local copies, waits for them, and re-layouts: 47.1 us -> 38 us
    psum x2 -> x0, waiting for transfers between devices: 131 us -> none  [on_device(): acc = lax.psum(acc, 'dp')]
    psum x4 -> x0, blocking collectives: 128 us -> none  [the longest x2 79.5 us: marginals(): row_potential = 1.0 / lax.psum(row_part, 'cent')]
    pallas_call x0 -> x9, Pallas kernels: none -> 74.5 us  [the longest x1 26.7 us: on_device(): call(second_kernel, (shape(KC, D, dtype=BF16),) + gshape + (sums, shape(S...]
    reduce_scatter x1 -> x0, waiting for transfers between devices: 74.1 us -> none  [on_device(): lax.psum_scatter(res_part.astype(jnp.bfloat16), 'cent', scatter_dimension...]
    dot_general x16 -> x0, matrix products: 67.5 us -> none  [tile_scores(): lax.dot_general(block, cents, (((1,), (1,)), ((), ())), preferred_element...]
    unnamed x5 -> x0, waiting for transfers between devices: 60.9 us -> none
    all_to_all x0 -> x4, blocking collectives: none -> 55.1 us  [exchange(): return lax.all_to_all(x, axis, 0, 0, tiled=True)]
    all_gather x2 -> x0, blocking collectives: 47.1 us -> none  [the longest x1 23.7 us: on_device(): lax.all_gather(assignments, 'cent', axis=1, tiled=True)]
  transfers between devices with their start and end apart: 4 -> 2, of which waited for: 4 -> 2; matrix products, arithmetic and copies ran while one was open for 3% -> 0% of each run, Pallas kernels for 0% -> 3%
where the time goes in v1:
time: 190 us; the launch traced here: 189 us
  Pallas kernels  74.5 us (39%)
  blocking collectives  55.1 us (29%)
  local copies, waits for them, and re-layouts  38 us (20%)
  starting transfers between devices  10.6 us (6%)
  waiting for transfers between devices  10.4 us (5%)
    all_to_all x4, blocking collectives, exchange(): return lax.all_to_all(x, axis, 0, 0, tiled=True)  55.1 us
    unnamed x48, local copies, waits for them, and re-layouts  38 us
    pallas_call x1, Pallas kernels, on_device(): call(second_kernel, (shape(KC, D, dtype=BF16),) + gshape + (sums, shape(S...  26.7 us
    pallas_call x1, Pallas kernels, on_device(): call(first_kernel, gshape + (sums,), 'first', 10 ** 10, 12, xacc)(rec, c0)  20.8 us
    pallas_call x2, Pallas kernels, columns(): call(body, (shape(ND, 352, 128, dtype=BF16), shape(SL, 128)), f'columns{i...  12.7 us
    all_to_all x2, starting transfers between devices, exchange(): return lax.all_to_all(x, axis, 0, 0, tiled=True)  10.6 us
    all_to_all x2, waiting for transfers between devices, exchange(): return lax.all_to_all(x, axis, 0, 0, tiled=True)  10.4 us
    pallas_call x1, Pallas kernels, on_device(): call(last_kernel, (shape(KC, D, dtype=BF16), shape(NC, 32, 128, dtype=BF1...  5.81 us
  transfers between devices with their start and end apart: 2, of which 2 were waited for; matrix products, arithmetic and copies ran while one was open for 0% of the time, Pallas kernels for 3%

profile of v1, /device:TPU:0, one launch (start us, length us, event | category | flops | bytes accessed | tf_op | source)
XLA Modules:
  0.0 189.4 jit_solution(2521105698654501739)
XLA Ops:
  0.6 0.0 copy-start.20
  0.6 0.7 copy-done.20
  1.4 0.0 copy-start.21
  1.4 0.7 copy-done.21
  2.1 1.0 pack.1
  3.1 7.1 %all-to-all-start = ((bf16[16,144,128]{2,1,0:T(8,128)(2,1)}), bf16[16,144,128]{2,1,0:T(8,128)(2,1)S(1)}, u32[]{:S(2)}, u32[]{:S(2)}) async-start(bf16[16,144,128]{2,1,0:T(8,128)(2,1)} %pack.1), calls=%async_computation | async-start | bytes 1179648 | tf_op jit(solution)/shard_map/all_to_all | solution.py:331
  10.2 0.0 copy-start.16
  10.2 1.6 copy-done.16
  11.8 3.8 %cents.1.old = bf16[8192,128]{1,0:T(8,128)(2,1)S(1)} custom-call(bf16[8192,128]{1,0:T(8,128)(2,1)S(1)} %copy-done.16), custom_call_target="tpu_custom_call" | custom-call | flops 1000000000 | bytes 2097152 | tf_op jit(solution)/shard_map/cents/pallas_call | solution.py:344
  15.6 0.0 copy-start.17
  15.6 6.8 %all-to-all-done.rec.pay = bf16[16,144,128]{2,1,0:T(8,128)(2,1)S(1)} async-done(((bf16[16,144,128]{2,1,0:T(8,128)(2,1)}), bf16[16,144,128]{2,1,0:T(8,128)(2,1)S(1)}, u32[]{:S(2)}, u32[]{:S(2)}) %all-to-all-start) | async-done | bytes 589856 | tf_op jit(solution)/shard_map/all_to_all | solution.py:331
  22.4 20.8 %first.1 = (bf16[2048,1024]{1,0:T(8,128)(2,1)S(1)}, bf16[2048,1024]{1,0:T(8,128)(2,1)S(1)}, bf16[2048,1024]{1,0:T(8,128)(2,1)S(1)}, bf16[2048,1024]{1,0:T(8,128)...) custom-call(bf16[16,144,128]{2,1,0:T(8,128)(2,1)S(1)} %all-to-all-do, ...), custom_call_target="tpu_custom_call" | custom-call | flops 10000000000 | bytes 2097152 | tf_op jit(solution)/shard_map/first/pallas_call | solution.py:345
  43.2 0.0 copy-done.17
  43.2 0.0 copy-start
  43.2 2.0 %copy-done = bf16[2048,1024]{1,0:T(8,128)(2,1)} copy-done((bf16[2048,1024]{1,0:T(8,128)(2,1)}, bf16[2048,1024]{1,0:T(8,128)(2,1)S(1)}, u32[]{:S(2)}) %copy-start) | copy-done | bytes 4194328
  45.2 0.0 copy-start.2
  45.2 2.0 %copy-done.2 = bf16[2048,1024]{1,0:T(8,128)(2,1)} copy-done((bf16[2048,1024]{1,0:T(8,128)(2,1)}, bf16[2048,1024]{1,0:T(8,128)(2,1)S(1)}, u32[]{:S(2)}) %copy-start.2) | copy-done | bytes 4194328
  47.2 0.0 copy-start.4
  47.2 2.0 %copy-done.4 = bf16[2048,1024]{1,0:T(8,128)(2,1)} copy-done((bf16[2048,1024]{1,0:T(8,128)(2,1)}, bf16[2048,1024]{1,0:T(8,128)(2,1)S(1)}, u32[]{:S(2)}) %copy-start.4) | copy-done | bytes 4194328
  49.2 0.0 copy-start.6
  49.2 1.9 %copy-done.6 = bf16[2048,1024]{1,0:T(8,128)(2,1)} copy-done((bf16[2048,1024]{1,0:T(8,128)(2,1)}, bf16[2048,1024]{1,0:T(8,128)(2,1)S(1)}, u32[]{:S(2)}) %copy-start.6) | copy-done | bytes 4194328
  51.1 0.0 copy-start.8
  51.1 2.0 %copy-done.8 = bf16[2048,1024]{1,0:T(8,128)(2,1)} copy-done((bf16[2048,1024]{1,0:T(8,128)(2,1)}, bf16[2048,1024]{1,0:T(8,128)(2,1)S(1)}, u32[]{:S(2)}) %copy-start.8) | copy-done | bytes 4194328
  53.1 0.0 copy-start.10
  53.1 2.0 %copy-done.10 = bf16[2048,1024]{1,0:T(8,128)(2,1)} copy-done((bf16[2048,1024]{1,0:T(8,128)(2,1)}, bf16[2048,1024]{1,0:T(8,128)(2,1)S(1)}, u32[]{:S(2)}) %copy-start.10) | copy-done | bytes 4194328
  55.1 0.0 copy-start.12
  55.1 2.0 %copy-done.12 = bf16[2048,1024]{1,0:T(8,128)(2,1)} copy-done((bf16[2048,1024]{1,0:T(8,128)(2,1)}, bf16[2048,1024]{1,0:T(8,128)(2,1)S(1)}, u32[]{:S(2)}) %copy-start.12) | copy-done | bytes 4194328
  57.1 0.0 copy-start.14
  57.1 2.0 %copy-done.14 = bf16[2048,1024]{1,0:T(8,128)(2,1)} copy-done((bf16[2048,1024]{1,0:T(8,128)(2,1)}, bf16[2048,1024]{1,0:T(8,128)(2,1)S(1)}, u32[]{:S(2)}) %copy-start.14) | copy-done | bytes 4194328
  59.1 3.5 %all-to-all-start.1 = ((f32[16,16,128]{2,1,0:T(8,128)}), f32[16,16,128]{2,1,0:T(8,128)S(1)}, u32[]{:S(2)}, u32[]{:S(2)}) async-start(f32[16,16,128]{2,1,0:T(8,128)} %get-tuple-element.38), calls=%async_computation.1 | async-start | bytes 262144 | tf_op jit(solution)/shard_map/all_to_all | solution.py:331
  62.6 0.0 copy-start.18
  62.6 1.6 copy-done.18
  64.2 2.7 %slots.1 = (bf16[2,256,2048]{2,1,0:T(8,128)(2,1)S(1)}, bf16[2,256,128]{2,1,0:T(8,128)(2,1)S(1)}, bf16[2,32,128]{2,1,0:T(8,128)(2,1)S(1)}, f32[2,8,256]{2,1,0:T(8...) custom-call(bf16[16,144,128]{2,1,0:T(8,128)(2,1)S(1)} %all-to-all-done.rec.pay, ...), custom_call_target="tpu_custom_call" | custom-call | flops 1000000000 | bytes 2097152 | tf_op jit(solution)/shard_map/slots/pallas_call | solution.py:347
  66.9 3.6 %all-to-all-done.1.refs_0_ = f32[16,16,128]{2,1,0:T(8,128)S(1)} async-done(((f32[16,16,128]{2,1,0:T(8,128)}), f32[16,16,128]{2,1,0:T(8,128)S(1)}, u32[]{:S(2)}, u32[]{:S(2)}) %all-to-all-start.1) | async-done | bytes 131104 | tf_op jit(solution)/shard_map/all_to_all | solution.py:331
  70.5 0.0 copy-start.1
  70.5 2.2 %copy-done.1 = bf16[2048,1024]{1,0:T(8,128)(2,1)S(1)} copy-done((bf16[2048,1024]{1,0:T(8,128)(2,1)S(1)}, bf16[2048,1024]{1,0:T(8,128)(2,1)}, u32[]{:S(2)}) %copy-start.1) | copy-done | bytes 4194328
  72.7 0.0 copy-start.3
  72.7 2.2 %copy-done.3 = bf16[2048,1024]{1,0:T(8,128)(2,1)S(1)} copy-done((bf16[2048,1024]{1,0:T(8,128)(2,1)S(1)}, bf16[2048,1024]{1,0:T(8,128)(2,1)}, u32[]{:S(2)}) %copy-start.3) | copy-done | bytes 4194328
  74.9 0.0 copy-start.5
  74.9 2.2 %copy-done.5 = bf16[2048,1024]{1,0:T(8,128)(2,1)S(1)} copy-done((bf16[2048,1024]{1,0:T(8,128)(2,1)S(1)}, bf16[2048,1024]{1,0:T(8,128)(2,1)}, u32[]{:S(2)}) %copy-start.5) | copy-done | bytes 4194328
  77.1 0.0 copy-start.7
  77.1 2.2 %copy-done.7 = bf16[2048,1024]{1,0:T(8,128)(2,1)S(1)} copy-done((bf16[2048,1024]{1,0:T(8,128)(2,1)S(1)}, bf16[2048,1024]{1,0:T(8,128)(2,1)}, u32[]{:S(2)}) %copy-start.7) | copy-done | bytes 4194328
  79.3 0.0 copy-start.9
  79.3 2.2 %copy-done.9 = bf16[2048,1024]{1,0:T(8,128)(2,1)S(1)} copy-done((bf16[2048,1024]{1,0:T(8,128)(2,1)S(1)}, bf16[2048,1024]{1,0:T(8,128)(2,1)}, u32[]{:S(2)}) %copy-start.9) | copy-done | bytes 4194328
  81.5 0.0 copy-start.11
  81.5 2.2 %copy-done.11 = bf16[2048,1024]{1,0:T(8,128)(2,1)S(1)} copy-done((bf16[2048,1024]{1,0:T(8,128)(2,1)S(1)}, bf16[2048,1024]{1,0:T(8,128)(2,1)}, u32[]{:S(2)}) %copy-start.11) | copy-done | bytes 4194328
  83.7 0.0 copy-start.13
  83.7 2.2 %copy-done.13 = bf16[2048,1024]{1,0:T(8,128)(2,1)S(1)} copy-done((bf16[2048,1024]{1,0:T(8,128)(2,1)S(1)}, bf16[2048,1024]{1,0:T(8,128)(2,1)}, u32[]{:S(2)}) %copy-start.13) | copy-done | bytes 4194328
  85.9 0.0 copy-start.15
  85.9 2.2 %copy-done.15 = bf16[2048,1024]{1,0:T(8,128)(2,1)S(1)} copy-done((bf16[2048,1024]{1,0:T(8,128)(2,1)S(1)}, bf16[2048,1024]{1,0:T(8,128)(2,1)}, u32[]{:S(2)}) %copy-start.15) | copy-done | bytes 4194328
  88.0 0.0 copy-start.19
  88.1 0.0 copy-start.23
  88.1 6.3 %columns0.1 = (bf16[8,352,128]{2,1,0:T(8,128)(2,1)S(1)}, f32[256,128]{1,0:T(8,128)S(1)}) custom-call(f32[16,16,128]{2,1,0:T(8,128)S(1)} %all-to-all-done.1.refs_0_, bf16[2,256,2048]{2,1,0:T(8,128)(2,1)S(1)} %get-tuple-element.39.refs_1_, bf16[2,256,128]{2,1,0:T(8,128)(2,1)S(1)} %get-tuple-element.40.refs_2_.xs_in, ...), custom_call_target="tpu_custom_call" | custom-call | flops 1000000000 | bytes 2097152 | tf_op jit(solution)/shard_map/columns0/pallas_call | solution.py:366
  94.4 17.7 %all_to_all.30.rec = bf16[8,352,128]{2,1,0:T(8,128)(2,1)S(1)} all-to-all(bf16[8,352,128]{2,1,0:T(8,128)(2,1)S(1)} %get-tuple-element.51), channel_id=1, replica_groups=mesh['dp'=8,'cent'=16] {'dp'}, dimensions={0} | all-to-all | bytes 1441792 | tf_op jit(solution)/shard_map/all_to_all | solution.py:331
  112.0 0.0 copy-done.19
  112.0 0.0 copy-done.23
  112.1 26.7 %second.1 = (bf16[8192,128]{1,0:T(8,128)(2,1)S(1)}, bf16[2048,1024]{1,0:T(8,128)(2,1)S(1)}, bf16[2048,1024]{1,0:T(8,128)(2,1)S(1)}, bf16[2048,1024]{1,0:T(8,128)...) custom-call(bf16[8,352,128]{2,1,0:T(8,128)(2,1)S(1)} %all_to_all.30., ...), custom_call_target="tpu_custom_call" | custom-call | flops 10000000000 | bytes 2097152 | tf_op jit(solution)/shard_map/second/pallas_call | solution.py:377
  138.7 11.4 %all_to_all.31.refs_0_ = f32[16,16,128]{2,1,0:T(8,128)S(1)} all-to-all(f32[16,16,128]{2,1,0:T(8,128)S(1)} %get-tuple-element.55), channel_id=1, replica_groups=mesh['dp'=8,'cent'=16] {'cent'}, dimensions={0} | all-to-all | bytes 262144 | tf_op jit(solution)/shard_map/all_to_all | solution.py:331
  150.1 6.3 %columns1.1 = (bf16[8,352,128]{2,1,0:T(8,128)(2,1)S(1)}, f32[256,128]{1,0:T(8,128)S(1)}) custom-call(f32[16,16,128]{2,1,0:T(8,128)S(1)} %all_to_all.31.refs_0_, bf16[2,256,2048]{2,1,0:T(8,128)(2,1)S(1)} %get-tuple-element.39.refs_1_, bf16[2,256,128]{2,1,0:T(8,128)(2,1)S(1)} %get-tuple-element.40.refs_2_.xs_in, ...), custom_call_target="tpu_custom_call" | custom-call | flops 1000000000 | bytes 2097152 | tf_op jit(solution)/shard_map/columns1/pallas_call | solution.py:366
  156.4 15.1 %all_to_all.32.rec = bf16[8,352,128]{2,1,0:T(8,128)(2,1)S(1)} all-to-all(bf16[8,352,128]{2,1,0:T(8,128)(2,1)S(1)} %get-tuple-element.65), channel_id=1, replica_groups=mesh['dp'=8,'cent'=16] {'dp'}, dimensions={0} | all-to-all | bytes 1441792 | tf_op jit(solution)/shard_map/all_to_all | solution.py:331
  171.5 5.8 %last.1 = (bf16[8192,128]{1,0:T(8,128)(2,1)}, bf16[16,32,128]{2,1,0:T(8,128)(2,1)S(1)}) custom-call(bf16[8,352,128]{2,1,0:T(8,128)(2,1)S(1)} %all_to_all.32.rec, f32[64,128]{1,0:T(8,128)S(1)} %bitcast.2, f32[2,8,256]{2,1,0:T(8,128)S(1)} %get-tuple-element.52.code_in, f32[2,256,128]{2,1,0:T(8,128)S(1)} %get-tuple-element.53.col_in, ...), custom_call_target="tpu_custom_call" | custom-call | flops 1000000000 | bytes 2097152 | tf_op jit(solution)/shard_map/last/pallas_call | solution.py:388
  177.3 11.1 %all_to_all.33.rec = bf16[16,32,128]{2,1,0:T(8,128)(2,1)S(1)} all-to-all(bf16[16,32,128]{2,1,0:T(8,128)(2,1)S(1)} %get-tuple-element.70), channel_id=1, replica_groups=mesh['dp'=8,'cent'=16] {'cent'}, dimensions={0} | all-to-all | bytes 262144 | tf_op jit(solution)/shard_map/all_to_all | solution.py:331
  188.4 0.0 copy-done.22
  188.4 1.0 unpack.1
  (1 shorter events, 0.0 us)
Async XLA Ops:
  0.6 0.8 copy-start.20
  1.4 0.7 copy-start.21
  3.1 19.4 %all-to-all-start = ((bf16[16,144,128]{2,1,0:T(8,128)(2,1)}), bf16[16,144,128]{2,1,0:T(8,128)(2,1)S(1)}, u32[]{:S(2)}, u32[]{:S(2)}) async-start(bf16[16,144,128]{2,1,0:T(8,128)(2,1)} %pack.1), calls=%async_computation | async-start | bytes 1179648 | tf_op jit(solution)/shard_map/all_to_all | solution.py:331
  10.2 1.6 copy-start.16
  15.6 27.6 %copy-start.17 = (bf16[8192,128]{1,0:T(8,128)(2,1)}, bf16[8192,128]{1,0:T(8,128)(2,1)S(1)}, u32[]{:S(2)}) copy-start(bf16[8192,128]{1,0:T(8,128)(2,1)S(1)} %cents.1.old) | copy-start | bytes 6291460
  43.2 2.0 %copy-start = (bf16[2048,1024]{1,0:T(8,128)(2,1)}, bf16[2048,1024]{1,0:T(8,128)(2,1)S(1)}, u32[]{:S(2)}) copy-start(bf16[2048,1024]{1,0:T(8,128)(2,1)S(1)} %get-tuple-element.43.refs_5_) | copy-start | bytes 12582916
  45.2 2.0 %copy-start.2 = (bf16[2048,1024]{1,0:T(8,128)(2,1)}, bf16[2048,1024]{1,0:T(8,128)(2,1)S(1)}, u32[]{:S(2)}) copy-start(bf16[2048,1024]{1,0:T(8,128)(2,1)S(1)} %get-tuple-element.44.refs_6_) | copy-start | bytes 12582916
  47.2 2.0 %copy-start.4 = (bf16[2048,1024]{1,0:T(8,128)(2,1)}, bf16[2048,1024]{1,0:T(8,128)(2,1)S(1)}, u32[]{:S(2)}) copy-start(bf16[2048,1024]{1,0:T(8,128)(2,1)S(1)} %get-tuple-element.45.refs_7_) | copy-start | bytes 12582916
  49.2 1.9 %copy-start.6 = (bf16[2048,1024]{1,0:T(8,128)(2,1)}, bf16[2048,1024]{1,0:T(8,128)(2,1)S(1)}, u32[]{:S(2)}) copy-start(bf16[2048,1024]{1,0:T(8,128)(2,1)S(1)} %get-tuple-element.46.refs_8_) | copy-start | bytes 12582916
  51.1 2.0 %copy-start.8 = (bf16[2048,1024]{1,0:T(8,128)(2,1)}, bf16[2048,1024]{1,0:T(8,128)(2,1)S(1)}, u32[]{:S(2)}) copy-start(bf16[2048,1024]{1,0:T(8,128)(2,1)S(1)} %get-tuple-element.47.refs_9_) | copy-start | bytes 12582916
  53.1 2.0 %copy-start.10 = (bf16[2048,1024]{1,0:T(8,128)(2,1)}, bf16[2048,1024]{1,0:T(8,128)(2,1)S(1)}, u32[]{:S(2)}) copy-start(bf16[2048,1024]{1,0:T(8,128)(2,1)S(1)} %get-tuple-element.48.refs_10_) | copy-start | bytes 12582916
  55.1 2.0 %copy-start.12 = (bf16[2048,1024]{1,0:T(8,128)(2,1)}, bf16[2048,1024]{1,0:T(8,128)(2,1)S(1)}, u32[]{:S(2)}) copy-start(bf16[2048,1024]{1,0:T(8,128)(2,1)S(1)} %get-tuple-element.49.refs_11_) | copy-start | bytes 12582916
  57.1 2.0 %copy-start.14 = (bf16[2048,1024]{1,0:T(8,128)(2,1)}, bf16[2048,1024]{1,0:T(8,128)(2,1)S(1)}, u32[]{:S(2)}) copy-start(bf16[2048,1024]{1,0:T(8,128)(2,1)S(1)} %get-tuple-element.50.refs_12_) | copy-start | bytes 12582916
  59.1 11.5 %all-to-all-start.1 = ((f32[16,16,128]{2,1,0:T(8,128)}), f32[16,16,128]{2,1,0:T(8,128)S(1)}, u32[]{:S(2)}, u32[]{:S(2)}) async-start(f32[16,16,128]{2,1,0:T(8,128)} %get-tuple-element.38), calls=%async_computation.1 | async-start | bytes 262144 | tf_op jit(solution)/shard_map/all_to_all | solution.py:331
  62.6 1.6 copy-start.18
  70.5 2.2 %copy-start.1 = (bf16[2048,1024]{1,0:T(8,128)(2,1)S(1)}, bf16[2048,1024]{1,0:T(8,128)(2,1)}, u32[]{:S(2)}) copy-start(bf16[2048,1024]{1,0:T(8,128)(2,1)} %copy-done) | copy-start | bytes 12582916
  72.7 2.2 %copy-start.3 = (bf16[2048,1024]{1,0:T(8,128)(2,1)S(1)}, bf16[2048,1024]{1,0:T(8,128)(2,1)}, u32[]{:S(2)}) copy-start(bf16[2048,1024]{1,0:T(8,128)(2,1)} %copy-done.2) | copy-start | bytes 12582916
  74.9 2.2 %copy-start.5 = (bf16[2048,1024]{1,0:T(8,128)(2,1)S(1)}, bf16[2048,1024]{1,0:T(8,128)(2,1)}, u32[]{:S(2)}) copy-start(bf16[2048,1024]{1,0:T(8,128)(2,1)} %copy-done.4) | copy-start | bytes 12582916
  77.1 2.2 %copy-start.7 = (bf16[2048,1024]{1,0:T(8,128)(2,1)S(1)}, bf16[2048,1024]{1,0:T(8,128)(2,1)}, u32[]{:S(2)}) copy-start(bf16[2048,1024]{1,0:T(8,128)(2,1)} %copy-done.6) | copy-start | bytes 12582916
  79.3 2.2 %copy-start.9 = (bf16[2048,1024]{1,0:T(8,128)(2,1)S(1)}, bf16[2048,1024]{1,0:T(8,128)(2,1)}, u32[]{:S(2)}) copy-start(bf16[2048,1024]{1,0:T(8,128)(2,1)} %copy-done.8) | copy-start | bytes 12582916
  81.5 2.2 %copy-start.11 = (bf16[2048,1024]{1,0:T(8,128)(2,1)S(1)}, bf16[2048,1024]{1,0:T(8,128)(2,1)}, u32[]{:S(2)}) copy-start(bf16[2048,1024]{1,0:T(8,128)(2,1)} %copy-done.10) | copy-start | bytes 12582916
  83.7 2.2 %copy-start.13 = (bf16[2048,1024]{1,0:T(8,128)(2,1)S(1)}, bf16[2048,1024]{1,0:T(8,128)(2,1)}, u32[]{:S(2)}) copy-start(bf16[2048,1024]{1,0:T(8,128)(2,1)} %copy-done.12) | copy-start | bytes 12582916
  85.9 2.2 %copy-start.15 = (bf16[2048,1024]{1,0:T(8,128)(2,1)S(1)}, bf16[2048,1024]{1,0:T(8,128)(2,1)}, u32[]{:S(2)}) copy-start(bf16[2048,1024]{1,0:T(8,128)(2,1)} %copy-done.14) | copy-start | bytes 12582916
  88.0 24.0 %copy-start.19 = (bf16[8192,128]{1,0:T(8,128)(2,1)S(1)}, bf16[8192,128]{1,0:T(8,128)(2,1)}, u32[]{:S(2)}) copy-start(bf16[8192,128]{1,0:T(8,128)(2,1)} %copy-done.17) | copy-start | bytes 6291460
  88.1 24.0 %copy-start.23 = (f32[8192]{0:T(1024)S(1)}, f32[8192]{0:T(1024)}, u32[]{:S(2)}) copy-start(f32[8192]{0:T(1024)} %param.6) | copy-start | bytes 98308
  156.4 32.0 %copy-start.22 = (s32[2,128]{1,0:T(2,128)S(1)}, s32[2,128]{1,0:T(2,128)}, u32[]{:S(2)}) copy-start(s32[2,128]{1,0:T(2,128)} %asg.3) | copy-start | bytes 3076

commit v2 on v1

--- a/solution.py
+++ b/solution.py
@@ -17,7 +17,7 @@
 SL = 256
 SCALE = 20.0 * math.log2(math.e)
 TOKENS, CENTROIDS = 16384, 131072
-TC = 256
+KW = 256
 MIB = 2**20
 
 NN = (((1,), (0,)), ((), ()))
@@ -124,21 +124,19 @@
 
 
 def score_block(x, cblk, g, acc, weight, first):
-    @pl.loop(0, T // TC)
-    def _(j):
-        at = pl.ds(pl.multiple_of(j * TC, TC), TC)
-        s = mm(x[at, :], cblk[...], NT)
-        e = jnp.exp2(s * SCALE)
-        g[at, :] = e.astype(BF16)
-        if weight is not None:
-            e = e * weight
-        part = e[:, 0:128]
-        for q in range(1, KO // 128):
-            part = part + e[:, q * 128 : (q + 1) * 128]
-        if first:
-            acc[at, :] = part
-        else:
-            acc[at, :] += part
+    part = None
+    for k in range(0, KO, KW):
+        e = jnp.exp2(mm(x[...], cblk[k : k + KW, :], NT) * SCALE)
+        g[:, k : k + KW] = e.astype(BF16)
+        for q in range(0, KW, 128):
+            t = e[:, q : q + 128]
+            if weight is not None:
+                t = t * weight[:, k + q : k + q + 128]
+            part = t if part is None else part + t
+    if first:
+        acc[...] = part
+    else:
+        acc[...] += part
 
 
 def finish_rows(acc, out):
@@ -342,8 +340,6 @@
     )
     rec = exchange(pay, "cent")
     c0 = call(cent_kernel, shape(KC, D, dtype=BF16), "cents", 10**9, 12)(centroids)
-    *g, rows = call(first_kernel, gshape + (sums,), "first", 10**10, 12, xacc)(rec, c0)
-    rows = exchange(rows, "cent")
     p, xs, ids, code, col, cs = call(
         slot_kernel,
         (
@@ -359,6 +355,9 @@
         16,
     )(rec, c0)
 
+    rec, c0, xs = lax.optimization_barrier((rec, c0, xs))
+    *g, rows = call(first_kernel, gshape + (sums,), "first", 10**10, 12, xacc)(rec, c0)
+    rows = exchange(rows, "cent")
     def columns(it, rows, cs, g):
         def body(*refs):
             colsum_kernel(it, *refs)

time: 190 us -> 135 us (0.71)
  local copies, waits for them, and re-layouts: 38 us -> 3.03 us
  Pallas kernels: 74.5 us -> 51.4 us
  blocking collectives: 55.1 us -> 65.9 us
  waiting for transfers between devices: 10.4 us -> 6.82 us
  starting transfers between devices: 10.6 us -> 7.12 us
    unnamed x48 -> x14, local copies, waits for them, and re-layouts: 38 us -> 3.03 us
    pallas_call x1, Pallas kernels: 20.8 us -> 9.03 us  [on_device(): call(first_kernel, gshape + (sums,), 'first', 10 ** 10, 12, xacc)(rec, c0)]
    pallas_call x1, Pallas kernels: 26.7 us -> 15.4 us  [on_device(): call(second_kernel, (shape(KC, D, dtype=BF16),) + gshape + (sums, shape(S...]
    all_to_all x4 -> x5, blocking collectives: 55.1 us -> 65.9 us  [exchange(): return lax.all_to_all(x, axis, 0, 0, tiled=True)]
    all_to_all x2 -> x1, waiting for transfers between devices: 10.4 us -> 6.82 us  [exchange(): return lax.all_to_all(x, axis, 0, 0, tiled=True)]
    all_to_all x2 -> x1, starting transfers between devices: 10.6 us -> 7.12 us  [exchange(): return lax.all_to_all(x, axis, 0, 0, tiled=True)]
  transfers between devices with their start and end apart: 2 -> 1, of which waited for: 2 -> 1; matrix products, arithmetic and copies ran while one was open for 0% -> 0% of each run, Pallas kernels for 3% -> 3%
where the time goes in v2:
time: 135 us
  blocking collectives  65.9 us (49%)
  Pallas kernels  51.4 us (38%)
  starting transfers between devices  7.12 us (5%)
  waiting for transfers between devices  6.82 us (5%)
  local copies, waits for them, and re-layouts  3.03 us (2%)
    all_to_all x5, blocking collectives, exchange(): return lax.all_to_all(x, axis, 0, 0, tiled=True)  65.9 us
    pallas_call x1, Pallas kernels, on_device(): call(second_kernel, (shape(KC, D, dtype=BF16),) + gshape + (sums, shape(S...  15.4 us
    pallas_call x2, Pallas kernels, columns(): call(body, (shape(ND, 352, 128, dtype=BF16), shape(SL, 128)), f'columns{i...  12.7 us
    pallas_call x1, Pallas kernels, on_device(): call(first_kernel, gshape + (sums,), 'first', 10 ** 10, 12, xacc)(rec, c0)  9.03 us
    all_to_all x1, starting transfers between devices, exchange(): return lax.all_to_all(x, axis, 0, 0, tiled=True)  7.12 us
    all_to_all x1, waiting for transfers between devices, exchange(): return lax.all_to_all(x, axis, 0, 0, tiled=True)  6.82 us
    pallas_call x1, Pallas kernels, on_device(): call(last_kernel, (shape(KC, D, dtype=BF16), shape(NC, 32, 128, dtype=BF1...  5.81 us
    pallas_call x1, Pallas kernels, on_device(): call(cent_kernel, shape(KC, D, dtype=BF16), 'cents', 10 ** 9, 12)(centroids)  3.8 us
  transfers between devices with their start and end apart: 1, of which 1 were waited for; matrix products, arithmetic and copies ran while one was open for 0% of the time, Pallas kernels for 3%

profile of v2, /device:TPU:0, one launch (start us, length us, event | category | flops | bytes accessed | tf_op | source)
XLA Modules:
  0.0 134.9 jit_solution(9198492077085515049)
XLA Ops:
  0.6 0.0 copy-start.3
  0.6 0.7 copy-done.3
  1.4 0.0 copy-start.4
  1.4 0.7 copy-done.4
  2.1 1.0 pack.1
  3.1 7.1 %all-to-all-start = ((bf16[16,144,128]{2,1,0:T(8,128)(2,1)}), bf16[16,144,128]{2,1,0:T(8,128)(2,1)S(1)}, u32[]{:S(2)}, u32[]{:S(2)}) async-start(bf16[16,144,128]{2,1,0:T(8,128)(2,1)} %pack.1), calls=%async_computation | async-start | bytes 1179648 | tf_op jit(solution)/shard_map/all_to_all | solution.py:329
  10.2 0.0 copy-start
  10.2 1.6 %copy-done = bf16[8192,128]{1,0:T(8,128)(2,1)S(1)} copy-done((bf16[8192,128]{1,0:T(8,128)(2,1)S(1)}, bf16[8192,128]{1,0:T(8,128)(2,1)}, u32[]{:S(2)}) %copy-start) | copy-done | bytes 2097176
  11.8 3.8 %cents.1.old = bf16[8192,128]{1,0:T(8,128)(2,1)S(1)} custom-call(bf16[8192,128]{1,0:T(8,128)(2,1)S(1)} %copy-done), custom_call_target="tpu_custom_call" | custom-call | flops 1000000000 | bytes 2097152 | tf_op jit(solution)/shard_map/cents/pallas_call | solution.py:342
  15.6 0.0 copy-start.1
  15.6 6.8 %all-to-all-done.rec.pay = bf16[16,144,128]{2,1,0:T(8,128)(2,1)S(1)} async-done(((bf16[16,144,128]{2,1,0:T(8,128)(2,1)}), bf16[16,144,128]{2,1,0:T(8,128)(2,1)S(1)}, u32[]{:S(2)}, u32[]{:S(2)}) %all-to-all-start) | async-done | bytes 589856 | tf_op jit(solution)/shard_map/all_to_all | solution.py:329
  22.4 2.7 %slots.1 = (bf16[2,256,2048]{2,1,0:T(8,128)(2,1)S(1)}, bf16[2,256,128]{2,1,0:T(8,128)(2,1)S(1)}, bf16[2,32,128]{2,1,0:T(8,128)(2,1)S(1)}, f32[2,8,256]{2,1,0:T(8...) custom-call(bf16[16,144,128]{2,1,0:T(8,128)(2,1)S(1)} %all-to-all-done.rec.pay, ...), custom_call_target="tpu_custom_call" | custom-call | flops 1000000000 | bytes 2097152 | tf_op jit(solution)/shard_map/slots/pallas_call | solution.py:343
  25.2 9.0 %first.1 = (bf16[2048,1024]{1,0:T(8,128)(2,1)S(1)}, bf16[2048,1024]{1,0:T(8,128)(2,1)S(1)}, bf16[2048,1024]{1,0:T(8,128)(2,1)S(1)}, bf16[2048,1024]{1,0:T(8,128)...) custom-call(bf16[16,144,128]{2,1,0:T(8,128)(2,1)S(1)} %all-to-all-do, ...), custom_call_target="tpu_custom_call" | custom-call | flops 10000000000 | bytes 2097152 | tf_op jit(solution)/shard_map/first/pallas_call | solution.py:359
  34.2 0.0 copy-done.1
  34.2 11.0 %all_to_all.30.refs_0_ = f32[16,16,128]{2,1,0:T(8,128)S(1)} all-to-all(f32[16,16,128]{2,1,0:T(8,128)S(1)} %get-tuple-element.44), channel_id=1, replica_groups=mesh['dp'=8,'cent'=16] {'cent'}, dimensions={0} | all-to-all | bytes 262144 | tf_op jit(solution)/shard_map/all_to_all | solution.py:329
  45.2 0.0 copy-start.2
  45.2 0.0 copy-start.6
  45.2 6.3 %columns0.1 = (bf16[8,352,128]{2,1,0:T(8,128)(2,1)S(1)}, f32[256,128]{1,0:T(8,128)S(1)}) custom-call(f32[16,16,128]{2,1,0:T(8,128)S(1)} %all_to_all.30.refs_0_, bf16[2,256,2048]{2,1,0:T(8,128)(2,1)S(1)} %get-tuple-element.45.refs_1_, bf16[2,256,128]{2,1,0:T(8,128)(2,1)S(1)} %get-tuple-element.46.refs_2_.xs_in, ...), custom_call_target="tpu_custom_call" | custom-call | flops 1000000000 | bytes 2097152 | tf_op jit(solution)/shard_map/columns0/pallas_call | solution.py:365
  51.5 17.7 %all_to_all.31.rec = bf16[8,352,128]{2,1,0:T(8,128)(2,1)S(1)} all-to-all(bf16[8,352,128]{2,1,0:T(8,128)(2,1)S(1)} %get-tuple-element.57), channel_id=1, replica_groups=mesh['dp'=8,'cent'=16] {'dp'}, dimensions={0} | all-to-all | bytes 1441792 | tf_op jit(solution)/shard_map/all_to_all | solution.py:329
  69.2 0.0 copy-done.2
  69.2 0.0 copy-done.6
  69.2 15.4 %second.1 = (bf16[8192,128]{1,0:T(8,128)(2,1)S(1)}, bf16[2048,1024]{1,0:T(8,128)(2,1)S(1)}, bf16[2048,1024]{1,0:T(8,128)(2,1)S(1)}, bf16[2048,1024]{1,0:T(8,128)...) custom-call(bf16[8,352,128]{2,1,0:T(8,128)(2,1)S(1)} %all_to_all.31., ...), custom_call_target="tpu_custom_call" | custom-call | flops 10000000000 | bytes 2097152 | tf_op jit(solution)/shard_map/second/pallas_call | solution.py:376
  84.6 11.1 %all_to_all.32.refs_0_ = f32[16,16,128]{2,1,0:T(8,128)S(1)} all-to-all(f32[16,16,128]{2,1,0:T(8,128)S(1)} %get-tuple-element.61), channel_id=1, replica_groups=mesh['dp'=8,'cent'=16] {'cent'}, dimensions={0} | all-to-all | bytes 262144 | tf_op jit(solution)/shard_map/all_to_all | solution.py:329
  95.6 6.3 %columns1.1 = (bf16[8,352,128]{2,1,0:T(8,128)(2,1)S(1)}, f32[256,128]{1,0:T(8,128)S(1)}) custom-call(f32[16,16,128]{2,1,0:T(8,128)S(1)} %all_to_all.32.refs_0_, bf16[2,256,2048]{2,1,0:T(8,128)(2,1)S(1)} %get-tuple-element.45.refs_1_, bf16[2,256,128]{2,1,0:T(8,128)(2,1)S(1)} %get-tuple-element.46.refs_2_.xs_in, ...), custom_call_target="tpu_custom_call" | custom-call | flops 1000000000 | bytes 2097152 | tf_op jit(solution)/shard_map/columns1/pallas_call | solution.py:365
  102.0 0.0 copy-start.5
  102.0 15.1 %all_to_all.33.rec = bf16[8,352,128]{2,1,0:T(8,128)(2,1)S(1)} all-to-all(bf16[8,352,128]{2,1,0:T(8,128)(2,1)S(1)} %get-tuple-element.71), channel_id=1, replica_groups=mesh['dp'=8,'cent'=16] {'dp'}, dimensions={0} | all-to-all | bytes 1441792 | tf_op jit(solution)/shard_map/all_to_all | solution.py:329
  117.1 5.8 %last.1 = (bf16[8192,128]{1,0:T(8,128)(2,1)}, bf16[16,32,128]{2,1,0:T(8,128)(2,1)S(1)}) custom-call(bf16[8,352,128]{2,1,0:T(8,128)(2,1)S(1)} %all_to_all.33.rec, f32[64,128]{1,0:T(8,128)S(1)} %bitcast.2, f32[2,8,256]{2,1,0:T(8,128)S(1)} %get-tuple-element.58.code_in, f32[2,256,128]{2,1,0:T(8,128)S(1)} %get-tuple-element.59.col_in, ...), custom_call_target="tpu_custom_call" | custom-call | flops 1000000000 | bytes 2097152 | tf_op jit(solution)/shard_map/last/pallas_call | solution.py:387
  122.9 11.1 %all_to_all.34.rec = bf16[16,32,128]{2,1,0:T(8,128)(2,1)S(1)} all-to-all(bf16[16,32,128]{2,1,0:T(8,128)(2,1)S(1)} %get-tuple-element.76), channel_id=1, replica_groups=mesh['dp'=8,'cent'=16] {'cent'}, dimensions={0} | all-to-all | bytes 262144 | tf_op jit(solution)/shard_map/all_to_all | solution.py:329
  133.9 0.0 copy-done.5
  133.9 1.0 unpack.1
Async XLA Ops:
  0.6 0.8 copy-start.3
  1.4 0.7 copy-start.4
  3.1 19.4 %all-to-all-start = ((bf16[16,144,128]{2,1,0:T(8,128)(2,1)}), bf16[16,144,128]{2,1,0:T(8,128)(2,1)S(1)}, u32[]{:S(2)}, u32[]{:S(2)}) async-start(bf16[16,144,128]{2,1,0:T(8,128)(2,1)} %pack.1), calls=%async_computation | async-start | bytes 1179648 | tf_op jit(solution)/shard_map/all_to_all | solution.py:329
  10.2 1.6 %copy-start = (bf16[8192,128]{1,0:T(8,128)(2,1)S(1)}, bf16[8192,128]{1,0:T(8,128)(2,1)}, u32[]{:S(2)}) copy-start(bf16[8192,128]{1,0:T(8,128)(2,1)} %cent.1) | copy-start | bytes 6291460
  15.6 18.6 %copy-start.1 = (bf16[8192,128]{1,0:T(8,128)(2,1)}, bf16[8192,128]{1,0:T(8,128)(2,1)S(1)}, u32[]{:S(2)}) copy-start(bf16[8192,128]{1,0:T(8,128)(2,1)S(1)} %cents.1.old) | copy-start | bytes 6291460
  45.2 24.0 %copy-start.2 = (bf16[8192,128]{1,0:T(8,128)(2,1)S(1)}, bf16[8192,128]{1,0:T(8,128)(2,1)}, u32[]{:S(2)}) copy-start(bf16[8192,128]{1,0:T(8,128)(2,1)} %copy-done.1) | copy-start | bytes 6291460
  45.2 24.0 %copy-start.6 = (f32[8192]{0:T(1024)S(1)}, f32[8192]{0:T(1024)}, u32[]{:S(2)}) copy-start(f32[8192]{0:T(1024)} %param.6) | copy-start | bytes 98308
  102.0 32.0 %copy-start.5 = (s32[2,128]{1,0:T(2,128)S(1)}, s32[2,128]{1,0:T(2,128)}, u32[]{:S(2)}) copy-start(s32[2,128]{1,0:T(2,128)} %asg.3) | copy-start | bytes 3076

commit v3 on v2

--- a/solution.py
+++ b/solution.py
@@ -140,10 +140,12 @@
 
 
 def finish_rows(acc, out):
-    for s in range(NC):
-        r = jnp.sum(acc[s * 128 : (s + 1) * 128, :].T, axis=0, keepdims=True)
-        for c in range(NC):
-            out[c, s : s + 1, :] = r
+    hi, lo = split(acc[...])
+    one = jnp.ones((8, 128), BF16)
+    r = mm(one, hi, NT) + mm(one, lo, NT)
+    r = jnp.concatenate([r[0:1, s * 128 : (s + 1) * 128] for s in range(NC)], axis=0)
+    for c in range(NC):
+        out[c] = r
 
 
 def first_kernel(rec, cents, *refs):
@@ -164,49 +166,52 @@
     ).astype(BF16)
 
 
-def slot_kernel(rec, cents, p_out, xs_out, id_out, code_out, col_out, cs_out):
+def slot_kernel(it, rec, *refs):
     me = lax.axis_index("dp")
-    for it in range(2):
-        base = TOK + 8 * it
-        hi = jnp.concatenate([rec[s, base : base + 1, :] for s in range(NC)], axis=1)
-        lo = jnp.concatenate([rec[s, base + 1 : base + 2, :] for s in range(NC)], axis=1)
-        pl_ = jnp.concatenate([rec[s, base + 2 : base + 3, :] for s in range(NC)], axis=1)
-        hi = hi.astype(F32).astype(jnp.int32)
-        lo = lo.astype(F32).astype(jnp.int32)
-        pl_ = pl_.astype(F32).astype(jnp.int32)
-        src = iota((1, T), 1) >> 7
-        valid = (hi + lo) > 0
-        lane32 = src * 2 + (pl_ & 1)
-        owner = pl_ >> 1
-        slot = jnp.where(valid, owner * 32 + lane32, -1)
-        p = jnp.where(iota((SL, T), 0) == slot, 1.0, 0.0).astype(BF16)
-        p_out[it] = p
-        x = jnp.concatenate([rec[s, 0:TOK, :] for s in range(NC)], axis=0)
-        xs_out[it] = mm(p, x).astype(BF16)
-        ohl = jnp.where(iota((SL, T), 0) == jnp.where(valid, me * 32 + lane32, -1), 1.0, 0.0).astype(BF16)
-        own8 = iota((8, T), 0) == owner
-        digits = jnp.concatenate(
-            [jnp.where(own8 & valid, hi, 0), jnp.where(own8 & valid, lo, 0)], axis=0
-        ).astype(F32).astype(BF16)
-        ids = mm(digits, ohl, NT)
-        id_out[it] = jnp.concatenate([ids[:, 0:128], ids[:, 128:256]], axis=0).astype(BF16)
-        flat = jnp.concatenate(
-            [hi.astype(F32), lo.astype(F32), jnp.zeros((6, T), F32)], axis=0
-        ).astype(BF16)
-        both = mm(flat, p, NT)
-        code = both[0:1, :] * 32.0 + both[1:2, :]
-        code_out[it] = jnp.broadcast_to(code, (8, SL))
-        col = column(code)
-        col_out[it] = col
-        if it == 0:
-            for o in range(NO):
-                oh = owner_onehot(col, o)
-                cs_out[o * 32 : (o + 1) * 32, :] = mm(
-                    oh, cents[o * KO : (o + 1) * KO, :]
-                ).astype(BF16)
-
-
-def colsum_kernel(it, rowp, p_in, xs_in, ids_in, cs_in, *refs):
+    if it == 0:
+        cents, p_out, xs_out, id_out, code_out, col_out, cs_out = refs
+    else:
+        p_out, xs_out, id_out, code_out, col_out = refs
+    base = TOK + 8 * it
+    hi = jnp.concatenate([rec[s, base : base + 1, :] for s in range(NC)], axis=1)
+    lo = jnp.concatenate([rec[s, base + 1 : base + 2, :] for s in range(NC)], axis=1)
+    pl_ = jnp.concatenate([rec[s, base + 2 : base + 3, :] for s in range(NC)], axis=1)
+    hi = hi.astype(F32).astype(jnp.int32)
+    lo = lo.astype(F32).astype(jnp.int32)
+    pl_ = pl_.astype(F32).astype(jnp.int32)
+    src = iota((1, T), 1) >> 7
+    valid = (hi + lo) > 0
+    lane32 = src * 2 + (pl_ & 1)
+    owner = pl_ >> 1
+    slot = jnp.where(valid, owner * 32 + lane32, -1)
+    p = jnp.where(iota((SL, T), 0) == slot, 1.0, 0.0).astype(BF16)
+    p_out[...] = p
+    x = jnp.concatenate([rec[s, 0:TOK, :] for s in range(NC)], axis=0)
+    xs_out[...] = mm(p, x).astype(BF16)
+    ohl = jnp.where(iota((SL, T), 0) == jnp.where(valid, me * 32 + lane32, -1), 1.0, 0.0).astype(BF16)
+    own8 = iota((8, T), 0) == owner
+    digits = jnp.concatenate(
+        [jnp.where(own8 & valid, hi, 0), jnp.where(own8 & valid, lo, 0)], axis=0
+    ).astype(F32).astype(BF16)
+    ids = mm(digits, ohl, NT)
+    id_out[...] = jnp.concatenate([ids[:, 0:128], ids[:, 128:256]], axis=0).astype(BF16)
+    flat = jnp.concatenate(
+        [hi.astype(F32), lo.astype(F32), jnp.zeros((6, T), F32)], axis=0
+    ).astype(BF16)
+    both = mm(flat, p, NT)
+    code = both[0:1, :] * 32.0 + both[1:2, :]
+    code_out[...] = jnp.broadcast_to(code, (8, SL))
+    col = column(code)
+    col_out[...] = col
+    if it == 0:
+        for o in range(NO):
+            oh = owner_onehot(col, o)
+            cs_out[o * 32 : (o + 1) * 32, :] = mm(
+                oh, cents[o * KO : (o + 1) * KO, :]
+            ).astype(BF16)
+
+
+def colsum_kernel(rowp, p_in, xs_in, ids_in, cs_in, *refs):
     gs, out, w_out, ucol = refs[:NO], refs[NO], refs[NO + 1], refs[NO + 2]
     u = 1.0 / jnp.sum(rowp[...], axis=0)
     for s in range(NC):
@@ -223,7 +228,7 @@
                 prod = (prod[0:32] + prod[32:64]).astype(F32)
                 return acc + ((prod[0:8] + prod[8:16]) + (prod[16:24] + prod[24:32]))
 
-            acc = lax.fori_loop(0, T // 128, body, jnp.zeros((8, W), F32))
+            acc = lax.fori_loop(0, T // 128, body, jnp.zeros((8, W), F32), unroll=8)
             tot = jnp.sum(acc, axis=0, keepdims=True)
             row = (o * KO + h * W) // 128
             rows = jnp.concatenate(
@@ -233,16 +238,16 @@
                 out[d, row : row + W // 128, :] = rows
     uflat = jnp.concatenate([u[s : s + 1, :] for s in range(NC)], axis=1)
     uhi, ulo = split(uflat)
-    us = mm(jnp.concatenate([uhi, ulo, jnp.zeros((6, T), BF16)], axis=0), p_in[it], NT)
+    us = mm(jnp.concatenate([uhi, ulo, jnp.zeros((6, T), BF16)], axis=0), p_in[...], NT)
     us = column(us[0:1, :] + us[1:2, :])
-    xs = xs_in[it].astype(F32)
+    xs = xs_in[...].astype(F32)
     aff = jnp.sum(xs * cs_in[...].astype(F32), axis=1, keepdims=True)
     w = (CENTROIDS * jnp.exp2(aff * SCALE)) * us
     w_out[...] = w
     rows = (w * xs).astype(BF16)
     for d in range(ND):
         out[d, 64:320, :] = rows
-        out[d, 320:352, :] = ids_in[it]
+        out[d, 320:352, :] = ids_in[...]
 
 
 def potentials(rec, target, vbuf):
@@ -259,8 +264,8 @@
     return hi * 32.0 + lo
 
 
-def own_masses(vbuf, code_in, it, w):
-    code = code_in[it][0:1, :]
+def own_masses(vbuf, code_in, w):
+    code = code_in[0:1, :]
     lid = (code - 1.0).astype(jnp.int32)
     lid = jnp.where(code > 0.0, lid, 0)
     owner = iota((1, SL), 1) >> 5
@@ -272,14 +277,22 @@
     return w * column(got)
 
 
-def refine(o, rec, codes, vbuf, old, new):
-    lid = codes[o : o + 1, :] - 1.0
-    pos = lid.astype(jnp.int32)
+def slot_potentials(o, codes, vbuf):
+    pos = (codes[o : o + 1, :] - 1.0).astype(jnp.int32)
     vhi, vlo = split(vbuf[o * 8 : (o + 1) * 8, :])
     oh = jnp.where(iota((128, 256), 0) == (pos & 127), 1.0, 0.0).astype(BF16)
     got = mm(vhi, oh) + mm(vlo, oh)
     vs = jnp.sum(jnp.where(iota((8, 256), 0) == (pos >> 7), got, 0.0), axis=0, keepdims=True)
-    rows = jnp.concatenate([rec[d, 64 + o * 32 : 96 + o * 32, :] for d in range(ND)], axis=0)
+    return pos, vs
+
+
+def slot_rows(o, rec):
+    return jnp.concatenate([rec[d, 64 + o * 32 : 96 + o * 32, :] for d in range(ND)], axis=0)
+
+
+def refine(o, rec, codes, vbuf, old, new):
+    pos, vs = slot_potentials(o, codes, vbuf)
+    rows = slot_rows(o, rec)
     for q in range(KO // 256):
         oht = jnp.where(iota((256, 256), 0) + q * 256 == pos, vs, 0.0).astype(BF16)
         at = slice(o * KO + q * 256, o * KO + (q + 1) * 256)
@@ -293,10 +306,11 @@
     for s in range(NC):
         x[s * TOK : (s + 1) * TOK, :] = pay[s, 0:TOK, :]
     codes = potentials(rec, target, vbuf)
-    mass_out[...] = own_masses(vbuf, code_in, 0, w_in[...])
-    col = col_in[1]
+    mass_out[...] = own_masses(vbuf, code_in, w_in[...])
+    col = col_in[...]
     for o in range(NO):
         refine(o, rec, codes, vbuf, old, new)
+    for o in range(NO):
         cblk = new.at[o * KO : (o + 1) * KO]
         cs_out[o * 32 : (o + 1) * 32, :] = mm(owner_onehot(col, o), cblk[...]).astype(BF16)
         vrow = jnp.concatenate([vbuf[o * 8 + q : o * 8 + q + 1, :] for q in range(8)], axis=1)
@@ -304,17 +318,21 @@
     finish_rows(acc, row_out)
 
 
-def last_kernel(rec, target, code_in, col_in, xs_in, w_in, mass1, old, new, out, vbuf):
+def tail_kernel(rec, target, code_in, col_in, xs_in, cs_in, w_in, mass1, out, vbuf):
     codes = potentials(rec, target, vbuf)
-    mass2 = own_masses(vbuf, code_in, 1, w_in[...])
+    mass2 = own_masses(vbuf, code_in, w_in[...])
     lane = iota((SL, 128), 1)
     m = jnp.where(lane == 0, mass1[...], jnp.where(lane == 1, mass2, 0.0))
-    col = col_in[1]
-    res = []
-    for o in range(NO):
-        refine(o, rec, codes, vbuf, old, new)
-        res.append(mm(owner_onehot(col, o), new[o * KO : (o + 1) * KO, :]))
-    r = xs_in[1].astype(F32) - jnp.concatenate(res, axis=0)
+    col = col_in[...]
+    new = []
+    for o in range(NO):
+        pos, vs = slot_potentials(o, codes, vbuf)
+        mine = col[o * 32 : (o + 1) * 32, :] - 1.0
+        mine = jnp.concatenate([mine, mine], axis=1).astype(jnp.int32)
+        oht = jnp.where(mine == pos, vs, 0.0).astype(BF16)
+        z = cs_in[o * 32 : (o + 1) * 32, :].astype(F32) + mm(oht, slot_rows(o, rec))
+        new.append(unit(z).astype(BF16).astype(F32))
+    r = xs_in[...].astype(F32) - jnp.concatenate(new, axis=0)
     i, j = iota((SL, SL), 0), iota((SL, SL), 1)
     want = ((i >> 1) & 7) * 32 + (i >> 4) * 2 + (i & 1)
     perm = jnp.where(j == want, 1.0, 0.0).astype(BF16)
@@ -325,6 +343,12 @@
         out[s, 16:32, :] = m[s * 16 : (s + 1) * 16]
 
 
+def last_kernel(rec, target, old, new, vbuf):
+    codes = potentials(rec, target, vbuf)
+    for o in range(NO):
+        refine(o, rec, codes, vbuf, old, new)
+
+
 def exchange(x, axis):
     return lax.all_to_all(x, axis, 0, 0, tiled=True)
 
@@ -340,59 +364,58 @@
     )
     rec = exchange(pay, "cent")
     c0 = call(cent_kernel, shape(KC, D, dtype=BF16), "cents", 10**9, 12)(centroids)
-    p, xs, ids, code, col, cs = call(
-        slot_kernel,
-        (
-            shape(2, SL, T, dtype=BF16),
-            shape(2, SL, D, dtype=BF16),
-            shape(2, 32, 128, dtype=BF16),
-            shape(2, 8, SL),
-            shape(2, SL, 128),
+    def slots(it, *args):
+        def body(*refs):
+            slot_kernel(it, *refs)
+
+        outs = (
+            shape(SL, T, dtype=BF16),
             shape(SL, D, dtype=BF16),
-        ),
-        "slots",
-        10**9,
-        16,
-    )(rec, c0)
-
-    rec, c0, xs = lax.optimization_barrier((rec, c0, xs))
-    *g, rows = call(first_kernel, gshape + (sums,), "first", 10**10, 12, xacc)(rec, c0)
-    rows = exchange(rows, "cent")
-    def columns(it, rows, cs, g):
-        def body(*refs):
-            colsum_kernel(it, *refs)
-
+            shape(32, 128, dtype=BF16),
+            shape(8, SL),
+            shape(SL, 128),
+        )
+        if it == 0:
+            outs += (shape(SL, D, dtype=BF16),)
+        return call(body, outs, f"slots{it}", 10**9, 16)(*args)
+
+    def columns(it, rows, p, xs, ids, cs, g):
         out, w = call(
-            body,
+            colsum_kernel,
             (shape(ND, 352, 128, dtype=BF16), shape(SL, 128)),
             f"columns{it}",
             10**9,
             12,
             (pltpu.VMEM((T, 128), BF16),),
         )(rows, p, xs, ids, cs, *g)
-        return exchange(out, "dp"), w
-
-    got, w = columns(0, rows, cs, g)
+        return out, w
+
+    p, xs, ids, code, col0, cs = slots(0, rec, c0)
+    rec, c0, xs = lax.optimization_barrier((rec, c0, xs))
+    *g, rows = call(first_kernel, gshape + (sums,), "first", 10**10, 12, xacc)(rec, c0)
+    rows = exchange(rows, "cent")
+    got, w = columns(0, rows, p, xs, ids, cs, g)
+    rec, got, w = lax.optimization_barrier((rec, got, w))
+    got = exchange(got, "dp")
+    p, xs, ids, code1, col = slots(1, rec)
     c1, *rest = call(
         second_kernel,
         (shape(KC, D, dtype=BF16),) + gshape + (sums, shape(SL, 128), shape(SL, D, dtype=BF16)),
         "second",
         10**10,
-        14,
+        12,
         xacc + vbuf,
     )(got, target, code, col, w, c0, rec)
     g, (rows, mass1, cs) = rest[:NO], rest[NO:]
     rows = exchange(rows, "cent")
-    got, w = columns(1, rows, cs, g)
-    c2, out = call(
-        last_kernel,
-        (shape(KC, D, dtype=BF16), shape(NC, 32, 128, dtype=BF16)),
-        "last",
-        10**9,
-        14,
-        vbuf,
-    )(got, target, code, col, xs, w, mass1, c1)
+    got, w = columns(1, rows, p, xs, ids, cs, g)
+    got = exchange(got, "dp")
+    out = call(tail_kernel, shape(NC, 32, 128, dtype=BF16), "tail", 10**8, 14, vbuf)(
+        got, target, code1, col, xs, cs, w, mass1
+    )
+    got, out = lax.optimization_barrier((got, out))
     back = exchange(out, "cent")
+    c2 = call(last_kernel, shape(KC, D, dtype=BF16), "last", 10**9, 14, vbuf)(got, target, c1)
     mass, res = call(unpack_kernel, (shape(2, TOK), shape(TOK, D, dtype=BF16)), "unpack", 10**6, 8)(
         assignments, back
     )

time: 135 us -> 132 us (0.978)
  blocking collectives: 65.9 us -> 37.1 us
  waiting for transfers between devices: 6.82 us -> 20.3 us
  starting transfers between devices: 7.12 us -> 16.1 us
  local copies, waits for them, and re-layouts: 3.03 us -> 8.1 us
  Pallas kernels: 51.4 us -> 49.1 us
    all_to_all x5 -> x3, blocking collectives: 65.9 us -> 37.1 us  [exchange(): return lax.all_to_all(x, axis, 0, 0, tiled=True)]
    all_to_all x1 -> x3, waiting for transfers between devices: 6.82 us -> 20.3 us  [exchange(): return lax.all_to_all(x, axis, 0, 0, tiled=True)]
    all_to_all x1 -> x3, starting transfers between devices: 7.12 us -> 16.1 us  [exchange(): return lax.all_to_all(x, axis, 0, 0, tiled=True)]
    unnamed x14 -> x28, local copies, waits for them, and re-layouts: 3.03 us -> 8.1 us
    pallas_call x4 -> x6, Pallas kernels: 21.2 us -> 19.9 us  [the longest x2 10.3 us: columns(): call(colsum_kernel, (shape(ND, 352, 128, dtype=BF16), shape(SL, 128)), f'...]
  transfers between devices with their start and end apart: 1 -> 3, of which waited for: 1 -> 3; matrix products, arithmetic and copies ran while one was open for 0% -> 0% of each run, Pallas kernels for 3% -> 7%
where the time goes in v3:
time: 132 us; the launch traced here: 131 us
  Pallas kernels  49.1 us (37%)
  blocking collectives  37.1 us (28%)
  waiting for transfers between devices  20.3 us (15%)
  starting transfers between devices  16.1 us (12%)
  local copies, waits for them, and re-layouts  8.1 us (6%)
    all_to_all x3, blocking collectives, exchange(): return lax.all_to_all(x, axis, 0, 0, tiled=True)  37.1 us
    all_to_all x3, waiting for transfers between devices, exchange(): return lax.all_to_all(x, axis, 0, 0, tiled=True)  20.3 us
    all_to_all x3, starting transfers between devices, exchange(): return lax.all_to_all(x, axis, 0, 0, tiled=True)  16.1 us
    pallas_call x1, Pallas kernels, on_device(): call(second_kernel, (shape(KC, D, dtype=BF16),) + gshape + (sums, shape(S...  14.2 us
    pallas_call x2, Pallas kernels, columns(): call(colsum_kernel, (shape(ND, 352, 128, dtype=BF16), shape(SL, 128)), f'...  10.3 us
    pallas_call x1, Pallas kernels, on_device(): call(first_kernel, gshape + (sums,), 'first', 10 ** 10, 12, xacc)(rec, c0)  9.18 us
    unnamed x28, local copies, waits for them, and re-layouts  8.1 us
    pallas_call x1, Pallas kernels, on_device(): call(last_kernel, shape(KC, D, dtype=BF16), 'last', 10 ** 9, 14, vbuf)  4 us
  transfers between devices with their start and end apart: 3, of which 3 were waited for; matrix products, arithmetic and copies ran while one was open for 0% of the time, Pallas kernels for 7%

profile of v3, /device:TPU:0, one launch (start us, length us, event | category | flops | bytes accessed | tf_op | source)
XLA Modules:
  0.0 131.4 jit_solution(17301953914758654626)
XLA Ops:
  0.6 0.0 copy-start.9
  0.6 0.7 copy-done.9
  1.4 0.0 copy-start.10
  1.4 0.7 copy-done.10
  2.1 1.0 pack.1
  3.1 7.1 %all-to-all-start = ((bf16[16,144,128]{2,1,0:T(8,128)(2,1)}), bf16[16,144,128]{2,1,0:T(8,128)(2,1)S(1)}, u32[]{:S(2)}, u32[]{:S(2)}) async-start(bf16[16,144,128]{2,1,0:T(8,128)(2,1)} %pack.1), calls=%async_computation | async-start | bytes 1179648 | tf_op jit(solution)/shard_map/all_to_all | solution.py:353
  10.2 0.0 copy-start
  10.2 1.6 %copy-done = bf16[8192,128]{1,0:T(8,128)(2,1)S(1)} copy-done((bf16[8192,128]{1,0:T(8,128)(2,1)S(1)}, bf16[8192,128]{1,0:T(8,128)(2,1)}, u32[]{:S(2)}) %copy-start) | copy-done | bytes 2097176
  11.8 3.8 %cents.1.refs_1_.old = bf16[8192,128]{1,0:T(8,128)(2,1)S(1)} custom-call(bf16[8192,128]{1,0:T(8,128)(2,1)S(1)} %copy-done), custom_call_target="tpu_custom_call" | custom-call | flops 1000000000 | bytes 2097152 | tf_op jit(solution)/shard_map/cents/pallas_call | solution.py:366
  15.6 0.0 copy-start.1
  15.6 6.8 %all-to-all-done.refs_0_.rec.pay = bf16[16,144,128]{2,1,0:T(8,128)(2,1)S(1)} async-done(((bf16[16,144,128]{2,1,0:T(8,128)(2,1)}), bf16[16,144,128]{2,1,0:T(8,128)(2,1)S(1)}, u32[]{:S(2)}, u32[]{:S(2)}) %all-to-all-start) | async-done | bytes 589856 | tf_op jit(solution)/shard_map/all_to_all | solution.py:353
  22.5 2.1 %slots0.1 = (bf16[256,2048]{1,0:T(8,128)(2,1)S(1)}, bf16[256,128]{1,0:T(8,128)(2,1)S(1)}, bf16[32,128]{1,0:T(8,128)(2,1)S(1)}, f32[8,256]{1,0:T(8,128)S(1)}, f32...) custom-call(bf16[16,144,128]{2,1,0:T(8,128)(2,1)S(1)} %all-to-all-done.refs_0_.rec.pay, bf16[8192,128]{1,0:T(8,128)(2,1)S(1)} %cents.1.refs_1_.old), custom_call_target="tpu_custom_call" | custom-call | flops 1000000000 | bytes 2097152 | tf_op jit(solution)/shard_map/slots0/pallas_call | solution.py:380
  24.5 9.2 %first.1 = (bf16[2048,1024]{1,0:T(8,128)(2,1)S(1)}, bf16[2048,1024]{1,0:T(8,128)(2,1)S(1)}, bf16[2048,1024]{1,0:T(8,128)(2,1)S(1)}, bf16[2048,1024]{1,0:T(8,128)...) custom-call(bf16[16,144,128]{2,1,0:T(8,128)(2,1)S(1)} %all-to-all-do, ...), custom_call_target="tpu_custom_call" | custom-call | flops 10000000000 | bytes 2097152 | tf_op jit(solution)/shard_map/first/pallas_call | solution.py:395
  33.7 0.0 copy-done.1
  33.7 11.0 %all_to_all.30.rowp = f32[16,16,128]{2,1,0:T(8,128)S(1)} all-to-all(f32[16,16,128]{2,1,0:T(8,128)S(1)} %get-tuple-element.51), channel_id=1, replica_groups=mesh['dp'=8,'cent'=16] {'cent'}, dimensions={0} | all-to-all | bytes 262144 | tf_op jit(solution)/shard_map/all_to_all | solution.py:353
  44.7 5.1 %columns0.1 = (bf16[8,352,128]{2,1,0:T(8,128)(2,1)}, f32[256,128]{1,0:T(8,128)S(1)}) custom-call(f32[16,16,128]{2,1,0:T(8,128)S(1)} %all_to_all.30.rowp, bf16[256,2048]{1,0:T(8,128)(2,1)S(1)} %get-tuple-element.52.p_in, bf16[256,128]{1,0:T(8,128)(2,1)S(1)} %get-tuple-element.53.xs_in, bf16[32,128]{1,0:T(8,128)(2,1)S(1)} %get-tuple-element.54.ids_in, ...), custom_call_target="tpu_custom_call" | custom-call | flops 1000000000 | bytes 2097152 | tf_op jit(solution)/shard_map/columns0/pallas_call | solution.py:383
  49.8 0.0 copy-start.12
  49.8 0.0 copy-start.5
  49.8 5.4 %all-to-all-start.2 = ((bf16[8,352,128]{2,1,0:T(8,128)(2,1)}), bf16[8,352,128]{2,1,0:T(8,128)(2,1)S(1)}, u32[]{:S(2)}, u32[]{:S(2)}) async-start(bf16[8,352,128]{2,1,0:T(8,128)(2,1)} %get-tuple-element.66), calls=%async_computation.2 | async-start | bytes 1441792 | tf_op jit(solution)/shard_map/all_to_all | solution.py:353
  55.3 1.2 slots1.1
  56.5 0.0 copy-start.3
  56.5 1.0 copy-done.3
  57.5 0.0 copy-start.6
  57.5 0.6 copy-done.6
  58.2 9.5 %all-to-all-done.2.rec = bf16[8,352,128]{2,1,0:T(8,128)(2,1)S(1)} async-done(((bf16[8,352,128]{2,1,0:T(8,128)(2,1)}), bf16[8,352,128]{2,1,0:T(8,128)(2,1)S(1)}, u32[]{:S(2)}, u32[]{:S(2)}) %all-to-all-start.2) | async-done | bytes 720928 | tf_op jit(solution)/shard_map/all_to_all | solution.py:353
  67.7 0.0 copy-done.12
  67.7 0.0 copy-done.5
  67.7 0.0 copy-start.2
  67.7 1.6 %copy-done.2 = bf16[8192,128]{1,0:T(8,128)(2,1)S(1)} copy-done((bf16[8192,128]{1,0:T(8,128)(2,1)S(1)}, bf16[8192,128]{1,0:T(8,128)(2,1)}, u32[]{:S(2)}) %copy-start.2) | copy-done | bytes 2097176
  69.3 0.0 copy-start.7
  69.3 0.9 copy-done.7
  70.2 0.0 copy-start.13
  70.2 0.9 copy-done.13
  71.1 0.0 copy-start.4
  71.1 14.2 %second.1 = (bf16[8192,128]{1,0:T(8,128)(2,1)S(1)}, bf16[2048,1024]{1,0:T(8,128)(2,1)S(1)}, bf16[2048,1024]{1,0:T(8,128)(2,1)S(1)}, bf16[2048,1024]{1,0:T(8,128)...) custom-call(bf16[8,352,128]{2,1,0:T(8,128)(2,1)S(1)} %all-to-all-don, ...), custom_call_target="tpu_custom_call" | custom-call | flops 10000000000 | bytes 2097152 | tf_op jit(solution)/shard_map/second/pallas_call | solution.py:401
  85.3 11.1 %all_to_all.31.rowp = f32[16,16,128]{2,1,0:T(8,128)S(1)} all-to-all(f32[16,16,128]{2,1,0:T(8,128)S(1)} %get-tuple-element.71), channel_id=1, replica_groups=mesh['dp'=8,'cent'=16] {'cent'}, dimensions={0} | all-to-all | bytes 262144 | tf_op jit(solution)/shard_map/all_to_all | solution.py:353
  96.4 0.0 copy-done.4
  96.4 0.0 copy-start.8
  96.4 5.2 %columns1.1 = (bf16[8,352,128]{2,1,0:T(8,128)(2,1)S(1)}, f32[256,128]{1,0:T(8,128)S(1)}) custom-call(f32[16,16,128]{2,1,0:T(8,128)S(1)} %all_to_all.31.rowp, bf16[256,2048]{1,0:T(8,128)(2,1)S(1)} %copy-done.4, bf16[256,128]{1,0:T(8,128)(2,1)S(1)} %get-tuple-element.73.xs_in, bf16[32,128]{1,0:T(8,128)(2,1)S(1)} %get-tuple-element.74.ids_in, ...), custom_call_target="tpu_custom_call" | custom-call | flops 1000000000 | bytes 2097152 | tf_op jit(solution)/shard_map/columns1/pallas_call | solution.py:383
  101.6 0.0 copy-start.11
  101.6 15.1 %all_to_all.32.rec = bf16[8,352,128]{2,1,0:T(8,128)(2,1)S(1)} all-to-all(bf16[8,352,128]{2,1,0:T(8,128)(2,1)S(1)} %get-tuple-element.84), channel_id=1, replica_groups=mesh['dp'=8,'cent'=16] {'dp'}, dimensions={0} | all-to-all | bytes 1441792 | tf_op jit(solution)/shard_map/all_to_all | solution.py:353
  116.7 0.0 copy-done.8
  116.7 2.3 %tail.1 = bf16[16,32,128]{2,1,0:T(8,128)(2,1)} custom-call(bf16[8,352,128]{2,1,0:T(8,128)(2,1)S(1)} %all_to_all.32.rec, f32[64,128]{1,0:T(8,128)S(1)} %bitcast.2, f32[8,256]{1,0:T(8,128)S(1)} %get-tuple-element.85.code_in, f32[256,128]{1,0:T(8,128)S(1)} %copy-done.8, bf16[256,128]{1,0:T(8,128)(2,1)S(1)} %get-tuple-element.73.xs_in, ...), custom_call_target="tpu_custom_call" | custom-call | flops 100000000 | bytes 2097152 | tf_op jit(solution)/shard_map/tail/pallas_call | solution.py:413
  119.0 3.5 %all-to-all-start.5 = ((bf16[16,32,128]{2,1,0:T(8,128)(2,1)}), bf16[16,32,128]{2,1,0:T(8,128)(2,1)S(1)}, u32[]{:S(2)}, u32[]{:S(2)}) async-start(bf16[16,32,128]{2,1,0:T(8,128)(2,1)} %tail.1), calls=%async_computation.5 | async-start | bytes 262144 | tf_op jit(solution)/shard_map/all_to_all | solution.py:353
  122.5 4.0 %last.1 = bf16[8192,128]{1,0:T(8,128)(2,1)} custom-call(bf16[8,352,128]{2,1,0:T(8,128)(2,1)S(1)} %all_to_all.32.rec, f32[64,128]{1,0:T(8,128)S(1)} %bitcast.3, bf16[8192,128]{1,0:T(8,128)(2,1)S(1)} %get-tuple-element.89.old), custom_call_target="tpu_custom_call" | custom-call | flops 1000000000 | bytes 2097152 | tf_op jit(solution)/shard_map/last/pallas_call | solution.py:418
  126.5 3.9 %all-to-all-done.5.rec = bf16[16,32,128]{2,1,0:T(8,128)(2,1)S(1)} async-done(((bf16[16,32,128]{2,1,0:T(8,128)(2,1)}), bf16[16,32,128]{2,1,0:T(8,128)(2,1)S(1)}, u32[]{:S(2)}, u32[]{:S(2)}) %all-to-all-start.5) | async-done | bytes 131104 | tf_op jit(solution)/shard_map/all_to_all | solution.py:353
  130.4 0.0 copy-done.11
  130.4 1.0 unpack.1
Async XLA Ops:
  0.6 0.8 copy-start.9
  1.4 0.7 copy-start.10
  3.1 19.4 %all-to-all-start = ((bf16[16,144,128]{2,1,0:T(8,128)(2,1)}), bf16[16,144,128]{2,1,0:T(8,128)(2,1)S(1)}, u32[]{:S(2)}, u32[]{:S(2)}) async-start(bf16[16,144,128]{2,1,0:T(8,128)(2,1)} %pack.1), calls=%async_computation | async-start | bytes 1179648 | tf_op jit(solution)/shard_map/all_to_all | solution.py:353
  10.2 1.6 %copy-start = (bf16[8192,128]{1,0:T(8,128)(2,1)S(1)}, bf16[8192,128]{1,0:T(8,128)(2,1)}, u32[]{:S(2)}) copy-start(bf16[8192,128]{1,0:T(8,128)(2,1)} %cent.1) | copy-start | bytes 6291460
  15.6 18.1 %copy-start.1 = (bf16[8192,128]{1,0:T(8,128)(2,1)}, bf16[8192,128]{1,0:T(8,128)(2,1)S(1)}, u32[]{:S(2)}) copy-start(bf16[8192,128]{1,0:T(8,128)(2,1)S(1)} %cents.1.refs_1_.old) | copy-start | bytes 6291460
  49.8 17.9 %copy-start.12 = (f32[256,128]{1,0:T(8,128)}, f32[256,128]{1,0:T(8,128)S(1)}, u32[]{:S(2)}) copy-start(f32[256,128]{1,0:T(8,128)S(1)} %get-tuple-element.70.w_in) | copy-start | bytes 393220
  49.8 17.9 %copy-start.5 = (f32[8192]{0:T(1024)S(1)}, f32[8192]{0:T(1024)}, u32[]{:S(2)}) copy-start(f32[8192]{0:T(1024)} %param.6) | copy-start | bytes 98308
  49.8 17.9 %all-to-all-start.2 = ((bf16[8,352,128]{2,1,0:T(8,128)(2,1)}), bf16[8,352,128]{2,1,0:T(8,128)(2,1)S(1)}, u32[]{:S(2)}, u32[]{:S(2)}) async-start(bf16[8,352,128]{2,1,0:T(8,128)(2,1)} %get-tuple-element.66), calls=%async_computation.2 | async-start | bytes 1441792 | tf_op jit(solution)/shard_map/all_to_all | solution.py:353
  56.5 1.0 copy-start.3
  57.5 0.6 copy-start.6
  67.7 1.6 %copy-start.2 = (bf16[8192,128]{1,0:T(8,128)(2,1)S(1)}, bf16[8192,128]{1,0:T(8,128)(2,1)}, u32[]{:S(2)}) copy-start(bf16[8192,128]{1,0:T(8,128)(2,1)} %copy-done.1) | copy-start | bytes 6291460
  69.3 0.9 copy-start.7
  70.2 0.9 copy-start.13
  71.1 25.3 %copy-start.4 = (bf16[256,2048]{1,0:T(8,128)(2,1)S(1)}, bf16[256,2048]{1,0:T(8,128)(2,1)}, u32[]{:S(2)}) copy-start(bf16[256,2048]{1,0:T(8,128)(2,1)} %copy-done.3) | copy-start | bytes 3145732
  96.4 20.3 %copy-start.8 = (f32[256,128]{1,0:T(8,128)S(1)}, f32[256,128]{1,0:T(8,128)}, u32[]{:S(2)}) copy-start(f32[256,128]{1,0:T(8,128)} %copy-done.6) | copy-start | bytes 393220
  101.6 28.8 %copy-start.11 = (s32[2,128]{1,0:T(2,128)S(1)}, s32[2,128]{1,0:T(2,128)}, u32[]{:S(2)}) copy-start(s32[2,128]{1,0:T(2,128)} %asg.3) | copy-start | bytes 3076
  119.0 11.5 %all-to-all-start.5 = ((bf16[16,32,128]{2,1,0:T(8,128)(2,1)}), bf16[16,32,128]{2,1,0:T(8,128)(2,1)S(1)}, u32[]{:S(2)}, u32[]{:S(2)}) async-start(bf16[16,32,128]{2,1,0:T(8,128)(2,1)} %tail.1), calls=%async_computation.5 | async-start | bytes 262144 | tf_op jit(solution)/shard_map/all_to_all | solution.py:353

commit v4 on v2

--- a/solution.py
+++ b/solution.py
@@ -123,15 +123,23 @@
         out[at, :] = unit(cent[at, :].astype(F32)).astype(BF16)
 
 
-def score_block(x, cblk, g, acc, weight, first):
+def score_rows(rec, x):
+    for s in range(NC):
+        hi, lo = split(rec[s, 0:TOK, :].astype(F32) * SCALE)
+        x[s * TOK : (s + 1) * TOK, :] = jnp.concatenate([hi, lo], axis=1)
+
+
+def score_block(x, cblk, g, acc, shift, first):
     part = None
     for k in range(0, KO, KW):
-        e = jnp.exp2(mm(x[...], cblk[k : k + KW, :], NT) * SCALE)
+        c = cblk[k : k + KW, :]
+        e = mm(x[...], jnp.concatenate([c, c], axis=1), NT)
+        if shift is not None:
+            e = e + shift[:, k : k + KW]
+        e = jnp.exp2(e)
         g[:, k : k + KW] = e.astype(BF16)
         for q in range(0, KW, 128):
             t = e[:, q : q + 128]
-            if weight is not None:
-                t = t * weight[:, k + q : k + q + 128]
             part = t if part is None else part + t
     if first:
         acc[...] = part
@@ -140,16 +148,17 @@
 
 
 def finish_rows(acc, out):
-    for s in range(NC):
-        r = jnp.sum(acc[s * 128 : (s + 1) * 128, :].T, axis=0, keepdims=True)
-        for c in range(NC):
-            out[c, s : s + 1, :] = r
+    hi, lo = split(acc[...])
+    one = jnp.ones((8, 128), BF16)
+    r = mm(one, hi, NT) + mm(one, lo, NT)
+    r = jnp.concatenate([r[0:1, s * 128 : (s + 1) * 128] for s in range(NC)], axis=0)
+    for c in range(NC):
+        out[c] = r
 
 
 def first_kernel(rec, cents, *refs):
     gs, row_out, x, acc = refs[:NO], refs[NO], refs[NO + 1], refs[NO + 2]
-    for s in range(NC):
-        x[s * TOK : (s + 1) * TOK, :] = rec[s, 0:TOK, :]
+    score_rows(rec, x)
     for o in range(NO):
         score_block(x, cents.at[o * KO : (o + 1) * KO], gs[o], acc, None, o == 0)
     finish_rows(acc, row_out)
@@ -164,50 +173,61 @@
     ).astype(BF16)
 
 
+def order_matrix(back):
+    i, j = iota((SL, SL), 0), iota((SL, SL), 1)
+    if back:
+        want = ((i >> 1) & 7) * 32 + (i >> 4) * 2 + (i & 1)
+    else:
+        want = ((i >> 1) & 15) * 16 + (i >> 5) * 2 + (i & 1)
+    return jnp.where(j == want, 1.0, 0.0).astype(BF16)
+
+
 def slot_kernel(rec, cents, p_out, xs_out, id_out, code_out, col_out, cs_out):
     me = lax.axis_index("dp")
+    order = order_matrix(False)
     for it in range(2):
         base = TOK + 8 * it
-        hi = jnp.concatenate([rec[s, base : base + 1, :] for s in range(NC)], axis=1)
-        lo = jnp.concatenate([rec[s, base + 1 : base + 2, :] for s in range(NC)], axis=1)
-        pl_ = jnp.concatenate([rec[s, base + 2 : base + 3, :] for s in range(NC)], axis=1)
-        hi = hi.astype(F32).astype(jnp.int32)
-        lo = lo.astype(F32).astype(jnp.int32)
-        pl_ = pl_.astype(F32).astype(jnp.int32)
-        src = iota((1, T), 1) >> 7
-        valid = (hi + lo) > 0
-        lane32 = src * 2 + (pl_ & 1)
-        owner = pl_ >> 1
-        slot = jnp.where(valid, owner * 32 + lane32, -1)
-        p = jnp.where(iota((SL, T), 0) == slot, 1.0, 0.0).astype(BF16)
-        p_out[it] = p
-        x = jnp.concatenate([rec[s, 0:TOK, :] for s in range(NC)], axis=0)
-        xs_out[it] = mm(p, x).astype(BF16)
-        ohl = jnp.where(iota((SL, T), 0) == jnp.where(valid, me * 32 + lane32, -1), 1.0, 0.0).astype(BF16)
-        own8 = iota((8, T), 0) == owner
-        digits = jnp.concatenate(
-            [jnp.where(own8 & valid, hi, 0), jnp.where(own8 & valid, lo, 0)], axis=0
-        ).astype(F32).astype(BF16)
-        ids = mm(digits, ohl, NT)
+        place16 = iota((16, TOK), 0).astype(F32)
+        xs, digits = [], []
+        for s in range(NC):
+            meta = rec[s, base : base + 8, :].astype(F32)
+            hi, lo, place = meta[0:1, :], meta[1:2, :], meta[2:3, :]
+            p = jnp.where((place16 == place) & (hi + lo > 0.0), 1.0, 0.0)
+            p_out[it, s * 16 : (s + 1) * 16, :] = p
+            xs.append(mm(p.astype(BF16), rec[s, 0:TOK, :]))
+            digits.append(
+                jnp.concatenate(
+                    [
+                        jnp.broadcast_to(jnp.sum(p * q, axis=1, keepdims=True), (16, 128))
+                        for q in (hi, lo)
+                    ],
+                    axis=1,
+                )
+            )
+        both = jnp.concatenate([jnp.concatenate(xs, axis=0), jnp.concatenate(digits, axis=0)], axis=1)
+        both = mm(order, both.astype(BF16))
+        xs_out[it] = both[:, 0:128].astype(BF16)
+        dhi, dlo = both[:, 128:256], both[:, 256:384]
+        col = dhi * 32.0 + dlo
+        col_out[it] = col
+        rhi = jnp.concatenate([dhi[0:128].T[0:1], dhi[128:256].T[0:1]], axis=1)
+        rlo = jnp.concatenate([dlo[0:128].T[0:1], dlo[128:256].T[0:1]], axis=1)
+        code_out[it] = jnp.broadcast_to(rhi * 32.0 + rlo, (8, SL))
+        slot = iota((SL, SL), 0)
+        lane = jnp.where(iota((SL, SL), 1) == me * 32 + (slot & 31), 1.0, 0.0).astype(BF16)
+        own = iota((8, SL), 0) == (iota((8, SL), 1) >> 5)
+        rows = jnp.concatenate([jnp.where(own, rhi, 0.0), jnp.where(own, rlo, 0.0)], axis=0)
+        ids = mm(rows.astype(BF16), lane)
         id_out[it] = jnp.concatenate([ids[:, 0:128], ids[:, 128:256]], axis=0).astype(BF16)
-        flat = jnp.concatenate(
-            [hi.astype(F32), lo.astype(F32), jnp.zeros((6, T), F32)], axis=0
-        ).astype(BF16)
-        both = mm(flat, p, NT)
-        code = both[0:1, :] * 32.0 + both[1:2, :]
-        code_out[it] = jnp.broadcast_to(code, (8, SL))
-        col = column(code)
-        col_out[it] = col
         if it == 0:
             for o in range(NO):
-                oh = owner_onehot(col, o)
                 cs_out[o * 32 : (o + 1) * 32, :] = mm(
-                    oh, cents[o * KO : (o + 1) * KO, :]
+                    owner_onehot(col, o), cents[o * KO : (o + 1) * KO, :]
                 ).astype(BF16)
 
 
 def colsum_kernel(it, rowp, p_in, xs_in, ids_in, cs_in, *refs):
-    gs, out, w_out, ucol = refs[:NO], refs[NO], refs[NO + 1], refs[NO + 2]
+    gs, out, w_out, ucol, tots = refs[:NO], refs[NO], refs[NO + 1], refs[NO + 2], refs[NO + 3]
     u = 1.0 / jnp.sum(rowp[...], axis=0)
     for s in range(NC):
         ucol[s * 128 : (s + 1) * 128, :] = jnp.broadcast_to(u[s : s + 1, :], (128, 128)).T.astype(BF16)
@@ -223,33 +243,40 @@
                 prod = (prod[0:32] + prod[32:64]).astype(F32)
                 return acc + ((prod[0:8] + prod[8:16]) + (prod[16:24] + prod[24:32]))
 
-            acc = lax.fori_loop(0, T // 128, body, jnp.zeros((8, W), F32))
+            acc = lax.fori_loop(0, T // 128, body, jnp.zeros((8, W), F32), unroll=8)
             tot = jnp.sum(acc, axis=0, keepdims=True)
             row = (o * KO + h * W) // 128
-            rows = jnp.concatenate(
-                [tot[:, q * 128 : (q + 1) * 128] for q in range(W // 128)], axis=0
-            ).astype(BF16)
-            for d in range(ND):
-                out[d, row : row + W // 128, :] = rows
-    uflat = jnp.concatenate([u[s : s + 1, :] for s in range(NC)], axis=1)
-    uhi, ulo = split(uflat)
-    us = mm(jnp.concatenate([uhi, ulo, jnp.zeros((6, T), BF16)], axis=0), p_in[it], NT)
-    us = column(us[0:1, :] + us[1:2, :])
+            for q in range(W // 128):
+                tots[row + q : row + q + 1, :] = tot[:, q * 128 : (q + 1) * 128]
+    us = jnp.concatenate(
+        [
+            jnp.sum(p_in[it, s * 16 : (s + 1) * 16, :] * u[s : s + 1, :], axis=1, keepdims=True)
+            for s in range(NC)
+        ],
+        axis=0,
+    )
+    uhi, ulo = split(jnp.broadcast_to(us, (SL, 128)))
+    both = mm(order_matrix(False), jnp.concatenate([uhi, ulo], axis=1))
+    us = both[:, 0:128] + both[:, 128:256]
     xs = xs_in[it].astype(F32)
     aff = jnp.sum(xs * cs_in[...].astype(F32), axis=1, keepdims=True)
     w = (CENTROIDS * jnp.exp2(aff * SCALE)) * us
     w_out[...] = w
     rows = (w * xs).astype(BF16)
+    tot = tots[...].astype(BF16)
     for d in range(ND):
+        out[d, 0:64, :] = tot
         out[d, 64:320, :] = rows
         out[d, 320:352, :] = ids_in[it]
 
 
-def potentials(rec, target, vbuf):
+def potentials(rec, target, vbuf, before=None):
     tot = rec[0, 0:64, :].astype(F32)
     for d in range(1, ND):
         tot = tot + rec[d, 0:64, :].astype(F32)
     v = target[...] * (TOKENS / CENTROIDS) / tot
+    if before is not None:
+        v = v * before[...]
     vbuf[...] = v
     ids = rec[0, 320:352, :].astype(F32)
     for d in range(1, ND):
@@ -272,52 +299,63 @@
     return w * column(got)
 
 
-def refine(o, rec, codes, vbuf, old, new):
-    lid = codes[o : o + 1, :] - 1.0
-    pos = lid.astype(jnp.int32)
+def slot_potentials(o, codes, vbuf):
+    pos = (codes[o : o + 1, :] - 1.0).astype(jnp.int32)
     vhi, vlo = split(vbuf[o * 8 : (o + 1) * 8, :])
     oh = jnp.where(iota((128, 256), 0) == (pos & 127), 1.0, 0.0).astype(BF16)
     got = mm(vhi, oh) + mm(vlo, oh)
     vs = jnp.sum(jnp.where(iota((8, 256), 0) == (pos >> 7), got, 0.0), axis=0, keepdims=True)
-    rows = jnp.concatenate([rec[d, 64 + o * 32 : 96 + o * 32, :] for d in range(ND)], axis=0)
-    for q in range(KO // 256):
-        oht = jnp.where(iota((256, 256), 0) + q * 256 == pos, vs, 0.0).astype(BF16)
-        at = slice(o * KO + q * 256, o * KO + (q + 1) * 256)
-        z = old[at, :].astype(F32) + mm(oht, rows)
-        new[at, :] = unit(z).astype(BF16)
+    return pos, vs
+
+
+def slot_rows(o, rec):
+    return jnp.concatenate([rec[d, 64 + o * 32 : 96 + o * 32, :] for d in range(ND)], axis=0)
+
+
+def refine(o, rec, codes, vbuf, old, new):
+    pos, vs = slot_potentials(o, codes, vbuf)
+    rows = slot_rows(o, rec)
+    oht = jnp.where(iota((KO, 256), 0) == pos, vs, 0.0).astype(BF16)
+    at = slice(o * KO, (o + 1) * KO)
+    z = old[at, :].astype(F32) + mm(oht, rows)
+    new[at, :] = unit(z).astype(BF16)
 
 
 def second_kernel(rec, target, code_in, col_in, w_in, old, pay, *refs):
-    new, gs, row_out, mass_out, cs_out = refs[0], refs[1 : 1 + NO], refs[1 + NO], refs[2 + NO], refs[3 + NO]
-    x, acc, vbuf = refs[4 + NO :]
-    for s in range(NC):
-        x[s * TOK : (s + 1) * TOK, :] = pay[s, 0:TOK, :]
+    new, gs, row_out, mass_out, cs_out, v_out = refs[0], refs[1 : 1 + NO], *refs[1 + NO : 5 + NO]
+    x, acc, vbuf = refs[5 + NO :]
+    score_rows(pay, x)
     codes = potentials(rec, target, vbuf)
+    v_out[...] = vbuf[...]
+    logv = jnp.log2(vbuf[...])
     mass_out[...] = own_masses(vbuf, code_in, 0, w_in[...])
     col = col_in[1]
     for o in range(NO):
         refine(o, rec, codes, vbuf, old, new)
+    for o in range(NO):
         cblk = new.at[o * KO : (o + 1) * KO]
         cs_out[o * 32 : (o + 1) * 32, :] = mm(owner_onehot(col, o), cblk[...]).astype(BF16)
-        vrow = jnp.concatenate([vbuf[o * 8 + q : o * 8 + q + 1, :] for q in range(8)], axis=1)
-        score_block(x, cblk, gs[o], acc, vrow, o == 0)
+        shift = jnp.concatenate([logv[o * 8 + q : o * 8 + q + 1, :] for q in range(8)], axis=1)
+        score_block(x, cblk, gs[o], acc, shift, o == 0)
     finish_rows(acc, row_out)
 
 
-def last_kernel(rec, target, code_in, col_in, xs_in, w_in, mass1, old, new, out, vbuf):
-    codes = potentials(rec, target, vbuf)
+def tail_kernel(rec, target, v_in, code_in, col_in, xs_in, cs_in, w_in, mass1, out, vbuf):
+    codes = potentials(rec, target, vbuf, v_in)
     mass2 = own_masses(vbuf, code_in, 1, w_in[...])
     lane = iota((SL, 128), 1)
     m = jnp.where(lane == 0, mass1[...], jnp.where(lane == 1, mass2, 0.0))
     col = col_in[1]
-    res = []
-    for o in range(NO):
-        refine(o, rec, codes, vbuf, old, new)
-        res.append(mm(owner_onehot(col, o), new[o * KO : (o + 1) * KO, :]))
-    r = xs_in[1].astype(F32) - jnp.concatenate(res, axis=0)
-    i, j = iota((SL, SL), 0), iota((SL, SL), 1)
-    want = ((i >> 1) & 7) * 32 + (i >> 4) * 2 + (i & 1)
-    perm = jnp.where(j == want, 1.0, 0.0).astype(BF16)
+    new = []
+    for o in range(NO):
+        pos, vs = slot_potentials(o, codes, vbuf)
+        mine = col[o * 32 : (o + 1) * 32, :] - 1.0
+        mine = jnp.concatenate([mine, mine], axis=1).astype(jnp.int32)
+        oht = jnp.where(mine == pos, vs, 0.0).astype(BF16)
+        z = cs_in[o * 32 : (o + 1) * 32, :].astype(F32) + mm(oht, slot_rows(o, rec))
+        new.append(unit(z).astype(BF16).astype(F32))
+    r = xs_in[1].astype(F32) - jnp.concatenate(new, axis=0)
+    perm = order_matrix(True)
     r = mm(perm, r.astype(BF16)).astype(BF16)
     m = mm(perm, m.astype(BF16)).astype(BF16)
     for s in range(NC):
@@ -325,6 +363,12 @@
         out[s, 16:32, :] = m[s * 16 : (s + 1) * 16]
 
 
+def last_kernel(rec, target, v_in, old, new, vbuf):
+    codes = potentials(rec, target, vbuf, v_in)
+    for o in range(NO):
+        refine(o, rec, codes, vbuf, old, new)
+
+
 def exchange(x, axis):
     return lax.all_to_all(x, axis, 0, 0, tiled=True)
 
@@ -333,7 +377,7 @@
     target = col_mass.reshape(KC // 128, 128)
     gshape = tuple(pltpu.VMEM((T, KO), BF16) for _ in range(NO))
     sums = shape(NC, NC, 128)
-    xacc = (pltpu.VMEM((T, D), BF16), pltpu.VMEM((T, 128), F32))
+    xacc = (pltpu.VMEM((T, 2 * D), BF16), pltpu.VMEM((T, 128), F32))
     vbuf = (pltpu.VMEM((KC // 128, 128), F32),)
     pay = call(pack_kernel, shape(NC, TOK + 16, 128, dtype=BF16), "pack", 10**6, 8)(
         embeddings, assignments
@@ -343,7 +387,7 @@
     p, xs, ids, code, col, cs = call(
         slot_kernel,
         (
-            shape(2, SL, T, dtype=BF16),
+            shape(2, SL, TOK),
             shape(2, SL, D, dtype=BF16),
             shape(2, 32, 128, dtype=BF16),
             shape(2, 8, SL),
@@ -352,12 +396,10 @@
         ),
         "slots",
         10**9,
-        16,
+        12,
     )(rec, c0)
-
     rec, c0, xs = lax.optimization_barrier((rec, c0, xs))
-    *g, rows = call(first_kernel, gshape + (sums,), "first", 10**10, 12, xacc)(rec, c0)
-    rows = exchange(rows, "cent")
+
     def columns(it, rows, cs, g):
         def body(*refs):
             colsum_kernel(it, *refs)
@@ -368,31 +410,31 @@
             f"columns{it}",
             10**9,
             12,
-            (pltpu.VMEM((T, 128), BF16),),
+            (pltpu.VMEM((T, 128), BF16), pltpu.VMEM((64, 128), F32)),
         )(rows, p, xs, ids, cs, *g)
         return exchange(out, "dp"), w
 
+    *g, rows = call(first_kernel, gshape + (sums,), "first", 10**10, 12, xacc)(rec, c0)
+    rows = exchange(rows, "cent")
     got, w = columns(0, rows, cs, g)
     c1, *rest = call(
         second_kernel,
-        (shape(KC, D, dtype=BF16),) + gshape + (sums, shape(SL, 128), shape(SL, D, dtype=BF16)),
+        (shape(KC, D, dtype=BF16),) + gshape
+        + (sums, shape(SL, 128), shape(SL, D, dtype=BF16), shape(KC // 128, 128)),
         "second",
         10**10,
-        14,
+        12,
         xacc + vbuf,
     )(got, target, code, col, w, c0, rec)
-    g, (rows, mass1, cs) = rest[:NO], rest[NO:]
+    g, (rows, mass1, cs, v1) = rest[:NO], rest[NO:]
     rows = exchange(rows, "cent")
     got, w = columns(1, rows, cs, g)
-    c2, out = call(
-        last_kernel,
-        (shape(KC, D, dtype=BF16), shape(NC, 32, 128, dtype=BF16)),
-        "last",
-        10**9,
-        14,
-        vbuf,
-    )(got, target, code, col, xs, w, mass1, c1)
+    out = call(tail_kernel, shape(NC, 32, 128, dtype=BF16), "tail", 10**8, 14, vbuf)(
+        got, target, v1, code, col, xs, cs, w, mass1
+    )
+    got, out = lax.optimization_barrier((got, out))
     back = exchange(out, "cent")
+    c2 = call(last_kernel, shape(KC, D, dtype=BF16), "last", 10**9, 14, vbuf)(got, target, v1, c1)
     mass, res = call(unpack_kernel, (shape(2, TOK), shape(TOK, D, dtype=BF16)), "unpack", 10**6, 8)(
         assignments, back
     )

time: 135 us -> 125 us (0.926)
  blocking collectives: 65.9 us -> 54.9 us
  Pallas kernels: 51.4 us -> 42.3 us
  waiting for transfers between devices: 6.82 us -> 11.3 us
  starting transfers between devices: 7.12 us -> 10.6 us
    all_to_all x5 -> x4, blocking collectives: 65.9 us -> 54.9 us  [exchange(): return lax.all_to_all(x, axis, 0, 0, tiled=True)]
    pallas_call x2, Pallas kernels: 12.7 us -> 7.99 us  [columns(): call(body, (shape(ND, 352, 128, dtype=BF16), shape(SL, 128)), f'columns{i...]
    all_to_all x1 -> x2, waiting for transfers between devices: 6.82 us -> 11.3 us  [exchange(): return lax.all_to_all(x, axis, 0, 0, tiled=True)]
    all_to_all x1 -> x2, starting transfers between devices: 7.12 us -> 10.6 us  [exchange(): return lax.all_to_all(x, axis, 0, 0, tiled=True)]
    pallas_call x1, Pallas kernels: 15.4 us -> 12.2 us  [on_device(): call(second_kernel, (shape(KC, D, dtype=BF16),) + gshape + (sums, shape(S...]
    pallas_call x2 -> x3, Pallas kernels: 8.55 us -> 7.13 us  [the longest x1 3.43 us: on_device(): call(last_kernel, shape(KC, D, dtype=BF16), 'last', 10 ** 9, 14, vbuf)]
  transfers between devices with their start and end apart: 1 -> 2, of which waited for: 1 -> 2; matrix products, arithmetic and copies ran while one was open for 0% -> 0% of each run, Pallas kernels for 3% -> 6%
where the time goes in v4:
time: 125 us; the launch traced here: 124 us
  blocking collectives  54.9 us (44%)
  Pallas kernels  42.3 us (34%)
  waiting for transfers between devices  11.3 us (9%)
  starting transfers between devices  10.6 us (8%)
  local copies, waits for them, and re-layouts  4.36 us (3%)
    all_to_all x4, blocking collectives, exchange(): return lax.all_to_all(x, axis, 0, 0, tiled=True)  54.9 us
    pallas_call x1, Pallas kernels, on_device(): call(second_kernel, (shape(KC, D, dtype=BF16),) + gshape + (sums, shape(S...  12.2 us
    all_to_all x2, waiting for transfers between devices, exchange(): return lax.all_to_all(x, axis, 0, 0, tiled=True)  11.3 us
    all_to_all x2, starting transfers between devices, exchange(): return lax.all_to_all(x, axis, 0, 0, tiled=True)  10.6 us
    pallas_call x1, Pallas kernels, on_device(): call(first_kernel, gshape + (sums,), 'first', 10 ** 10, 12, xacc)(rec, c0)  9.17 us
    pallas_call x2, Pallas kernels, columns(): call(body, (shape(ND, 352, 128, dtype=BF16), shape(SL, 128)), f'columns{i...  7.99 us
    unnamed x14, local copies, waits for them, and re-layouts  4.36 us
    pallas_call x1, Pallas kernels, on_device(): call(cent_kernel, shape(KC, D, dtype=BF16), 'cents', 10 ** 9, 12)(centroids)  3.8 us
  transfers between devices with their start and end apart: 2, of which 2 were waited for; matrix products, arithmetic and copies ran while one was open for 0% of the time, Pallas kernels for 6%

profile of v4, /device:TPU:0, one launch (start us, length us, event | category | flops | bytes accessed | tf_op | source)
XLA Modules:
  0.0 124.3 jit_solution(10998685887904488279)
XLA Ops:
  0.6 0.0 copy-start.4
  0.6 0.7 copy-done.4
  1.4 0.0 copy-start.5
  1.4 0.7 copy-done.5
  2.1 1.0 pack.1
  3.1 7.1 %all-to-all-start = ((bf16[16,144,128]{2,1,0:T(8,128)(2,1)}), bf16[16,144,128]{2,1,0:T(8,128)(2,1)S(1)}, u32[]{:S(2)}, u32[]{:S(2)}) async-start(bf16[16,144,128]{2,1,0:T(8,128)(2,1)} %pack.1), calls=%async_computation | async-start | bytes 1179648 | tf_op jit(solution)/shard_map/all_to_all | solution.py:373
  10.2 0.0 copy-start
  10.2 1.6 %copy-done = bf16[8192,128]{1,0:T(8,128)(2,1)S(1)} copy-done((bf16[8192,128]{1,0:T(8,128)(2,1)S(1)}, bf16[8192,128]{1,0:T(8,128)(2,1)}, u32[]{:S(2)}) %copy-start) | copy-done | bytes 2097176
  11.8 3.8 %cents.1.old = bf16[8192,128]{1,0:T(8,128)(2,1)S(1)} custom-call(bf16[8192,128]{1,0:T(8,128)(2,1)S(1)} %copy-done), custom_call_target="tpu_custom_call" | custom-call | flops 1000000000 | bytes 2097152 | tf_op jit(solution)/shard_map/cents/pallas_call | solution.py:386
  15.6 6.8 %all-to-all-done.rec.pay = bf16[16,144,128]{2,1,0:T(8,128)(2,1)S(1)} async-done(((bf16[16,144,128]{2,1,0:T(8,128)(2,1)}), bf16[16,144,128]{2,1,0:T(8,128)(2,1)S(1)}, u32[]{:S(2)}, u32[]{:S(2)}) %all-to-all-start) | async-done | bytes 589856 | tf_op jit(solution)/shard_map/all_to_all | solution.py:373
  22.4 1.4 %slots.1 = (f32[2,256,128]{2,1,0:T(8,128)S(1)}, bf16[2,256,128]{2,1,0:T(8,128)(2,1)S(1)}, bf16[2,32,128]{2,1,0:T(8,128)(2,1)S(1)}, f32[2,8,256]{2,1,0:T(8,128)S(...) custom-call(bf16[16,144,128]{2,1,0:T(8,128)(2,1)S(1)} %all-to-all-done.rec.pay, bf16[8192,128]{1,0:T(8,128)(2,1)S(1)} %cents.1.old), custom_call_target="tpu_custom_call" | custom-call | flops 1000000000 | bytes 2097152 | tf_op jit(solution)/shard_map/slots/pallas_call | solution.py:387
  23.8 9.2 %first.1 = (bf16[2048,1024]{1,0:T(8,128)(2,1)S(1)}, bf16[2048,1024]{1,0:T(8,128)(2,1)S(1)}, bf16[2048,1024]{1,0:T(8,128)(2,1)S(1)}, bf16[2048,1024]{1,0:T(8,128)...) custom-call(bf16[16,144,128]{2,1,0:T(8,128)(2,1)S(1)} %all-to-all-do, ...), custom_call_target="tpu_custom_call" | custom-call | flops 10000000000 | bytes 2097152 | tf_op jit(solution)/shard_map/first/pallas_call | solution.py:417
  33.0 11.0 %all_to_all.30.refs_0_ = f32[16,16,128]{2,1,0:T(8,128)S(1)} all-to-all(f32[16,16,128]{2,1,0:T(8,128)S(1)} %get-tuple-element.45), channel_id=1, replica_groups=mesh['dp'=8,'cent'=16] {'cent'}, dimensions={0} | all-to-all | bytes 262144 | tf_op jit(solution)/shard_map/all_to_all | solution.py:373
  44.0 0.0 copy-start.3
  44.0 4.0 %columns0.1 = (bf16[8,352,128]{2,1,0:T(8,128)(2,1)S(1)}, f32[256,128]{1,0:T(8,128)S(1)}) custom-call(f32[16,16,128]{2,1,0:T(8,128)S(1)} %all_to_all.30.refs_0_, f32[2,256,128]{2,1,0:T(8,128)S(1)} %get-tuple-element.46.refs_1_, bf16[2,256,128]{2,1,0:T(8,128)(2,1)S(1)} %get-tuple-element.47.refs_2_.xs_in, bf16[2,32,128]{2,1,0:T(8,128)(2,1)S(1)} %get-tuple-element.48.refs_3_, ...), custom_call_target="tpu_custom_call" | custom-call | flops 1000000000 | bytes 2097152 | tf_op jit(solution)/shard_map/columns0/pallas_call | solution.py:407
  48.0 17.7 %all_to_all.31.rec = bf16[8,352,128]{2,1,0:T(8,128)(2,1)S(1)} all-to-all(bf16[8,352,128]{2,1,0:T(8,128)(2,1)S(1)} %get-tuple-element.58), channel_id=1, replica_groups=mesh['dp'=8,'cent'=16] {'dp'}, dimensions={0} | all-to-all | bytes 1441792 | tf_op jit(solution)/shard_map/all_to_all | solution.py:373
  65.7 0.0 copy-done.3
  65.7 12.2 %second.1 = (bf16[8192,128]{1,0:T(8,128)(2,1)S(1)}, bf16[2048,1024]{1,0:T(8,128)(2,1)S(1)}, bf16[2048,1024]{1,0:T(8,128)(2,1)S(1)}, bf16[2048,1024]{1,0:T(8,128)...) custom-call(bf16[8,352,128]{2,1,0:T(8,128)(2,1)S(1)} %all_to_all.31., ...), custom_call_target="tpu_custom_call" | custom-call | flops 10000000000 | bytes 2097152 | tf_op jit(solution)/shard_map/second/pallas_call | solution.py:420
  77.9 0.0 copy-start.1
  77.9 1.3 %copy-done.1 = bf16[8192,128]{1,0:T(8,128)(2,1)} copy-done((bf16[8192,128]{1,0:T(8,128)(2,1)}, bf16[8192,128]{1,0:T(8,128)(2,1)S(1)}, u32[]{:S(2)}) %copy-start.1) | copy-done | bytes 2097176
  79.2 11.2 %all_to_all.32.refs_0_ = f32[16,16,128]{2,1,0:T(8,128)S(1)} all-to-all(f32[16,16,128]{2,1,0:T(8,128)S(1)} %get-tuple-element.62), channel_id=1, replica_groups=mesh['dp'=8,'cent'=16] {'cent'}, dimensions={0} | all-to-all | bytes 262144 | tf_op jit(solution)/shard_map/all_to_all | solution.py:373
  90.4 4.0 %columns1.1 = (bf16[8,352,128]{2,1,0:T(8,128)(2,1)S(1)}, f32[256,128]{1,0:T(8,128)S(1)}) custom-call(f32[16,16,128]{2,1,0:T(8,128)S(1)} %all_to_all.32.refs_0_, f32[2,256,128]{2,1,0:T(8,128)S(1)} %get-tuple-element.46.refs_1_, bf16[2,256,128]{2,1,0:T(8,128)(2,1)S(1)} %get-tuple-element.47.refs_2_.xs_in, bf16[2,32,128]{2,1,0:T(8,128)(2,1)S(1)} %get-tuple-element.48.refs_3_, ...), custom_call_target="tpu_custom_call" | custom-call | flops 1000000000 | bytes 2097152 | tf_op jit(solution)/shard_map/columns1/pallas_call | solution.py:407
  94.4 0.0 copy-start.2
  94.4 0.0 copy-start.6
  94.4 15.1 %all_to_all.33.rec = bf16[8,352,128]{2,1,0:T(8,128)(2,1)S(1)} all-to-all(bf16[8,352,128]{2,1,0:T(8,128)(2,1)S(1)} %get-tuple-element.72), channel_id=1, replica_groups=mesh['dp'=8,'cent'=16] {'dp'}, dimensions={0} | all-to-all | bytes 1441792 | tf_op jit(solution)/shard_map/all_to_all | solution.py:373
  109.5 2.3 %tail.1 = bf16[16,32,128]{2,1,0:T(8,128)(2,1)} custom-call(bf16[8,352,128]{2,1,0:T(8,128)(2,1)S(1)} %all_to_all.33.rec, f32[64,128]{1,0:T(8,128)S(1)} %bitcast.2, f32[64,128]{1,0:T(8,128)S(1)} %get-tuple-element.73.v_in, f32[2,8,256]{2,1,0:T(8,128)S(1)} %get-tuple-element.59.code_in, f32[2,256,128]{2,1,0:T(8,128)S(1)} %get-tuple-element.60.col_in, ...), custom_call_target="tpu_custom_call" | custom-call | flops 100000000 | bytes 2097152 | tf_op jit(solution)/shard_map/tail/pallas_call | solution.py:432
  111.8 3.5 %all-to-all-start.5 = ((bf16[16,32,128]{2,1,0:T(8,128)(2,1)}), bf16[16,32,128]{2,1,0:T(8,128)(2,1)S(1)}, u32[]{:S(2)}, u32[]{:S(2)}) async-start(bf16[16,32,128]{2,1,0:T(8,128)(2,1)} %tail.1), calls=%async_computation.5 | async-start | bytes 262144 | tf_op jit(solution)/shard_map/all_to_all | solution.py:373
  115.3 0.0 copy-done.2
  115.3 3.4 %last.1 = bf16[8192,128]{1,0:T(8,128)(2,1)} custom-call(bf16[8,352,128]{2,1,0:T(8,128)(2,1)S(1)} %all_to_all.33.rec, f32[64,128]{1,0:T(8,128)S(1)} %bitcast.3, f32[64,128]{1,0:T(8,128)S(1)} %get-tuple-element.73.v_in, bf16[8192,128]{1,0:T(8,128)(2,1)S(1)} %copy-done.2), custom_call_target="tpu_custom_call" | custom-call | flops 1000000000 | bytes 2097152 | tf_op jit(solution)/shard_map/last/pallas_call | solution.py:437
  118.8 4.5 %all-to-all-done.5.rec = bf16[16,32,128]{2,1,0:T(8,128)(2,1)S(1)} async-done(((bf16[16,32,128]{2,1,0:T(8,128)(2,1)}), bf16[16,32,128]{2,1,0:T(8,128)(2,1)S(1)}, u32[]{:S(2)}, u32[]{:S(2)}) %all-to-all-start.5) | async-done | bytes 131104 | tf_op jit(solution)/shard_map/all_to_all | solution.py:373
  123.3 0.0 copy-done.6
  123.3 1.0 unpack.1
Async XLA Ops:
  0.6 0.8 copy-start.4
  1.4 0.7 copy-start.5
  3.1 19.4 %all-to-all-start = ((bf16[16,144,128]{2,1,0:T(8,128)(2,1)}), bf16[16,144,128]{2,1,0:T(8,128)(2,1)S(1)}, u32[]{:S(2)}, u32[]{:S(2)}) async-start(bf16[16,144,128]{2,1,0:T(8,128)(2,1)} %pack.1), calls=%async_computation | async-start | bytes 1179648 | tf_op jit(solution)/shard_map/all_to_all | solution.py:373
  10.2 1.6 %copy-start = (bf16[8192,128]{1,0:T(8,128)(2,1)S(1)}, bf16[8192,128]{1,0:T(8,128)(2,1)}, u32[]{:S(2)}) copy-start(bf16[8192,128]{1,0:T(8,128)(2,1)} %cent.1) | copy-start | bytes 6291460
  44.0 21.7 %copy-start.3 = (f32[8192]{0:T(1024)S(1)}, f32[8192]{0:T(1024)}, u32[]{:S(2)}) copy-start(f32[8192]{0:T(1024)} %param.6) | copy-start | bytes 98308
  77.9 1.3 %copy-start.1 = (bf16[8192,128]{1,0:T(8,128)(2,1)}, bf16[8192,128]{1,0:T(8,128)(2,1)S(1)}, u32[]{:S(2)}) copy-start(bf16[8192,128]{1,0:T(8,128)(2,1)S(1)} %get-tuple-element.77.old) | copy-start | bytes 6291460
  94.4 20.9 %copy-start.2 = (bf16[8192,128]{1,0:T(8,128)(2,1)S(1)}, bf16[8192,128]{1,0:T(8,128)(2,1)}, u32[]{:S(2)}) copy-start(bf16[8192,128]{1,0:T(8,128)(2,1)} %copy-done.1) | copy-start | bytes 6291460
  94.4 28.9 %copy-start.6 = (s32[2,128]{1,0:T(2,128)S(1)}, s32[2,128]{1,0:T(2,128)}, u32[]{:S(2)}) copy-start(s32[2,128]{1,0:T(2,128)} %asg.3) | copy-start | bytes 3076
  111.8 11.5 %all-to-all-start.5 = ((bf16[16,32,128]{2,1,0:T(8,128)(2,1)}), bf16[16,32,128]{2,1,0:T(8,128)(2,1)S(1)}, u32[]{:S(2)}, u32[]{:S(2)}) async-start(bf16[16,32,128]{2,1,0:T(8,128)(2,1)} %tail.1), calls=%async_computation.5 | async-start | bytes 262144 | tf_op jit(solution)/shard_map/all_to_all | solution.py:373

commit v5 on v4

--- a/solution.py
+++ b/solution.py
@@ -51,9 +51,10 @@
     )
 
 
-def call(body, outs, name, flops, limit, scratch=()):
+def call(body, outs, name, flops, limit, scratch=(), **specs):
     return pl.pallas_call(
         body,
+        **specs,
         out_shape=outs,
         scratch_shapes=list(scratch),
         name=name,
@@ -68,7 +69,15 @@
     return jax.ShapeDtypeStruct(dims, dtype)
 
 
-def pack_kernel(emb, asg, out):
+def pack_kernel(emb_hbm, asg_hbm, out, emb, asg, sems):
+    copies = [
+        pltpu.make_async_copy(emb_hbm, emb, sems.at[0]),
+        pltpu.make_async_copy(asg_hbm, asg, sems.at[1]),
+    ]
+    for c in copies:
+        c.start()
+    for c in copies:
+        c.wait()
     xn = unit(emb[...].astype(F32)).astype(BF16)
     rows = []
     for it in range(2):
@@ -182,8 +191,7 @@
     return jnp.where(j == want, 1.0, 0.0).astype(BF16)
 
 
-def slot_kernel(rec, cents, p_out, xs_out, id_out, code_out, col_out, cs_out):
-    me = lax.axis_index("dp")
+def slot_kernel(rec, cents, p_out, xs_out, id_out, col_out, cs_out):
     order = order_matrix(False)
     for it in range(2):
         base = TOK + 8 * it
@@ -212,13 +220,10 @@
         col_out[it] = col
         rhi = jnp.concatenate([dhi[0:128].T[0:1], dhi[128:256].T[0:1]], axis=1)
         rlo = jnp.concatenate([dlo[0:128].T[0:1], dlo[128:256].T[0:1]], axis=1)
-        code_out[it] = jnp.broadcast_to(rhi * 32.0 + rlo, (8, SL))
-        slot = iota((SL, SL), 0)
-        lane = jnp.where(iota((SL, SL), 1) == me * 32 + (slot & 31), 1.0, 0.0).astype(BF16)
+        lane = jnp.where(iota((SL, 128), 1) == (iota((SL, 128), 0) & 31), 1.0, 0.0).astype(BF16)
         own = iota((8, SL), 0) == (iota((8, SL), 1) >> 5)
         rows = jnp.concatenate([jnp.where(own, rhi, 0.0), jnp.where(own, rlo, 0.0)], axis=0)
-        ids = mm(rows.astype(BF16), lane)
-        id_out[it] = jnp.concatenate([ids[:, 0:128], ids[:, 128:256]], axis=0).astype(BF16)
+        id_out[it] = mm(rows.astype(BF16), lane).astype(BF16)
         if it == 0:
             for o in range(NO):
                 cs_out[o * 32 : (o + 1) * 32, :] = mm(
@@ -226,8 +231,8 @@
                 ).astype(BF16)
 
 
-def colsum_kernel(it, rowp, p_in, xs_in, ids_in, cs_in, *refs):
-    gs, out, w_out, ucol, tots = refs[:NO], refs[NO], refs[NO + 1], refs[NO + 2], refs[NO + 3]
+def colsum_kernel(it, rowp, p_in, xs_in, cs_in, meta, *refs):
+    gs, (out, w_out, ucol, tots) = refs[:NO], refs[NO:]
     u = 1.0 / jnp.sum(rowp[...], axis=0)
     for s in range(NC):
         ucol[s * 128 : (s + 1) * 128, :] = jnp.broadcast_to(u[s : s + 1, :], (128, 128)).T.astype(BF16)
@@ -263,110 +268,133 @@
     w = (CENTROIDS * jnp.exp2(aff * SCALE)) * us
     w_out[...] = w
     rows = (w * xs).astype(BF16)
-    tot = tots[...].astype(BF16)
+    if it == 0:
+        tot = tots[...].astype(BF16)
+    else:
+        got = jnp.concatenate([slot_values(o, meta, tots)[1] for o in range(NO)], axis=0)
+        tot = jnp.concatenate([got[:, 0:128], got[:, 128:256]], axis=0).astype(BF16)
+    base = tot.shape[0]
     for d in range(ND):
-        out[d, 0:64, :] = tot
-        out[d, 64:320, :] = rows
-        out[d, 320:352, :] = ids_in[it]
-
-
-def potentials(rec, target, vbuf, before=None):
-    tot = rec[0, 0:64, :].astype(F32)
-    for d in range(1, ND):
-        tot = tot + rec[d, 0:64, :].astype(F32)
-    v = target[...] * (TOKENS / CENTROIDS) / tot
-    if before is not None:
-        v = v * before[...]
-    vbuf[...] = v
-    ids = rec[0, 320:352, :].astype(F32)
-    for d in range(1, ND):
-        ids = ids + rec[d, 320:352, :].astype(F32)
-    hi = jnp.concatenate([ids[0:8], ids[16:24]], axis=1)
-    lo = jnp.concatenate([ids[8:16], ids[24:32]], axis=1)
-    return hi * 32.0 + lo
-
-
-def own_masses(vbuf, code_in, it, w):
-    code = code_in[it][0:1, :]
-    lid = (code - 1.0).astype(jnp.int32)
-    lid = jnp.where(code > 0.0, lid, 0)
-    owner = iota((1, SL), 1) >> 5
-    row = owner * 8 + (lid >> 7)
-    oh = jnp.where(iota((128, SL), 0) == (lid & 127), 1.0, 0.0).astype(BF16)
-    vhi, vlo = split(vbuf[...])
-    got = mm(vhi, oh) + mm(vlo, oh)
-    got = jnp.sum(jnp.where(iota((64, SL), 0) == row, got, 0.0), axis=0, keepdims=True)
-    return w * column(got)
-
-
-def slot_potentials(o, codes, vbuf):
+        out[d, 0:base, :] = tot
+        out[d, base : base + SL, :] = rows
+        if it == 0:
+            out[d, 320:336, :] = meta[0]
+            out[d, 336:352, :] = meta[1]
+
+
+def slot_codes(rec, base):
+    halves = []
+    for h in range(2):
+        tot = rec[4 * h, base : base + 16, :].astype(F32)
+        for q in range(1, 4):
+            tot = tot + pltpu.roll(rec[4 * h + q, base : base + 16, :].astype(F32), 32 * q, 1)
+        halves.append(tot)
+    both = jnp.concatenate(halves, axis=1)
+    return both[0:8] * 32.0 + both[8:16]
+
+
+def own_row(values):
+    at = lax.axis_index("dp") * 32 + (iota((SL, SL), 1) & 31)
+    pick = jnp.where(iota((SL, SL), 0) == at, 1.0, 0.0).astype(BF16)
+    hi, lo = split(values)
+    got = mm(jnp.concatenate([hi, lo], axis=0), pick)
+    got = got[0:8] + got[8:16]
+    own = iota((8, SL), 0) == (iota((8, SL), 1) >> 5)
+    return jnp.sum(jnp.where(own, got, 0.0), axis=0, keepdims=True)
+
+
+def slot_values(o, codes, table):
     pos = (codes[o : o + 1, :] - 1.0).astype(jnp.int32)
-    vhi, vlo = split(vbuf[o * 8 : (o + 1) * 8, :])
+    hi, lo = split(table[o * 8 : (o + 1) * 8, :])
     oh = jnp.where(iota((128, 256), 0) == (pos & 127), 1.0, 0.0).astype(BF16)
-    got = mm(vhi, oh) + mm(vlo, oh)
-    vs = jnp.sum(jnp.where(iota((8, 256), 0) == (pos >> 7), got, 0.0), axis=0, keepdims=True)
-    return pos, vs
-
-
-def slot_rows(o, rec):
-    return jnp.concatenate([rec[d, 64 + o * 32 : 96 + o * 32, :] for d in range(ND)], axis=0)
-
-
-def refine(o, rec, codes, vbuf, old, new):
-    pos, vs = slot_potentials(o, codes, vbuf)
-    rows = slot_rows(o, rec)
+    got = mm(jnp.concatenate([hi, lo], axis=0), oh)
+    got = got[0:8] + got[8:16]
+    val = jnp.sum(jnp.where(iota((8, 256), 0) == (pos >> 7), got, 0.0), axis=0, keepdims=True)
+    return pos, val
+
+
+def slot_rows(o, rec, base):
+    return jnp.concatenate(
+        [rec[d, base + o * 32 : base + (o + 1) * 32, :] for d in range(ND)], axis=0
+    )
+
+
+def refine(o, pos, vs, rows, old, new):
     oht = jnp.where(iota((KO, 256), 0) == pos, vs, 0.0).astype(BF16)
     at = slice(o * KO, (o + 1) * KO)
     z = old[at, :].astype(F32) + mm(oht, rows)
     new[at, :] = unit(z).astype(BF16)
 
 
-def second_kernel(rec, target, code_in, col_in, w_in, old, pay, *refs):
-    new, gs, row_out, mass_out, cs_out, v_out = refs[0], refs[1 : 1 + NO], *refs[1 + NO : 5 + NO]
-    x, acc, vbuf = refs[5 + NO :]
+def second_kernel(rec, target, col_in, w_in, old, pay, *refs):
+    gs, (new_hbm, row_out, mass_out, cs_out, code_out, tv_out) = refs[:NO], refs[NO : 6 + NO]
+    x, acc, vbuf, new, sem = refs[6 + NO :]
     score_rows(pay, x)
-    codes = potentials(rec, target, vbuf)
-    v_out[...] = vbuf[...]
-    logv = jnp.log2(vbuf[...])
-    mass_out[...] = own_masses(vbuf, code_in, 0, w_in[...])
+    tot = rec[0, 0:64, :].astype(F32)
+    for d in range(1, ND):
+        tot = tot + rec[d, 0:64, :].astype(F32)
+    goal = target[...] * (TOKENS / CENTROIDS)
+    v = goal / tot
+    vbuf[...] = v
+    logv = jnp.log2(v)
+    codes = slot_codes(rec, 320)
+    slots = [slot_values(o, codes, vbuf) for o in range(NO)]
+    for o in range(NO):
+        refine(o, *slots[o], slot_rows(o, rec, 64), old, new)
+    save = pltpu.make_async_copy(new, new_hbm, sem)
+    save.start()
+    vs = jnp.concatenate([val for _, val in slots], axis=0)
+    mass_out[...] = w_in[...] * column(own_row(vs))
+    codes = slot_codes(rec, 336)
+    code_out[...] = codes
+    vbuf[...] = goal * v
+    tv_out[...] = jnp.concatenate([slot_values(o, codes, vbuf)[1] for o in range(NO)], axis=0)
     col = col_in[1]
-    for o in range(NO):
-        refine(o, rec, codes, vbuf, old, new)
     for o in range(NO):
         cblk = new.at[o * KO : (o + 1) * KO]
         cs_out[o * 32 : (o + 1) * 32, :] = mm(owner_onehot(col, o), cblk[...]).astype(BF16)
         shift = jnp.concatenate([logv[o * 8 + q : o * 8 + q + 1, :] for q in range(8)], axis=1)
         score_block(x, cblk, gs[o], acc, shift, o == 0)
     finish_rows(acc, row_out)
-
-
-def tail_kernel(rec, target, v_in, code_in, col_in, xs_in, cs_in, w_in, mass1, out, vbuf):
-    codes = potentials(rec, target, vbuf, v_in)
-    mass2 = own_masses(vbuf, code_in, 1, w_in[...])
+    save.wait()
+
+
+def last_potentials(rec, codes, tv):
+    tot = rec[0, 0:16, :].astype(F32)
+    for d in range(1, ND):
+        tot = tot + rec[d, 0:16, :].astype(F32)
+    tot = jnp.concatenate([tot[0:8], tot[8:16]], axis=1)
+    some = codes[...] > 0.0
+    return jnp.where(some, tv[...] / jnp.where(some, tot, 1.0), 0.0)
+
+
+def tail_kernel(rec, codes, tv, col_in, xs_in, cs_in, w_in, mass1, out):
+    vs = last_potentials(rec, codes, tv)
+    mass2 = w_in[...] * column(own_row(vs))
     lane = iota((SL, 128), 1)
     m = jnp.where(lane == 0, mass1[...], jnp.where(lane == 1, mass2, 0.0))
+    pos = (codes[...] - 1.0).astype(jnp.int32)
     col = col_in[1]
     new = []
     for o in range(NO):
-        pos, vs = slot_potentials(o, codes, vbuf)
         mine = col[o * 32 : (o + 1) * 32, :] - 1.0
         mine = jnp.concatenate([mine, mine], axis=1).astype(jnp.int32)
-        oht = jnp.where(mine == pos, vs, 0.0).astype(BF16)
-        z = cs_in[o * 32 : (o + 1) * 32, :].astype(F32) + mm(oht, slot_rows(o, rec))
+        oht = jnp.where(mine == pos[o : o + 1, :], vs[o : o + 1, :], 0.0).astype(BF16)
+        z = cs_in[o * 32 : (o + 1) * 32, :].astype(F32) + mm(oht, slot_rows(o, rec, 16))
         new.append(unit(z).astype(BF16).astype(F32))
     r = xs_in[1].astype(F32) - jnp.concatenate(new, axis=0)
-    perm = order_matrix(True)
-    r = mm(perm, r.astype(BF16)).astype(BF16)
-    m = mm(perm, m.astype(BF16)).astype(BF16)
+    both = jnp.concatenate([r.astype(BF16), m.astype(BF16)], axis=1)
+    both = mm(order_matrix(True), both).astype(BF16)
     for s in range(NC):
-        out[s, 0:16, :] = r[s * 16 : (s + 1) * 16]
-        out[s, 16:32, :] = m[s * 16 : (s + 1) * 16]
-
-
-def last_kernel(rec, target, v_in, old, new, vbuf):
-    codes = potentials(rec, target, vbuf, v_in)
-    for o in range(NO):
-        refine(o, rec, codes, vbuf, old, new)
+        out[s, 0:16, :] = both[s * 16 : (s + 1) * 16, 0:128]
+        out[s, 16:32, :] = both[s * 16 : (s + 1) * 16, 128:256]
+
+
+def last_kernel(rec, codes, tv, old, new):
+    vs = last_potentials(rec, codes, tv)
+    pos = (codes[...] - 1.0).astype(jnp.int32)
+    for o in range(NO):
+        refine(o, pos[o : o + 1, :], vs[o : o + 1, :], slot_rows(o, rec, 16), old, new)
 
 
 def exchange(x, axis):
@@ -378,19 +406,23 @@
     gshape = tuple(pltpu.VMEM((T, KO), BF16) for _ in range(NO))
     sums = shape(NC, NC, 128)
     xacc = (pltpu.VMEM((T, 2 * D), BF16), pltpu.VMEM((T, 128), F32))
-    vbuf = (pltpu.VMEM((KC // 128, 128), F32),)
-    pay = call(pack_kernel, shape(NC, TOK + 16, 128, dtype=BF16), "pack", 10**6, 8)(
-        embeddings, assignments
-    )
+    pay = call(
+        pack_kernel,
+        shape(NC, TOK + 16, 128, dtype=BF16),
+        "pack",
+        10**6,
+        8,
+        (pltpu.VMEM((TOK, D), BF16), pltpu.VMEM((2, TOK), jnp.int32), pltpu.SemaphoreType.DMA((2,))),
+        in_specs=[pl.BlockSpec(memory_space=pl.ANY)] * 2,
+    )(embeddings, assignments)
     rec = exchange(pay, "cent")
     c0 = call(cent_kernel, shape(KC, D, dtype=BF16), "cents", 10**9, 12)(centroids)
-    p, xs, ids, code, col, cs = call(
+    p, xs, ids, col, cs = call(
         slot_kernel,
         (
             shape(2, SL, TOK),
             shape(2, SL, D, dtype=BF16),
-            shape(2, 32, 128, dtype=BF16),
-            shape(2, 8, SL),
+            shape(2, 16, 128, dtype=BF16),
             shape(2, SL, 128),
             shape(SL, D, dtype=BF16),
         ),
@@ -400,41 +432,49 @@
     )(rec, c0)
     rec, c0, xs = lax.optimization_barrier((rec, c0, xs))
 
-    def columns(it, rows, cs, g):
+    def columns(it, rows, cs, meta, g):
         def body(*refs):
             colsum_kernel(it, *refs)
 
         out, w = call(
             body,
-            (shape(ND, 352, 128, dtype=BF16), shape(SL, 128)),
+            (shape(ND, 272 if it else 352, 128, dtype=BF16), shape(SL, 128)),
             f"columns{it}",
             10**9,
             12,
             (pltpu.VMEM((T, 128), BF16), pltpu.VMEM((64, 128), F32)),
-        )(rows, p, xs, ids, cs, *g)
+        )(rows, p, xs, cs, meta, *g)
         return exchange(out, "dp"), w
 
     *g, rows = call(first_kernel, gshape + (sums,), "first", 10**10, 12, xacc)(rec, c0)
     rows = exchange(rows, "cent")
-    got, w = columns(0, rows, cs, g)
-    c1, *rest = call(
+    got, w = columns(0, rows, cs, ids, g)
+    vmem = pl.BlockSpec(memory_space=pltpu.VMEM)
+    *g, c1, rows, mass1, cs, codes, tv = call(
         second_kernel,
-        (shape(KC, D, dtype=BF16),) + gshape
-        + (sums, shape(SL, 128), shape(SL, D, dtype=BF16), shape(KC // 128, 128)),
+        gshape
+        + (
+            pltpu.HBM((KC, D), BF16),
+            sums,
+            shape(SL, 128),
+            shape(SL, D, dtype=BF16),
+            shape(NO, SL),
+            shape(NO, SL),
+        ),
         "second",
         10**10,
         12,
-        xacc + vbuf,
-    )(got, target, code, col, w, c0, rec)
-    g, (rows, mass1, cs, v1) = rest[:NO], rest[NO:]
+        xacc + (pltpu.VMEM((KC // 128, 128), F32), pltpu.VMEM((KC, D), BF16), pltpu.SemaphoreType.DMA),
+        out_specs=(vmem,) * NO + (pl.BlockSpec(memory_space=pltpu.HBM),) + (vmem,) * 5,
+    )(got, target, col, w, c0, rec)
     rows = exchange(rows, "cent")
-    got, w = columns(1, rows, cs, g)
-    out = call(tail_kernel, shape(NC, 32, 128, dtype=BF16), "tail", 10**8, 14, vbuf)(
-        got, target, v1, code, col, xs, cs, w, mass1
+    got, w = columns(1, rows, cs, codes, g)
+    out = call(tail_kernel, shape(NC, 32, 128, dtype=BF16), "tail", 10**8, 12)(
+        got, codes, tv, col, xs, cs, w, mass1
     )
     got, out = lax.optimization_barrier((got, out))
     back = exchange(out, "cent")
-    c2 = call(last_kernel, shape(KC, D, dtype=BF16), "last", 10**9, 14, vbuf)(got, target, v1, c1)
+    c2 = call(last_kernel, shape(KC, D, dtype=BF16), "last", 10**9, 12)(got, codes, tv, c1)
     mass, res = call(unpack_kernel, (shape(2, TOK), shape(TOK, D, dtype=BF16)), "unpack", 10**6, 8)(
         assignments, back
     )

time: 125 us -> 121 us (0.968)
  blocking collectives: 54.9 us -> 52.8 us
  Pallas kernels: 42.3 us -> 40.9 us
  local copies, waits for them, and re-layouts: 4.36 us -> 3.03 us
    all_to_all x4, blocking collectives: 54.9 us -> 52.8 us  [exchange(): return lax.all_to_all(x, axis, 0, 0, tiled=True)]
    pallas_call x6, Pallas kernels: 26.9 us -> 25.6 us  [the longest x1 12.3 us: on_device(): call(second_kernel, gshape + (pltpu.HBM((KC, D), BF16), sums, shape(SL, 1...]
    unnamed x14 -> x12, local copies, waits for them, and re-layouts: 4.36 us -> 3.03 us
where the time goes in v5:
time: 121 us; the launch traced here: 120 us
  blocking collectives  52.8 us (44%)
  Pallas kernels  40.9 us (34%)
  waiting for transfers between devices  11.8 us (10%)
  starting transfers between devices  10.6 us (9%)
  local copies, waits for them, and re-layouts  3.03 us (3%)
    all_to_all x4, blocking collectives, exchange(): return lax.all_to_all(x, axis, 0, 0, tiled=True)  52.8 us
    pallas_call x1, Pallas kernels, on_device(): call(second_kernel, gshape + (pltpu.HBM((KC, D), BF16), sums, shape(SL, 1...  12.3 us
    all_to_all x2, waiting for transfers between devices, exchange(): return lax.all_to_all(x, axis, 0, 0, tiled=True)  11.8 us
    all_to_all x2, starting transfers between devices, exchange(): return lax.all_to_all(x, axis, 0, 0, tiled=True)  10.6 us
    pallas_call x1, Pallas kernels, on_device(): call(first_kernel, gshape + (sums,), 'first', 10 ** 10, 12, xacc)(rec, c0)  9.17 us
    pallas_call x2, Pallas kernels, columns(): call(body, (shape(ND, 272 if it else 352, 128, dtype=BF16), shape(SL, 128...  8.06 us
    pallas_call x1, Pallas kernels, on_device(): call(cent_kernel, shape(KC, D, dtype=BF16), 'cents', 10 ** 9, 12)(centroids)  3.8 us
    unnamed x12, local copies, waits for them, and re-layouts  3.03 us
  transfers between devices with their start and end apart: 2, of which 2 were waited for; matrix products, arithmetic and copies ran while one was open for 0% of the time, Pallas kernels for 6%

profile of v5, /device:TPU:0, one launch (start us, length us, event | category | flops | bytes accessed | tf_op | source)
XLA Modules:
  0.0 120.0 jit_solution(383643925365547785)
XLA Ops:
  0.6 0.0 copy-start.2
  0.6 0.7 copy-done.2
  1.4 0.0 copy-start.3
  1.4 0.7 copy-done.3
  2.1 1.0 pack.1
  3.1 7.1 %all-to-all-start = ((bf16[16,144,128]{2,1,0:T(8,128)(2,1)}), bf16[16,144,128]{2,1,0:T(8,128)(2,1)S(1)}, u32[]{:S(2)}, u32[]{:S(2)}) async-start(bf16[16,144,128]{2,1,0:T(8,128)(2,1)} %pack.1), calls=%async_computation | async-start | bytes 1179648 | tf_op jit(solution)/shard_map/all_to_all | solution.py:401
  10.2 0.0 copy-start.1
  10.2 1.6 %copy-done.1 = bf16[8192,128]{1,0:T(8,128)(2,1)S(1)} copy-done((bf16[8192,128]{1,0:T(8,128)(2,1)S(1)}, bf16[8192,128]{1,0:T(8,128)(2,1)}, u32[]{:S(2)}) %copy-start.1) | copy-done | bytes 2097176
  11.8 3.8 %cents.1.old = bf16[8192,128]{1,0:T(8,128)(2,1)S(1)} custom-call(bf16[8192,128]{1,0:T(8,128)(2,1)S(1)} %copy-done.1), custom_call_target="tpu_custom_call" | custom-call | flops 1000000000 | bytes 2097152 | tf_op jit(solution)/shard_map/cents/pallas_call | solution.py:419
  15.6 6.8 %all-to-all-done.rec.pay = bf16[16,144,128]{2,1,0:T(8,128)(2,1)S(1)} async-done(((bf16[16,144,128]{2,1,0:T(8,128)(2,1)}), bf16[16,144,128]{2,1,0:T(8,128)(2,1)S(1)}, u32[]{:S(2)}, u32[]{:S(2)}) %all-to-all-start) | async-done | bytes 589856 | tf_op jit(solution)/shard_map/all_to_all | solution.py:401
  22.5 1.4 %slots.1 = (f32[2,256,128]{2,1,0:T(8,128)S(1)}, bf16[2,256,128]{2,1,0:T(8,128)(2,1)S(1)}, bf16[2,16,128]{2,1,0:T(8,128)(2,1)S(1)}, f32[2,256,128]{2,1,0:T(8,128)S(1)}, bf16[256,128]{1,0:T(8,128)(2,1)S(1)}) custom-call(bf16[16,144,128]{2,1,0:T(8,128)(2,1)S(1)} %all-to-all-done.rec.pay, bf16[8192,128]{1,0:T(8,128)(2,1)S(1)} %cents.1.old), custom_call_target="tpu_custom_call" | custom-call | flops 1000000000 | bytes 2097152 | tf_op jit(solution)/shard_map/slots/pallas_call | solution.py:420
  23.9 9.2 %first.1 = (bf16[2048,1024]{1,0:T(8,128)(2,1)S(1)}, bf16[2048,1024]{1,0:T(8,128)(2,1)S(1)}, bf16[2048,1024]{1,0:T(8,128)(2,1)S(1)}, bf16[2048,1024]{1,0:T(8,128)...) custom-call(bf16[16,144,128]{2,1,0:T(8,128)(2,1)S(1)} %all-to-all-do, ...), custom_call_target="tpu_custom_call" | custom-call | flops 10000000000 | bytes 2097152 | tf_op jit(solution)/shard_map/first/pallas_call | solution.py:449
  33.1 11.0 %all_to_all.30.refs_0_ = f32[16,16,128]{2,1,0:T(8,128)S(1)} all-to-all(f32[16,16,128]{2,1,0:T(8,128)S(1)} %get-tuple-element.45), channel_id=1, replica_groups=mesh['dp'=8,'cent'=16] {'cent'}, dimensions={0} | all-to-all | bytes 262144 | tf_op jit(solution)/shard_map/all_to_all | solution.py:401
  44.1 0.0 copy-start.5
  44.1 4.0 %columns0.1 = (bf16[8,352,128]{2,1,0:T(8,128)(2,1)S(1)}, f32[256,128]{1,0:T(8,128)S(1)}) custom-call(f32[16,16,128]{2,1,0:T(8,128)S(1)} %all_to_all.30.refs_0_, f32[2,256,128]{2,1,0:T(8,128)S(1)} %get-tuple-element.46.refs_1_, bf16[2,256,128]{2,1,0:T(8,128)(2,1)S(1)} %get-tuple-element.47.refs_2_.xs_in, bf16[256,128]{1,0:T(8,128)(2,1)S(1)} %get-tuple-element.48.refs_3_, ...), custom_call_target="tpu_custom_call" | custom-call | flops 1000000000 | bytes 2097152 | tf_op jit(solution)/shard_map/columns0/pallas_call | solution.py:439
  48.1 17.7 %all_to_all.31.rec = bf16[8,352,128]{2,1,0:T(8,128)(2,1)S(1)} all-to-all(bf16[8,352,128]{2,1,0:T(8,128)(2,1)S(1)} %get-tuple-element.58), channel_id=1, replica_groups=mesh['dp'=8,'cent'=16] {'dp'}, dimensions={0} | all-to-all | bytes 1441792 | tf_op jit(solution)/shard_map/all_to_all | solution.py:401
  65.7 0.0 copy-done.5
  65.7 12.3 %second.1 = (bf16[2048,1024]{1,0:T(8,128)(2,1)S(1)}, bf16[2048,1024]{1,0:T(8,128)(2,1)S(1)}, bf16[2048,1024]{1,0:T(8,128)(2,1)S(1)}, bf16[2048,1024]{1,0:T(8,128...) custom-call(bf16[8,352,128]{2,1,0:T(8,128)(2,1)S(1)} %all_to_all.31., ...), custom_call_target="tpu_custom_call" | custom-call | flops 10000000000 | bytes 2097152 | tf_op jit(solution)/shard_map/second/pallas_call | solution.py:453
  78.0 11.1 %all_to_all.32.refs_0_ = f32[16,16,128]{2,1,0:T(8,128)S(1)} all-to-all(f32[16,16,128]{2,1,0:T(8,128)S(1)} %get-tuple-element.61), channel_id=1, replica_groups=mesh['dp'=8,'cent'=16] {'cent'}, dimensions={0} | all-to-all | bytes 262144 | tf_op jit(solution)/shard_map/all_to_all | solution.py:401
  89.1 0.0 copy-start
  89.1 4.1 %columns1.1 = (bf16[8,272,128]{2,1,0:T(8,128)(2,1)S(1)}, f32[256,128]{1,0:T(8,128)S(1)}) custom-call(f32[16,16,128]{2,1,0:T(8,128)S(1)} %all_to_all.32.refs_0_, f32[2,256,128]{2,1,0:T(8,128)S(1)} %get-tuple-element.46.refs_1_, bf16[2,256,128]{2,1,0:T(8,128)(2,1)S(1)} %get-tuple-element.47.refs_2_.xs_in, ...), custom_call_target="tpu_custom_call" | custom-call | flops 1000000000 | bytes 2097152 | tf_op jit(solution)/shard_map/columns1/pallas_call | solution.py:439
  93.2 0.0 copy-start.4
  93.2 13.1 %all_to_all.33.rec = bf16[8,272,128]{2,1,0:T(8,128)(2,1)S(1)} all-to-all(bf16[8,272,128]{2,1,0:T(8,128)(2,1)S(1)} %get-tuple-element.72), channel_id=1, replica_groups=mesh['dp'=8,'cent'=16] {'dp'}, dimensions={0} | all-to-all | bytes 1114112 | tf_op jit(solution)/shard_map/all_to_all | solution.py:401
  106.3 1.2 %tail.1 = bf16[16,32,128]{2,1,0:T(8,128)(2,1)} custom-call(bf16[8,272,128]{2,1,0:T(8,128)(2,1)S(1)} %all_to_all.33.rec, f32[8,256]{1,0:T(8,128)S(1)} %get-tuple-element.63.refs_4_.codes, f32[8,256]{1,0:T(8,128)S(1)} %get-tuple-element.73.tv, f32[2,256,128]{2,1,0:T(8,128)S(1)} %get-tuple-element.59.col_in, ...), custom_call_target="tpu_custom_call" | custom-call | flops 100000000 | bytes 2097152 | tf_op jit(solution)/shard_map/tail/pallas_call | solution.py:472
  107.5 3.5 %all-to-all-start.5 = ((bf16[16,32,128]{2,1,0:T(8,128)(2,1)}), bf16[16,32,128]{2,1,0:T(8,128)(2,1)S(1)}, u32[]{:S(2)}, u32[]{:S(2)}) async-start(bf16[16,32,128]{2,1,0:T(8,128)(2,1)} %tail.1), calls=%async_computation.5 | async-start | bytes 262144 | tf_op jit(solution)/shard_map/all_to_all | solution.py:401
  111.1 0.0 copy-done
  111.1 2.9 %last.1 = bf16[8192,128]{1,0:T(8,128)(2,1)} custom-call(bf16[8,272,128]{2,1,0:T(8,128)(2,1)S(1)} %all_to_all.33.rec, f32[8,256]{1,0:T(8,128)S(1)} %get-tuple-element.63.refs_4_.codes, f32[8,256]{1,0:T(8,128)S(1)} %get-tuple-element.73.tv, bf16[8192,128]{1,0:T(8,128)(2,1)S(1)} %copy-done), custom_call_target="tpu_custom_call" | custom-call | flops 1000000000 | bytes 2097152 | tf_op jit(solution)/shard_map/last/pallas_call | solution.py:477
  114.0 5.0 %all-to-all-done.5.rec = bf16[16,32,128]{2,1,0:T(8,128)(2,1)S(1)} async-done(((bf16[16,32,128]{2,1,0:T(8,128)(2,1)}), bf16[16,32,128]{2,1,0:T(8,128)(2,1)S(1)}, u32[]{:S(2)}, u32[]{:S(2)}) %all-to-all-start.5) | async-done | bytes 131104 | tf_op jit(solution)/shard_map/all_to_all | solution.py:401
  119.0 0.0 copy-done.4
  119.0 1.0 unpack.1
Async XLA Ops:
  0.6 0.8 copy-start.2
  1.4 0.7 copy-start.3
  3.1 19.4 %all-to-all-start = ((bf16[16,144,128]{2,1,0:T(8,128)(2,1)}), bf16[16,144,128]{2,1,0:T(8,128)(2,1)S(1)}, u32[]{:S(2)}, u32[]{:S(2)}) async-start(bf16[16,144,128]{2,1,0:T(8,128)(2,1)} %pack.1), calls=%async_computation | async-start | bytes 1179648 | tf_op jit(solution)/shard_map/all_to_all | solution.py:401
  10.2 1.6 %copy-start.1 = (bf16[8192,128]{1,0:T(8,128)(2,1)S(1)}, bf16[8192,128]{1,0:T(8,128)(2,1)}, u32[]{:S(2)}) copy-start(bf16[8192,128]{1,0:T(8,128)(2,1)} %cent.1) | copy-start | bytes 6291460
  44.1 21.7 %copy-start.5 = (f32[8192]{0:T(1024)S(1)}, f32[8192]{0:T(1024)}, u32[]{:S(2)}) copy-start(f32[8192]{0:T(1024)} %param.6) | copy-start | bytes 98308
  89.1 22.0 %copy-start = (bf16[8192,128]{1,0:T(8,128)(2,1)S(1)}, bf16[8192,128]{1,0:T(8,128)(2,1)}, u32[]{:S(2)}) copy-start(bf16[8192,128]{1,0:T(8,128)(2,1)} %get-tuple-element.77.old) | copy-start | bytes 6291460
  93.2 25.9 %copy-start.4 = (s32[2,128]{1,0:T(2,128)S(1)}, s32[2,128]{1,0:T(2,128)}, u32[]{:S(2)}) copy-start(s32[2,128]{1,0:T(2,128)} %asg.1) | copy-start | bytes 3076
  107.5 11.5 %all-to-all-start.5 = ((bf16[16,32,128]{2,1,0:T(8,128)(2,1)}), bf16[16,32,128]{2,1,0:T(8,128)(2,1)S(1)}, u32[]{:S(2)}, u32[]{:S(2)}) async-start(bf16[16,32,128]{2,1,0:T(8,128)(2,1)} %tail.1), calls=%async_computation.5 | async-start | bytes 262144 | tf_op jit(solution)/shard_map/all_to_all | solution.py:401

commit v6 on v5

--- a/solution.py
+++ b/solution.py
@@ -160,13 +160,13 @@
     hi, lo = split(acc[...])
     one = jnp.ones((8, 128), BF16)
     r = mm(one, hi, NT) + mm(one, lo, NT)
-    r = jnp.concatenate([r[0:1, s * 128 : (s + 1) * 128] for s in range(NC)], axis=0)
+    r = jnp.concatenate([r[0:1, s * 128 : (s + 1) * 128] for s in range(NC)], axis=0).astype(BF16)
     for c in range(NC):
         out[c] = r
 
 
 def first_kernel(rec, cents, *refs):
-    gs, row_out, x, acc = refs[:NO], refs[NO], refs[NO + 1], refs[NO + 2]
+    gs, (x, row_out, acc) = refs[:NO], refs[NO:]
     score_rows(rec, x)
     for o in range(NO):
         score_block(x, cents.at[o * KO : (o + 1) * KO], gs[o], acc, None, o == 0)
@@ -193,6 +193,7 @@
 
 def slot_kernel(rec, cents, p_out, xs_out, id_out, col_out, cs_out):
     order = order_matrix(False)
+    ids = []
     for it in range(2):
         base = TOK + 8 * it
         place16 = iota((16, TOK), 0).astype(F32)
@@ -220,20 +221,22 @@
         col_out[it] = col
         rhi = jnp.concatenate([dhi[0:128].T[0:1], dhi[128:256].T[0:1]], axis=1)
         rlo = jnp.concatenate([dlo[0:128].T[0:1], dlo[128:256].T[0:1]], axis=1)
-        lane = jnp.where(iota((SL, 128), 1) == (iota((SL, 128), 0) & 31), 1.0, 0.0).astype(BF16)
+        at = (iota((SL, 128), 0) & 31) + 32 * it
+        lane = jnp.where(iota((SL, 128), 1) == at, 1.0, 0.0).astype(BF16)
         own = iota((8, SL), 0) == (iota((8, SL), 1) >> 5)
         rows = jnp.concatenate([jnp.where(own, rhi, 0.0), jnp.where(own, rlo, 0.0)], axis=0)
-        id_out[it] = mm(rows.astype(BF16), lane).astype(BF16)
+        ids.append(mm(rows.astype(BF16), lane))
         if it == 0:
             for o in range(NO):
                 cs_out[o * 32 : (o + 1) * 32, :] = mm(
                     owner_onehot(col, o), cents[o * KO : (o + 1) * KO, :]
                 ).astype(BF16)
+    id_out[...] = (ids[0] + ids[1]).astype(BF16)
 
 
 def colsum_kernel(it, rowp, p_in, xs_in, cs_in, meta, *refs):
     gs, (out, w_out, ucol, tots) = refs[:NO], refs[NO:]
-    u = 1.0 / jnp.sum(rowp[...], axis=0)
+    u = 1.0 / jnp.sum(rowp[...].astype(F32), axis=0)
     for s in range(NC):
         ucol[s * 128 : (s + 1) * 128, :] = jnp.broadcast_to(u[s : s + 1, :], (128, 128)).T.astype(BF16)
     W = 512
@@ -278,16 +281,18 @@
         out[d, 0:base, :] = tot
         out[d, base : base + SL, :] = rows
         if it == 0:
-            out[d, 320:336, :] = meta[0]
-            out[d, 336:352, :] = meta[1]
-
-
-def slot_codes(rec, base):
+            out[d, 320:336, :] = meta[...]
+
+
+def slot_codes(rec, it):
+    mine = (iota((16, 128), 1) >> 5) == it
     halves = []
     for h in range(2):
-        tot = rec[4 * h, base : base + 16, :].astype(F32)
-        for q in range(1, 4):
-            tot = tot + pltpu.roll(rec[4 * h + q, base : base + 16, :].astype(F32), 32 * q, 1)
+        tot = jnp.zeros((16, 128), F32)
+        for q in range(4):
+            ids = jnp.where(mine, rec[4 * h + q, 320:336, :].astype(F32), 0.0)
+            by = 32 * ((q - it) % 4)
+            tot = tot + (pltpu.roll(ids, by, 1) if by else ids)
         halves.append(tot)
     both = jnp.concatenate(halves, axis=1)
     return both[0:8] * 32.0 + both[8:16]
@@ -326,10 +331,9 @@
     new[at, :] = unit(z).astype(BF16)
 
 
-def second_kernel(rec, target, col_in, w_in, old, pay, *refs):
+def second_kernel(rec, target, col_in, w_in, old, x, *refs):
     gs, (new_hbm, row_out, mass_out, cs_out, code_out, tv_out) = refs[:NO], refs[NO : 6 + NO]
-    x, acc, vbuf, new, sem = refs[6 + NO :]
-    score_rows(pay, x)
+    acc, vbuf, new, sem = refs[6 + NO :]
     tot = rec[0, 0:64, :].astype(F32)
     for d in range(1, ND):
         tot = tot + rec[d, 0:64, :].astype(F32)
@@ -337,7 +341,7 @@
     v = goal / tot
     vbuf[...] = v
     logv = jnp.log2(v)
-    codes = slot_codes(rec, 320)
+    codes = slot_codes(rec, 0)
     slots = [slot_values(o, codes, vbuf) for o in range(NO)]
     for o in range(NO):
         refine(o, *slots[o], slot_rows(o, rec, 64), old, new)
@@ -345,7 +349,7 @@
     save.start()
     vs = jnp.concatenate([val for _, val in slots], axis=0)
     mass_out[...] = w_in[...] * column(own_row(vs))
-    codes = slot_codes(rec, 336)
+    codes = slot_codes(rec, 1)
     code_out[...] = codes
     vbuf[...] = goal * v
     tv_out[...] = jnp.concatenate([slot_values(o, codes, vbuf)[1] for o in range(NO)], axis=0)
@@ -404,8 +408,8 @@
 def on_device(embeddings, centroids, col_mass, assignments):
     target = col_mass.reshape(KC // 128, 128)
     gshape = tuple(pltpu.VMEM((T, KO), BF16) for _ in range(NO))
-    sums = shape(NC, NC, 128)
-    xacc = (pltpu.VMEM((T, 2 * D), BF16), pltpu.VMEM((T, 128), F32))
+    sums = shape(NC, NC, 128, dtype=BF16)
+    racc = (pltpu.VMEM((T, 128), F32),)
     pay = call(
         pack_kernel,
         shape(NC, TOK + 16, 128, dtype=BF16),
@@ -413,8 +417,8 @@
         10**6,
         8,
         (pltpu.VMEM((TOK, D), BF16), pltpu.VMEM((2, TOK), jnp.int32), pltpu.SemaphoreType.DMA((2,))),
-        in_specs=[pl.BlockSpec(memory_space=pl.ANY)] * 2,
-    )(embeddings, assignments)
+        in_specs=[pl.BlockSpec(memory_space=pltpu.HBM)] * 2,
+    )(*(pltpu.with_memory_space_constraint(a, pltpu.HBM) for a in (embeddings, assignments)))
     rec = exchange(pay, "cent")
     c0 = call(cent_kernel, shape(KC, D, dtype=BF16), "cents", 10**9, 12)(centroids)
     p, xs, ids, col, cs = call(
@@ -422,7 +426,7 @@
         (
             shape(2, SL, TOK),
             shape(2, SL, D, dtype=BF16),
-            shape(2, 16, 128, dtype=BF16),
+            shape(16, 128, dtype=BF16),
             shape(2, SL, 128),
             shape(SL, D, dtype=BF16),
         ),
@@ -438,7 +442,7 @@
 
         out, w = call(
             body,
-            (shape(ND, 272 if it else 352, 128, dtype=BF16), shape(SL, 128)),
+            (shape(ND, 272 if it else 336, 128, dtype=BF16), shape(SL, 128)),
             f"columns{it}",
             10**9,
             12,
@@ -446,7 +450,9 @@
         )(rows, p, xs, cs, meta, *g)
         return exchange(out, "dp"), w
 
-    *g, rows = call(first_kernel, gshape + (sums,), "first", 10**10, 12, xacc)(rec, c0)
+    *g, x, rows = call(
+        first_kernel, gshape + (pltpu.VMEM((T, 2 * D), BF16), sums), "first", 10**10, 12, racc
+    )(rec, c0)
     rows = exchange(rows, "cent")
     got, w = columns(0, rows, cs, ids, g)
     vmem = pl.BlockSpec(memory_space=pltpu.VMEM)
@@ -464,9 +470,9 @@
         "second",
         10**10,
         12,
-        xacc + (pltpu.VMEM((KC // 128, 128), F32), pltpu.VMEM((KC, D), BF16), pltpu.SemaphoreType.DMA),
+        racc + (pltpu.VMEM((KC // 128, 128), F32), pltpu.VMEM((KC, D), BF16), pltpu.SemaphoreType.DMA),
         out_specs=(vmem,) * NO + (pl.BlockSpec(memory_space=pltpu.HBM),) + (vmem,) * 5,
-    )(got, target, col, w, c0, rec)
+    )(got, target, col, w, c0, x)
     rows = exchange(rows, "cent")
     got, w = columns(1, rows, cs, codes, g)
     out = call(tail_kernel, shape(NC, 32, 128, dtype=BF16), "tail", 10**8, 12)(

time: 121 us -> 119 us (0.983)
  local copies, waits for them, and re-layouts: 3.03 us -> 1.6 us
    unnamed x12 -> x8, local copies, waits for them, and re-layouts: 3.03 us -> 1.6 us
where the time goes in v6:
time: 119 us; the launch traced here: 118 us
  blocking collectives  51.9 us (44%)
  Pallas kernels  41.7 us (35%)
  waiting for transfers between devices  11.8 us (10%)
  starting transfers between devices  10.6 us (9%)
  local copies, waits for them, and re-layouts  1.6 us (1%)
    all_to_all x4, blocking collectives, exchange(): return lax.all_to_all(x, axis, 0, 0, tiled=True)  51.9 us
    pallas_call x1, Pallas kernels, on_device(): call(second_kernel, gshape + (pltpu.HBM((KC, D), BF16), sums, shape(SL, 1...  12.4 us
    all_to_all x2, waiting for transfers between devices, exchange(): return lax.all_to_all(x, axis, 0, 0, tiled=True)  11.8 us
    all_to_all x2, starting transfers between devices, exchange(): return lax.all_to_all(x, axis, 0, 0, tiled=True)  10.6 us
    pallas_call x1, Pallas kernels, on_device(): call(first_kernel, gshape + (pltpu.VMEM((T, 2 * D), BF16), sums), 'first'...  9.11 us
    pallas_call x2, Pallas kernels, columns(): call(body, (shape(ND, 272 if it else 336, 128, dtype=BF16), shape(SL, 128...  8.06 us
    pallas_call x1, Pallas kernels, on_device(): call(cent_kernel, shape(KC, D, dtype=BF16), 'cents', 10 ** 9, 12)(centroids)  3.8 us
    pallas_call x1, Pallas kernels, on_device(): call(last_kernel, shape(KC, D, dtype=BF16), 'last', 10 ** 9, 12)  2.94 us
  transfers between devices with their start and end apart: 2, of which 2 were waited for; matrix products, arithmetic and copies ran while one was open for 0% of the time, Pallas kernels for 6%

profile of v6, /device:TPU:0, one launch (start us, length us, event | category | flops | bytes accessed | tf_op | source)
XLA Modules:
  0.0 118.3 jit_solution(13848349015787733035)
XLA Ops:
  0.6 1.8 %pack.1 = bf16[16,144,128]{2,1,0:T(8,128)(2,1)} custom-call(bf16[128,128]{1,0:T(8,128)(2,1)} %emb_hbm.1, s32[2,128]{1,0:T(2,128)} %asg.1), custom_call_target="tpu_custom_call" | custom-call | flops 1000000 | bytes 2097152 | tf_op jit(solution)/shard_map/pack/pallas_call | solution.py:413
  2.4 7.1 %all-to-all-start = ((bf16[16,144,128]{2,1,0:T(8,128)(2,1)}), bf16[16,144,128]{2,1,0:T(8,128)(2,1)S(1)}, u32[]{:S(2)}, u32[]{:S(2)}) async-start(bf16[16,144,128]{2,1,0:T(8,128)(2,1)} %pack.1), calls=%async_computation | async-start | bytes 1179648 | tf_op jit(solution)/shard_map/all_to_all | solution.py:405
  9.5 0.0 copy-start.1
  9.6 1.6 %copy-done.1 = bf16[8192,128]{1,0:T(8,128)(2,1)S(1)} copy-done((bf16[8192,128]{1,0:T(8,128)(2,1)S(1)}, bf16[8192,128]{1,0:T(8,128)(2,1)}, u32[]{:S(2)}) %copy-start.1) | copy-done | bytes 2097176
  11.1 3.8 %cents.1.old = bf16[8192,128]{1,0:T(8,128)(2,1)S(1)} custom-call(bf16[8192,128]{1,0:T(8,128)(2,1)S(1)} %copy-done.1), custom_call_target="tpu_custom_call" | custom-call | flops 1000000000 | bytes 2097152 | tf_op jit(solution)/shard_map/cents/pallas_call | solution.py:423
  14.9 6.8 %all-to-all-done.rec = bf16[16,144,128]{2,1,0:T(8,128)(2,1)S(1)} async-done(((bf16[16,144,128]{2,1,0:T(8,128)(2,1)}), bf16[16,144,128]{2,1,0:T(8,128)(2,1)S(1)}, u32[]{:S(2)}, u32[]{:S(2)}) %all-to-all-start) | async-done | bytes 589856 | tf_op jit(solution)/shard_map/all_to_all | solution.py:405
  21.8 1.3 %slots.1 = (f32[2,256,128]{2,1,0:T(8,128)S(1)}, bf16[2,256,128]{2,1,0:T(8,128)(2,1)S(1)}, bf16[16,128]{1,0:T(8,128)(2,1)S(1)}, f32[2,256,128]{2,1,0:T(8,128)S(1)}, bf16[256,128]{1,0:T(8,128)(2,1)S(1)}) custom-call(bf16[16,144,128]{2,1,0:T(8,128)(2,1)S(1)} %all-to-all-done.rec, bf16[8192,128]{1,0:T(8,128)(2,1)S(1)} %cents.1.old), custom_call_target="tpu_custom_call" | custom-call | flops 1000000000 | bytes 2097152 | tf_op jit(solution)/shard_map/slots/pallas_call | solution.py:424
  23.1 9.1 %first.1 = (bf16[2048,1024]{1,0:T(8,128)(2,1)S(1)}, bf16[2048,1024]{1,0:T(8,128)(2,1)S(1)}, bf16[2048,1024]{1,0:T(8,128)(2,1)S(1)}, bf16[2048,1024]{1,0:T(8,128)...) custom-call(bf16[16,144,128]{2,1,0:T(8,128)(2,1)S(1)} %all-to-all-do, ...), custom_call_target="tpu_custom_call" | custom-call | flops 10000000000 | bytes 2097152 | tf_op jit(solution)/shard_map/first/pallas_call | solution.py:453
  32.2 10.7 %all_to_all.30.refs_0_ = bf16[16,16,128]{2,1,0:T(8,128)(2,1)S(1)} all-to-all(bf16[16,16,128]{2,1,0:T(8,128)(2,1)S(1)} %get-tuple-element.46), channel_id=1, replica_groups=mesh['dp'=8,'cent'=16] {'cent'}, dimensions={0} | all-to-all | bytes 131072 | tf_op jit(solution)/shard_map/all_to_all | solution.py:405
  42.9 0.0 copy-start.3
  42.9 4.0 %columns0.1 = (bf16[8,336,128]{2,1,0:T(8,128)(2,1)S(1)}, f32[256,128]{1,0:T(8,128)S(1)}) custom-call(bf16[16,16,128]{2,1,0:T(8,128)(2,1)S(1)} %all_to_all.30.refs_0_, f32[2,256,128]{2,1,0:T(8,128)S(1)} %get-tuple-element.47.refs_1_, bf16[2,256,128]{2,1,0:T(8,128)(2,1)S(1)} %get-tuple-element.48.refs_2_.xs_in, ...), custom_call_target="tpu_custom_call" | custom-call | flops 1000000000 | bytes 2097152 | tf_op jit(solution)/shard_map/columns0/pallas_call | solution.py:443
  46.9 17.3 %all_to_all.31.rec = bf16[8,336,128]{2,1,0:T(8,128)(2,1)S(1)} all-to-all(bf16[8,336,128]{2,1,0:T(8,128)(2,1)S(1)} %get-tuple-element.59), channel_id=1, replica_groups=mesh['dp'=8,'cent'=16] {'dp'}, dimensions={0} | all-to-all | bytes 1376256 | tf_op jit(solution)/shard_map/all_to_all | solution.py:405
  64.2 0.0 copy-done.3
  64.2 12.4 %second.1 = (bf16[2048,1024]{1,0:T(8,128)(2,1)S(1)}, bf16[2048,1024]{1,0:T(8,128)(2,1)S(1)}, bf16[2048,1024]{1,0:T(8,128)(2,1)S(1)}, bf16[2048,1024]{1,0:T(8,128...) custom-call(bf16[8,336,128]{2,1,0:T(8,128)(2,1)S(1)} %all_to_all.31., ...), custom_call_target="tpu_custom_call" | custom-call | flops 10000000000 | bytes 2097152 | tf_op jit(solution)/shard_map/second/pallas_call | solution.py:459
  76.6 10.8 %all_to_all.32.refs_0_ = bf16[16,16,128]{2,1,0:T(8,128)(2,1)S(1)} all-to-all(bf16[16,16,128]{2,1,0:T(8,128)(2,1)S(1)} %get-tuple-element.63), channel_id=1, replica_groups=mesh['dp'=8,'cent'=16] {'cent'}, dimensions={0} | all-to-all | bytes 131072 | tf_op jit(solution)/shard_map/all_to_all | solution.py:405
  87.4 0.0 copy-start
  87.4 4.1 %columns1.1 = (bf16[8,272,128]{2,1,0:T(8,128)(2,1)S(1)}, f32[256,128]{1,0:T(8,128)S(1)}) custom-call(bf16[16,16,128]{2,1,0:T(8,128)(2,1)S(1)} %all_to_all.32.refs_0_, f32[2,256,128]{2,1,0:T(8,128)S(1)} %get-tuple-element.47.refs_1_, bf16[2,256,128]{2,1,0:T(8,128)(2,1)S(1)} %get-tuple-element.48.refs_2_.xs_in, ...), custom_call_target="tpu_custom_call" | custom-call | flops 1000000000 | bytes 2097152 | tf_op jit(solution)/shard_map/columns1/pallas_call | solution.py:443
  91.5 0.0 copy-start.2
  91.5 13.1 %all_to_all.33.rec = bf16[8,272,128]{2,1,0:T(8,128)(2,1)S(1)} all-to-all(bf16[8,272,128]{2,1,0:T(8,128)(2,1)S(1)} %get-tuple-element.74), channel_id=1, replica_groups=mesh['dp'=8,'cent'=16] {'dp'}, dimensions={0} | all-to-all | bytes 1114112 | tf_op jit(solution)/shard_map/all_to_all | solution.py:405
  104.6 1.2 %tail.1 = bf16[16,32,128]{2,1,0:T(8,128)(2,1)} custom-call(bf16[8,272,128]{2,1,0:T(8,128)(2,1)S(1)} %all_to_all.33.rec, f32[8,256]{1,0:T(8,128)S(1)} %get-tuple-element.65.refs_4_.codes, f32[8,256]{1,0:T(8,128)S(1)} %get-tuple-element.75.tv, f32[2,256,128]{2,1,0:T(8,128)S(1)} %get-tuple-element.60.col_in, ...), custom_call_target="tpu_custom_call" | custom-call | flops 100000000 | bytes 2097152 | tf_op jit(solution)/shard_map/tail/pallas_call | solution.py:478
  105.9 3.5 %all-to-all-start.5 = ((bf16[16,32,128]{2,1,0:T(8,128)(2,1)}), bf16[16,32,128]{2,1,0:T(8,128)(2,1)S(1)}, u32[]{:S(2)}, u32[]{:S(2)}) async-start(bf16[16,32,128]{2,1,0:T(8,128)(2,1)} %tail.1), calls=%async_computation.5 | async-start | bytes 262144 | tf_op jit(solution)/shard_map/all_to_all | solution.py:405
  109.4 0.0 copy-done
  109.4 2.9 %last.1 = bf16[8192,128]{1,0:T(8,128)(2,1)} custom-call(bf16[8,272,128]{2,1,0:T(8,128)(2,1)S(1)} %all_to_all.33.rec, f32[8,256]{1,0:T(8,128)S(1)} %get-tuple-element.65.refs_4_.codes, f32[8,256]{1,0:T(8,128)S(1)} %get-tuple-element.75.tv, bf16[8192,128]{1,0:T(8,128)(2,1)S(1)} %copy-done), custom_call_target="tpu_custom_call" | custom-call | flops 1000000000 | bytes 2097152 | tf_op jit(solution)/shard_map/last/pallas_call | solution.py:483
  112.3 5.0 %all-to-all-done.5.rec = bf16[16,32,128]{2,1,0:T(8,128)(2,1)S(1)} async-done(((bf16[16,32,128]{2,1,0:T(8,128)(2,1)}), bf16[16,32,128]{2,1,0:T(8,128)(2,1)S(1)}, u32[]{:S(2)}, u32[]{:S(2)}) %all-to-all-start.5) | async-done | bytes 131104 | tf_op jit(solution)/shard_map/all_to_all | solution.py:405
  117.3 0.0 copy-done.2
  117.3 1.0 unpack.1
Async XLA Ops:
  2.4 19.4 %all-to-all-start = ((bf16[16,144,128]{2,1,0:T(8,128)(2,1)}), bf16[16,144,128]{2,1,0:T(8,128)(2,1)S(1)}, u32[]{:S(2)}, u32[]{:S(2)}) async-start(bf16[16,144,128]{2,1,0:T(8,128)(2,1)} %pack.1), calls=%async_computation | async-start | bytes 1179648 | tf_op jit(solution)/shard_map/all_to_all | solution.py:405
  9.5 1.6 %copy-start.1 = (bf16[8192,128]{1,0:T(8,128)(2,1)S(1)}, bf16[8192,128]{1,0:T(8,128)(2,1)}, u32[]{:S(2)}) copy-start(bf16[8192,128]{1,0:T(8,128)(2,1)} %cent.1) | copy-start | bytes 6291460
  42.9 21.3 %copy-start.3 = (f32[8192]{0:T(1024)S(1)}, f32[8192]{0:T(1024)}, u32[]{:S(2)}) copy-start(f32[8192]{0:T(1024)} %param.6) | copy-start | bytes 98308
  87.4 22.0 %copy-start = (bf16[8192,128]{1,0:T(8,128)(2,1)S(1)}, bf16[8192,128]{1,0:T(8,128)(2,1)}, u32[]{:S(2)}) copy-start(bf16[8192,128]{1,0:T(8,128)(2,1)} %get-tuple-element.79.old) | copy-start | bytes 6291460
  91.5 25.8 %copy-start.2 = (s32[2,128]{1,0:T(2,128)S(1)}, s32[2,128]{1,0:T(2,128)}, u32[]{:S(2)}) copy-start(s32[2,128]{1,0:T(2,128)} %asg.1) | copy-start | bytes 3076
  105.9 11.5 %all-to-all-start.5 = ((bf16[16,32,128]{2,1,0:T(8,128)(2,1)}), bf16[16,32,128]{2,1,0:T(8,128)(2,1)S(1)}, u32[]{:S(2)}, u32[]{:S(2)}) async-start(bf16[16,32,128]{2,1,0:T(8,128)(2,1)} %tail.1), calls=%async_computation.5 | async-start | bytes 262144 | tf_op jit(solution)/shard_map/all_to_all | solution.py:405

commit v7 on v6

--- a/solution.py
+++ b/solution.py
@@ -165,14 +165,6 @@
         out[c] = r
 
 
-def first_kernel(rec, cents, *refs):
-    gs, (x, row_out, acc) = refs[:NO], refs[NO:]
-    score_rows(rec, x)
-    for o in range(NO):
-        score_block(x, cents.at[o * KO : (o + 1) * KO], gs[o], acc, None, o == 0)
-    finish_rows(acc, row_out)
-
-
 def owner_onehot(idcol, o):
     ids = idcol[o * 32 : (o + 1) * 32, :]
     lane = iota((32, 128), 1).astype(F32)
@@ -191,7 +183,12 @@
     return jnp.where(j == want, 1.0, 0.0).astype(BF16)
 
 
-def slot_kernel(rec, cents, p_out, xs_out, id_out, col_out, cs_out):
+def affinity(xs, cs):
+    dot = jnp.sum(xs * cs, axis=1, keepdims=True)
+    return jnp.broadcast_to(CENTROIDS * jnp.exp2(dot * SCALE), (SL, 128))
+
+
+def slot_lists(rec, cents, p_out, xs_out, id_out, col_out, aff_out):
     order = order_matrix(False)
     ids = []
     for it in range(2):
@@ -227,14 +224,24 @@
         rows = jnp.concatenate([jnp.where(own, rhi, 0.0), jnp.where(own, rlo, 0.0)], axis=0)
         ids.append(mm(rows.astype(BF16), lane))
         if it == 0:
-            for o in range(NO):
-                cs_out[o * 32 : (o + 1) * 32, :] = mm(
-                    owner_onehot(col, o), cents[o * KO : (o + 1) * KO, :]
-                ).astype(BF16)
+            cs = [
+                mm(owner_onehot(col, o), cents[o * KO : (o + 1) * KO, :]) for o in range(NO)
+            ]
+            aff_out[...] = affinity(both[:, 0:128], jnp.concatenate(cs, axis=0))
     id_out[...] = (ids[0] + ids[1]).astype(BF16)
 
 
-def colsum_kernel(it, rowp, p_in, xs_in, cs_in, meta, *refs):
+def first_kernel(rec, cents, *refs):
+    gs, (x, row_out), slot_refs, acc = refs[:NO], refs[NO : NO + 2], refs[NO + 2 : -1], refs[-1]
+    score_rows(rec, x)
+    for o in range(NO):
+        score_block(x, cents.at[o * KO : (o + 1) * KO], gs[o], acc, None, o == 0)
+        if o == 0:
+            slot_lists(rec, cents, *slot_refs)
+    finish_rows(acc, row_out)
+
+
+def colsum_kernel(it, rowp, p_in, xs_in, aff_in, meta, *refs):
     gs, (out, w_out, ucol, tots) = refs[:NO], refs[NO:]
     u = 1.0 / jnp.sum(rowp[...].astype(F32), axis=0)
     for s in range(NC):
@@ -266,11 +273,9 @@
     uhi, ulo = split(jnp.broadcast_to(us, (SL, 128)))
     both = mm(order_matrix(False), jnp.concatenate([uhi, ulo], axis=1))
     us = both[:, 0:128] + both[:, 128:256]
-    xs = xs_in[it].astype(F32)
-    aff = jnp.sum(xs * cs_in[...].astype(F32), axis=1, keepdims=True)
-    w = (CENTROIDS * jnp.exp2(aff * SCALE)) * us
+    w = aff_in[...] * us
     w_out[...] = w
-    rows = (w * xs).astype(BF16)
+    rows = (w * xs_in[it].astype(F32)).astype(BF16)
     if it == 0:
         tot = tots[...].astype(BF16)
     else:
@@ -331,9 +336,9 @@
     new[at, :] = unit(z).astype(BF16)
 
 
-def second_kernel(rec, target, col_in, w_in, old, x, *refs):
-    gs, (new_hbm, row_out, mass_out, cs_out, code_out, tv_out) = refs[:NO], refs[NO : 6 + NO]
-    acc, vbuf, new, sem = refs[6 + NO :]
+def second_kernel(rec, target, col_in, xs_in, w_in, old, x, *refs):
+    gs, (new_hbm, row_out, mass_out, cs_out, aff_out, code_out, tv_out) = refs[:NO], refs[NO : 7 + NO]
+    acc, vbuf, new, sem = refs[7 + NO :]
     tot = rec[0, 0:64, :].astype(F32)
     for d in range(1, ND):
         tot = tot + rec[d, 0:64, :].astype(F32)
@@ -359,6 +364,7 @@
         cs_out[o * 32 : (o + 1) * 32, :] = mm(owner_onehot(col, o), cblk[...]).astype(BF16)
         shift = jnp.concatenate([logv[o * 8 + q : o * 8 + q + 1, :] for q in range(8)], axis=1)
         score_block(x, cblk, gs[o], acc, shift, o == 0)
+    aff_out[...] = affinity(xs_in[1].astype(F32), cs_out[...].astype(F32))
     finish_rows(acc, row_out)
     save.wait()
 
@@ -421,22 +427,26 @@
     )(*(pltpu.with_memory_space_constraint(a, pltpu.HBM) for a in (embeddings, assignments)))
     rec = exchange(pay, "cent")
     c0 = call(cent_kernel, shape(KC, D, dtype=BF16), "cents", 10**9, 12)(centroids)
-    p, xs, ids, col, cs = call(
-        slot_kernel,
-        (
+    *g, x, rows, p, xs, ids, col, aff = call(
+        first_kernel,
+        gshape
+        + (
+            pltpu.VMEM((T, 2 * D), BF16),
+            sums,
             shape(2, SL, TOK),
             shape(2, SL, D, dtype=BF16),
             shape(16, 128, dtype=BF16),
             shape(2, SL, 128),
-            shape(SL, D, dtype=BF16),
+            shape(SL, 128),
         ),
-        "slots",
-        10**9,
-        12,
+        "first",
+        10**10,
+        14,
+        racc,
     )(rec, c0)
-    rec, c0, xs = lax.optimization_barrier((rec, c0, xs))
-
-    def columns(it, rows, cs, meta, g):
+    rows = exchange(rows, "cent")
+
+    def columns(it, rows, aff, meta, g):
         def body(*refs):
             colsum_kernel(it, *refs)
 
@@ -447,16 +457,12 @@
             10**9,
             12,
             (pltpu.VMEM((T, 128), BF16), pltpu.VMEM((64, 128), F32)),
-        )(rows, p, xs, cs, meta, *g)
+        )(rows, p, xs, aff, meta, *g)
         return exchange(out, "dp"), w
 
-    *g, x, rows = call(
-        first_kernel, gshape + (pltpu.VMEM((T, 2 * D), BF16), sums), "first", 10**10, 12, racc
-    )(rec, c0)
-    rows = exchange(rows, "cent")
-    got, w = columns(0, rows, cs, ids, g)
+    got, w = columns(0, rows, aff, ids, g)
     vmem = pl.BlockSpec(memory_space=pltpu.VMEM)
-    *g, c1, rows, mass1, cs, codes, tv = call(
+    *g, c1, rows, mass1, cs, aff, codes, tv = call(
         second_kernel,
         gshape
         + (
@@ -464,6 +470,7 @@
             sums,
             shape(SL, 128),
             shape(SL, D, dtype=BF16),
+            shape(SL, 128),
             shape(NO, SL),
             shape(NO, SL),
         ),
@@ -471,10 +478,10 @@
         10**10,
         12,
         racc + (pltpu.VMEM((KC // 128, 128), F32), pltpu.VMEM((KC, D), BF16), pltpu.SemaphoreType.DMA),
-        out_specs=(vmem,) * NO + (pl.BlockSpec(memory_space=pltpu.HBM),) + (vmem,) * 5,
-    )(got, target, col, w, c0, x)
+        out_specs=(vmem,) * NO + (pl.BlockSpec(memory_space=pltpu.HBM),) + (vmem,) * 6,
+    )(got, target, col, xs, w, c0, x)
     rows = exchange(rows, "cent")
-    got, w = columns(1, rows, cs, codes, g)
+    got, w = columns(1, rows, aff, codes, g)
     out = call(tail_kernel, shape(NC, 32, 128, dtype=BF16), "tail", 10**8, 12)(
         got, codes, tv, col, xs, cs, w, mass1
     )

time: 119 us -> 120 us (level)
    pallas_call x2 -> x1, Pallas kernels: 10.5 us -> 10.4 us  [on_device(): call(first_kernel, gshape + (pltpu.VMEM((T, 2 * D), BF16), sums, shape(2,...]
where the time goes in v7:
time: 120 us; the launch traced here: 119 us
  blocking collectives  51.9 us (43%)
  Pallas kernels  42.4 us (35%)
  waiting for transfers between devices  11.8 us (10%)
  starting transfers between devices  10.6 us (9%)
  local copies, waits for them, and re-layouts  1.6 us (1%)
    all_to_all x4, blocking collectives, exchange(): return lax.all_to_all(x, axis, 0, 0, tiled=True)  51.9 us
    pallas_call x1, Pallas kernels, on_device(): call(second_kernel, gshape + (pltpu.HBM((KC, D), BF16), sums, shape(SL, 1...  13 us
    all_to_all x2, waiting for transfers between devices, exchange(): return lax.all_to_all(x, axis, 0, 0, tiled=True)  11.8 us
    all_to_all x2, starting transfers between devices, exchange(): return lax.all_to_all(x, axis, 0, 0, tiled=True)  10.6 us
    pallas_call x1, Pallas kernels, on_device(): call(first_kernel, gshape + (pltpu.VMEM((T, 2 * D), BF16), sums, shape(2,...  10.4 us
    pallas_call x2, Pallas kernels, columns(): call(body, (shape(ND, 272 if it else 336, 128, dtype=BF16), shape(SL, 128...  8.21 us
    pallas_call x1, Pallas kernels, on_device(): call(cent_kernel, shape(KC, D, dtype=BF16), 'cents', 10 ** 9, 12)(centroids)  3.8 us
    pallas_call x1, Pallas kernels, on_device(): call(last_kernel, shape(KC, D, dtype=BF16), 'last', 10 ** 9, 12)  2.94 us
  transfers between devices with their start and end apart: 2, of which 2 were waited for; matrix products, arithmetic and copies ran while one was open for 0% of the time, Pallas kernels for 6%

profile of v7, /device:TPU:0, one launch (start us, length us, event | category | flops | bytes accessed | tf_op | source)
XLA Modules:
  0.0 119.0 jit_solution(15498628726424952605)
XLA Ops:
  0.6 1.8 %pack.1 = bf16[16,144,128]{2,1,0:T(8,128)(2,1)} custom-call(bf16[128,128]{1,0:T(8,128)(2,1)} %emb_hbm.1, s32[2,128]{1,0:T(2,128)} %asg.1), custom_call_target="tpu_custom_call" | custom-call | flops 1000000 | bytes 2097152 | tf_op jit(solution)/shard_map/pack/pallas_call | solution.py:419
  2.4 7.1 %all-to-all-start = ((bf16[16,144,128]{2,1,0:T(8,128)(2,1)}), bf16[16,144,128]{2,1,0:T(8,128)(2,1)S(1)}, u32[]{:S(2)}, u32[]{:S(2)}) async-start(bf16[16,144,128]{2,1,0:T(8,128)(2,1)} %pack.1), calls=%async_computation | async-start | bytes 1179648 | tf_op jit(solution)/shard_map/all_to_all | solution.py:411
  9.5 0.0 copy-start.1
  9.6 1.6 %copy-done.1 = bf16[8192,128]{1,0:T(8,128)(2,1)S(1)} copy-done((bf16[8192,128]{1,0:T(8,128)(2,1)S(1)}, bf16[8192,128]{1,0:T(8,128)(2,1)}, u32[]{:S(2)}) %copy-start.1) | copy-done | bytes 2097176
  11.1 3.8 %cents.1.old = bf16[8192,128]{1,0:T(8,128)(2,1)S(1)} custom-call(bf16[8192,128]{1,0:T(8,128)(2,1)S(1)} %copy-done.1), custom_call_target="tpu_custom_call" | custom-call | flops 1000000000 | bytes 2097152 | tf_op jit(solution)/shard_map/cents/pallas_call | solution.py:429
  14.9 6.8 %all-to-all-done.rec = bf16[16,144,128]{2,1,0:T(8,128)(2,1)S(1)} async-done(((bf16[16,144,128]{2,1,0:T(8,128)(2,1)}), bf16[16,144,128]{2,1,0:T(8,128)(2,1)S(1)}, u32[]{:S(2)}, u32[]{:S(2)}) %all-to-all-start) | async-done | bytes 589856 | tf_op jit(solution)/shard_map/all_to_all | solution.py:411
  21.8 10.4 %first.1 = (bf16[2048,1024]{1,0:T(8,128)(2,1)S(1)}, bf16[2048,1024]{1,0:T(8,128)(2,1)S(1)}, bf16[2048,1024]{1,0:T(8,128)(2,1)S(1)}, bf16[2048,1024]{1,0:T(8,128)...) custom-call(bf16[16,144,128]{2,1,0:T(8,128)(2,1)S(1)} %all-to-all-do, ...), custom_call_target="tpu_custom_call" | custom-call | flops 10000000000 | bytes 2097152 | tf_op jit(solution)/shard_map/first/pallas_call | solution.py:430
  32.2 10.7 %all_to_all.30.refs_0_ = bf16[16,16,128]{2,1,0:T(8,128)(2,1)S(1)} all-to-all(bf16[16,16,128]{2,1,0:T(8,128)(2,1)S(1)} %get-tuple-element.41), channel_id=1, replica_groups=mesh['dp'=8,'cent'=16] {'cent'}, dimensions={0} | all-to-all | bytes 131072 | tf_op jit(solution)/shard_map/all_to_all | solution.py:411
  42.9 0.0 copy-start.3
  42.9 4.2 %columns0.1 = (bf16[8,336,128]{2,1,0:T(8,128)(2,1)S(1)}, f32[256,128]{1,0:T(8,128)S(1)}) custom-call(bf16[16,16,128]{2,1,0:T(8,128)(2,1)S(1)} %all_to_all.30.refs_0_, f32[2,256,128]{2,1,0:T(8,128)S(1)} %get-tuple-element.42.refs_1_, bf16[2,256,128]{2,1,0:T(8,128)(2,1)S(1)} %get-tuple-element.43.refs_2_.xs_in, f32[256,128]{1,0:T(8,128)S(1)} %get-tuple-element.44.refs_3_, ...), custom_call_target="tpu_custom_call" | custom-call | flops 1000000000 | bytes 2097152 | tf_op jit(solution)/shard_map/columns0/pallas_call | solution.py:453
  47.0 17.3 %all_to_all.31.rec = bf16[8,336,128]{2,1,0:T(8,128)(2,1)S(1)} all-to-all(bf16[8,336,128]{2,1,0:T(8,128)(2,1)S(1)} %get-tuple-element.54), channel_id=1, replica_groups=mesh['dp'=8,'cent'=16] {'dp'}, dimensions={0} | all-to-all | bytes 1376256 | tf_op jit(solution)/shard_map/all_to_all | solution.py:411
  64.3 0.0 copy-done.3
  64.3 13.0 %second.1 = (bf16[2048,1024]{1,0:T(8,128)(2,1)S(1)}, bf16[2048,1024]{1,0:T(8,128)(2,1)S(1)}, bf16[2048,1024]{1,0:T(8,128)(2,1)S(1)}, bf16[2048,1024]{1,0:T(8,128...) custom-call(bf16[8,336,128]{2,1,0:T(8,128)(2,1)S(1)} %all_to_all.31., ...), custom_call_target="tpu_custom_call" | custom-call | flops 10000000000 | bytes 2097152 | tf_op jit(solution)/shard_map/second/pallas_call | solution.py:465
  77.4 10.8 %all_to_all.32.refs_0_ = bf16[16,16,128]{2,1,0:T(8,128)(2,1)S(1)} all-to-all(bf16[16,16,128]{2,1,0:T(8,128)(2,1)S(1)} %get-tuple-element.58), channel_id=1, replica_groups=mesh['dp'=8,'cent'=16] {'cent'}, dimensions={0} | all-to-all | bytes 131072 | tf_op jit(solution)/shard_map/all_to_all | solution.py:411
  88.2 0.0 copy-start
  88.2 4.1 %columns1.1 = (bf16[8,272,128]{2,1,0:T(8,128)(2,1)S(1)}, f32[256,128]{1,0:T(8,128)S(1)}) custom-call(bf16[16,16,128]{2,1,0:T(8,128)(2,1)S(1)} %all_to_all.32.refs_0_, f32[2,256,128]{2,1,0:T(8,128)S(1)} %get-tuple-element.42.refs_1_, bf16[2,256,128]{2,1,0:T(8,128)(2,1)S(1)} %get-tuple-element.43.refs_2_.xs_in, f32[256,128]{1,0:T(8,128)S(1)} %get-tuple-element.59.refs_3_, ...), custom_call_target="tpu_custom_call" | custom-call | flops 1000000000 | bytes 2097152 | tf_op jit(solution)/shard_map/columns1/pallas_call | solution.py:453
  92.2 0.0 copy-start.2
  92.2 13.1 %all_to_all.33.rec = bf16[8,272,128]{2,1,0:T(8,128)(2,1)S(1)} all-to-all(bf16[8,272,128]{2,1,0:T(8,128)(2,1)S(1)} %get-tuple-element.69), channel_id=1, replica_groups=mesh['dp'=8,'cent'=16] {'dp'}, dimensions={0} | all-to-all | bytes 1114112 | tf_op jit(solution)/shard_map/all_to_all | solution.py:411
  105.4 1.2 %tail.1 = bf16[16,32,128]{2,1,0:T(8,128)(2,1)} custom-call(bf16[8,272,128]{2,1,0:T(8,128)(2,1)S(1)} %all_to_all.33.rec, f32[8,256]{1,0:T(8,128)S(1)} %get-tuple-element.60.refs_4_.codes, f32[8,256]{1,0:T(8,128)S(1)} %get-tuple-element.70.tv, f32[2,256,128]{2,1,0:T(8,128)S(1)} %get-tuple-element.55.col_in, ...), custom_call_target="tpu_custom_call" | custom-call | flops 100000000 | bytes 2097152 | tf_op jit(solution)/shard_map/tail/pallas_call | solution.py:485
  106.6 3.5 %all-to-all-start.5 = ((bf16[16,32,128]{2,1,0:T(8,128)(2,1)}), bf16[16,32,128]{2,1,0:T(8,128)(2,1)S(1)}, u32[]{:S(2)}, u32[]{:S(2)}) async-start(bf16[16,32,128]{2,1,0:T(8,128)(2,1)} %tail.1), calls=%async_computation.5 | async-start | bytes 262144 | tf_op jit(solution)/shard_map/all_to_all | solution.py:411
  110.1 0.0 copy-done
  110.1 2.9 %last.1 = bf16[8192,128]{1,0:T(8,128)(2,1)} custom-call(bf16[8,272,128]{2,1,0:T(8,128)(2,1)S(1)} %all_to_all.33.rec, f32[8,256]{1,0:T(8,128)S(1)} %get-tuple-element.60.refs_4_.codes, f32[8,256]{1,0:T(8,128)S(1)} %get-tuple-element.70.tv, bf16[8192,128]{1,0:T(8,128)(2,1)S(1)} %copy-done), custom_call_target="tpu_custom_call" | custom-call | flops 1000000000 | bytes 2097152 | tf_op jit(solution)/shard_map/last/pallas_call | solution.py:490
  113.1 5.0 %all-to-all-done.5.rec = bf16[16,32,128]{2,1,0:T(8,128)(2,1)S(1)} async-done(((bf16[16,32,128]{2,1,0:T(8,128)(2,1)}), bf16[16,32,128]{2,1,0:T(8,128)(2,1)S(1)}, u32[]{:S(2)}, u32[]{:S(2)}) %all-to-all-start.5) | async-done | bytes 131104 | tf_op jit(solution)/shard_map/all_to_all | solution.py:411
  118.1 0.0 copy-done.2
  118.1 1.0 unpack.1
Async XLA Ops:
  2.4 19.4 %all-to-all-start = ((bf16[16,144,128]{2,1,0:T(8,128)(2,1)}), bf16[16,144,128]{2,1,0:T(8,128)(2,1)S(1)}, u32[]{:S(2)}, u32[]{:S(2)}) async-start(bf16[16,144,128]{2,1,0:T(8,128)(2,1)} %pack.1), calls=%async_computation | async-start | bytes 1179648 | tf_op jit(solution)/shard_map/all_to_all | solution.py:411
  9.5 1.6 %copy-start.1 = (bf16[8192,128]{1,0:T(8,128)(2,1)S(1)}, bf16[8192,128]{1,0:T(8,128)(2,1)}, u32[]{:S(2)}) copy-start(bf16[8192,128]{1,0:T(8,128)(2,1)} %cent.1) | copy-start | bytes 6291460
  42.9 21.4 %copy-start.3 = (f32[8192]{0:T(1024)S(1)}, f32[8192]{0:T(1024)}, u32[]{:S(2)}) copy-start(f32[8192]{0:T(1024)} %param.6) | copy-start | bytes 98308
  88.2 22.0 %copy-start = (bf16[8192,128]{1,0:T(8,128)(2,1)S(1)}, bf16[8192,128]{1,0:T(8,128)(2,1)}, u32[]{:S(2)}) copy-start(bf16[8192,128]{1,0:T(8,128)(2,1)} %get-tuple-element.75.old) | copy-start | bytes 6291460
  92.2 25.8 %copy-start.2 = (s32[2,128]{1,0:T(2,128)S(1)}, s32[2,128]{1,0:T(2,128)}, u32[]{:S(2)}) copy-start(s32[2,128]{1,0:T(2,128)} %asg.1) | copy-start | bytes 3076
  106.6 11.5 %all-to-all-start.5 = ((bf16[16,32,128]{2,1,0:T(8,128)(2,1)}), bf16[16,32,128]{2,1,0:T(8,128)(2,1)S(1)}, u32[]{:S(2)}, u32[]{:S(2)}) async-start(bf16[16,32,128]{2,1,0:T(8,128)(2,1)} %tail.1), calls=%async_computation.5 | async-start | bytes 262144 | tf_op jit(solution)/shard_map/all_to_all | solution.py:411

commit v8 on v6

--- a/solution.py
+++ b/solution.py
@@ -17,7 +17,7 @@
 SL = 256
 SCALE = 20.0 * math.log2(math.e)
 TOKENS, CENTROIDS = 16384, 131072
-KW = 256
+TR = 256
 MIB = 2**20
 
 NN = (((1,), (0,)), ((), ()))
@@ -139,21 +139,21 @@
 
 
 def score_block(x, cblk, g, acc, shift, first):
-    part = None
-    for k in range(0, KO, KW):
-        c = cblk[k : k + KW, :]
-        e = mm(x[...], jnp.concatenate([c, c], axis=1), NT)
+    c = jnp.concatenate([cblk[...], cblk[...]], axis=1)
+    for r in range(0, T, TR):
+        at = slice(r, r + TR)
+        e = mm(x[at, :], c, NT)
         if shift is not None:
-            e = e + shift[:, k : k + KW]
+            e = e + shift
         e = jnp.exp2(e)
-        g[:, k : k + KW] = e.astype(BF16)
-        for q in range(0, KW, 128):
-            t = e[:, q : q + 128]
-            part = t if part is None else part + t
-    if first:
-        acc[...] = part
-    else:
-        acc[...] += part
+        g[at, :] = e.astype(BF16)
+        part = e[:, 0:128]
+        for q in range(128, KO, 128):
+            part = part + e[:, q : q + 128]
+        if first:
+            acc[at, :] = part
+        else:
+            acc[at, :] += part
 
 
 def finish_rows(acc, out):
@@ -248,8 +248,9 @@
                 uu = ucol[at, :]
                 prod = gs[o][at, h * W : (h + 1) * W] * jnp.concatenate([uu] * (W // 128), axis=1)
                 prod = prod[0:64] + prod[64:128]
-                prod = (prod[0:32] + prod[32:64]).astype(F32)
-                return acc + ((prod[0:8] + prod[8:16]) + (prod[16:24] + prod[24:32]))
+                prod = prod[0:32] + prod[32:64]
+                prod = (prod[0:16] + prod[16:32]).astype(F32)
+                return acc + (prod[0:8] + prod[8:16])
 
             acc = lax.fori_loop(0, T // 128, body, jnp.zeros((8, W), F32), unroll=8)
             tot = jnp.sum(acc, axis=0, keepdims=True)

time: 119 us -> 118 us (level)
  no operation moved by 1% of the time
where the time goes in v8:
time: 118 us; the launch traced here: 117 us
  blocking collectives  51.9 us (44%)
  Pallas kernels  40.8 us (35%)
  waiting for transfers between devices  11.8 us (10%)
  starting transfers between devices  10.6 us (9%)
  local copies, waits for them, and re-layouts  1.6 us (1%)
    all_to_all x4, blocking collectives, exchange(): return lax.all_to_all(x, axis, 0, 0, tiled=True)  51.9 us
    pallas_call x1, Pallas kernels, on_device(): call(second_kernel, gshape + (pltpu.HBM((KC, D), BF16), sums, shape(SL, 1...  12.1 us
    all_to_all x2, waiting for transfers between devices, exchange(): return lax.all_to_all(x, axis, 0, 0, tiled=True)  11.8 us
    all_to_all x2, starting transfers between devices, exchange(): return lax.all_to_all(x, axis, 0, 0, tiled=True)  10.6 us
    pallas_call x1, Pallas kernels, on_device(): call(first_kernel, gshape + (pltpu.VMEM((T, 2 * D), BF16), sums), 'first'...  9.17 us
    pallas_call x2, Pallas kernels, columns(): call(body, (shape(ND, 272 if it else 336, 128, dtype=BF16), shape(SL, 128...  7.39 us
    pallas_call x1, Pallas kernels, on_device(): call(cent_kernel, shape(KC, D, dtype=BF16), 'cents', 10 ** 9, 12)(centroids)  3.8 us
    pallas_call x1, Pallas kernels, on_device(): call(last_kernel, shape(KC, D, dtype=BF16), 'last', 10 ** 9, 12)  2.94 us
  transfers between devices with their start and end apart: 2, of which 2 were waited for; matrix products, arithmetic and copies ran while one was open for 0% of the time, Pallas kernels for 6%

profile of v8, /device:TPU:0, one launch (start us, length us, event | category | flops | bytes accessed | tf_op | source)
XLA Modules:
  0.0 117.4 jit_solution(11577254754112964946)
XLA Ops:
  0.6 1.8 %pack.1 = bf16[16,144,128]{2,1,0:T(8,128)(2,1)} custom-call(bf16[128,128]{1,0:T(8,128)(2,1)} %emb_hbm.1, s32[2,128]{1,0:T(2,128)} %asg.1), custom_call_target="tpu_custom_call" | custom-call | flops 1000000 | bytes 2097152 | tf_op jit(solution)/shard_map/pack/pallas_call | solution.py:414
  2.4 7.1 %all-to-all-start = ((bf16[16,144,128]{2,1,0:T(8,128)(2,1)}), bf16[16,144,128]{2,1,0:T(8,128)(2,1)S(1)}, u32[]{:S(2)}, u32[]{:S(2)}) async-start(bf16[16,144,128]{2,1,0:T(8,128)(2,1)} %pack.1), calls=%async_computation | async-start | bytes 1179648 | tf_op jit(solution)/shard_map/all_to_all | solution.py:406
  9.5 0.0 copy-start.1
  9.6 1.6 %copy-done.1 = bf16[8192,128]{1,0:T(8,128)(2,1)S(1)} copy-done((bf16[8192,128]{1,0:T(8,128)(2,1)S(1)}, bf16[8192,128]{1,0:T(8,128)(2,1)}, u32[]{:S(2)}) %copy-start.1) | copy-done | bytes 2097176
  11.1 3.8 %cents.1.old = bf16[8192,128]{1,0:T(8,128)(2,1)S(1)} custom-call(bf16[8192,128]{1,0:T(8,128)(2,1)S(1)} %copy-done.1), custom_call_target="tpu_custom_call" | custom-call | flops 1000000000 | bytes 2097152 | tf_op jit(solution)/shard_map/cents/pallas_call | solution.py:424
  14.9 6.8 %all-to-all-done.rec = bf16[16,144,128]{2,1,0:T(8,128)(2,1)S(1)} async-done(((bf16[16,144,128]{2,1,0:T(8,128)(2,1)}), bf16[16,144,128]{2,1,0:T(8,128)(2,1)S(1)}, u32[]{:S(2)}, u32[]{:S(2)}) %all-to-all-start) | async-done | bytes 589856 | tf_op jit(solution)/shard_map/all_to_all | solution.py:406
  21.8 1.3 %slots.1 = (f32[2,256,128]{2,1,0:T(8,128)S(1)}, bf16[2,256,128]{2,1,0:T(8,128)(2,1)S(1)}, bf16[16,128]{1,0:T(8,128)(2,1)S(1)}, f32[2,256,128]{2,1,0:T(8,128)S(1)}, bf16[256,128]{1,0:T(8,128)(2,1)S(1)}) custom-call(bf16[16,144,128]{2,1,0:T(8,128)(2,1)S(1)} %all-to-all-done.rec, bf16[8192,128]{1,0:T(8,128)(2,1)S(1)} %cents.1.old), custom_call_target="tpu_custom_call" | custom-call | flops 1000000000 | bytes 2097152 | tf_op jit(solution)/shard_map/slots/pallas_call | solution.py:425
  23.1 9.2 %first.1 = (bf16[2048,1024]{1,0:T(8,128)(2,1)S(1)}, bf16[2048,1024]{1,0:T(8,128)(2,1)S(1)}, bf16[2048,1024]{1,0:T(8,128)(2,1)S(1)}, bf16[2048,1024]{1,0:T(8,128)...) custom-call(bf16[16,144,128]{2,1,0:T(8,128)(2,1)S(1)} %all-to-all-do, ...), custom_call_target="tpu_custom_call" | custom-call | flops 10000000000 | bytes 2097152 | tf_op jit(solution)/shard_map/first/pallas_call | solution.py:454
  32.3 10.7 %all_to_all.30.refs_0_ = bf16[16,16,128]{2,1,0:T(8,128)(2,1)S(1)} all-to-all(bf16[16,16,128]{2,1,0:T(8,128)(2,1)S(1)} %get-tuple-element.46), channel_id=1, replica_groups=mesh['dp'=8,'cent'=16] {'cent'}, dimensions={0} | all-to-all | bytes 131072 | tf_op jit(solution)/shard_map/all_to_all | solution.py:406
  43.0 0.0 copy-start.3
  43.0 3.7 %columns0.1 = (bf16[8,336,128]{2,1,0:T(8,128)(2,1)S(1)}, f32[256,128]{1,0:T(8,128)S(1)}) custom-call(bf16[16,16,128]{2,1,0:T(8,128)(2,1)S(1)} %all_to_all.30.refs_0_, f32[2,256,128]{2,1,0:T(8,128)S(1)} %get-tuple-element.47.refs_1_, bf16[2,256,128]{2,1,0:T(8,128)(2,1)S(1)} %get-tuple-element.48.refs_2_.xs_in, ...), custom_call_target="tpu_custom_call" | custom-call | flops 1000000000 | bytes 2097152 | tf_op jit(solution)/shard_map/columns0/pallas_call | solution.py:444
  46.6 17.3 %all_to_all.31.rec = bf16[8,336,128]{2,1,0:T(8,128)(2,1)S(1)} all-to-all(bf16[8,336,128]{2,1,0:T(8,128)(2,1)S(1)} %get-tuple-element.59), channel_id=1, replica_groups=mesh['dp'=8,'cent'=16] {'dp'}, dimensions={0} | all-to-all | bytes 1376256 | tf_op jit(solution)/shard_map/all_to_all | solution.py:406
  63.9 0.0 copy-done.3
  63.9 12.1 %second.1 = (bf16[2048,1024]{1,0:T(8,128)(2,1)S(1)}, bf16[2048,1024]{1,0:T(8,128)(2,1)S(1)}, bf16[2048,1024]{1,0:T(8,128)(2,1)S(1)}, bf16[2048,1024]{1,0:T(8,128...) custom-call(bf16[8,336,128]{2,1,0:T(8,128)(2,1)S(1)} %all_to_all.31., ...), custom_call_target="tpu_custom_call" | custom-call | flops 10000000000 | bytes 2097152 | tf_op jit(solution)/shard_map/second/pallas_call | solution.py:460
  76.1 10.8 %all_to_all.32.refs_0_ = bf16[16,16,128]{2,1,0:T(8,128)(2,1)S(1)} all-to-all(bf16[16,16,128]{2,1,0:T(8,128)(2,1)S(1)} %get-tuple-element.63), channel_id=1, replica_groups=mesh['dp'=8,'cent'=16] {'cent'}, dimensions={0} | all-to-all | bytes 131072 | tf_op jit(solution)/shard_map/all_to_all | solution.py:406
  86.9 0.0 copy-start
  86.9 3.7 %columns1.1 = (bf16[8,272,128]{2,1,0:T(8,128)(2,1)S(1)}, f32[256,128]{1,0:T(8,128)S(1)}) custom-call(bf16[16,16,128]{2,1,0:T(8,128)(2,1)S(1)} %all_to_all.32.refs_0_, f32[2,256,128]{2,1,0:T(8,128)S(1)} %get-tuple-element.47.refs_1_, bf16[2,256,128]{2,1,0:T(8,128)(2,1)S(1)} %get-tuple-element.48.refs_2_.xs_in, ...), custom_call_target="tpu_custom_call" | custom-call | flops 1000000000 | bytes 2097152 | tf_op jit(solution)/shard_map/columns1/pallas_call | solution.py:444
  90.6 0.0 copy-start.2
  90.6 13.1 %all_to_all.33.rec = bf16[8,272,128]{2,1,0:T(8,128)(2,1)S(1)} all-to-all(bf16[8,272,128]{2,1,0:T(8,128)(2,1)S(1)} %get-tuple-element.74), channel_id=1, replica_groups=mesh['dp'=8,'cent'=16] {'dp'}, dimensions={0} | all-to-all | bytes 1114112 | tf_op jit(solution)/shard_map/all_to_all | solution.py:406
  103.7 1.2 %tail.1 = bf16[16,32,128]{2,1,0:T(8,128)(2,1)} custom-call(bf16[8,272,128]{2,1,0:T(8,128)(2,1)S(1)} %all_to_all.33.rec, f32[8,256]{1,0:T(8,128)S(1)} %get-tuple-element.65.refs_4_.codes, f32[8,256]{1,0:T(8,128)S(1)} %get-tuple-element.75.tv, f32[2,256,128]{2,1,0:T(8,128)S(1)} %get-tuple-element.60.col_in, ...), custom_call_target="tpu_custom_call" | custom-call | flops 100000000 | bytes 2097152 | tf_op jit(solution)/shard_map/tail/pallas_call | solution.py:479
  105.0 3.5 %all-to-all-start.5 = ((bf16[16,32,128]{2,1,0:T(8,128)(2,1)}), bf16[16,32,128]{2,1,0:T(8,128)(2,1)S(1)}, u32[]{:S(2)}, u32[]{:S(2)}) async-start(bf16[16,32,128]{2,1,0:T(8,128)(2,1)} %tail.1), calls=%async_computation.5 | async-start | bytes 262144 | tf_op jit(solution)/shard_map/all_to_all | solution.py:406
  108.5 0.0 copy-done
  108.5 2.9 %last.1 = bf16[8192,128]{1,0:T(8,128)(2,1)} custom-call(bf16[8,272,128]{2,1,0:T(8,128)(2,1)S(1)} %all_to_all.33.rec, f32[8,256]{1,0:T(8,128)S(1)} %get-tuple-element.65.refs_4_.codes, f32[8,256]{1,0:T(8,128)S(1)} %get-tuple-element.75.tv, bf16[8192,128]{1,0:T(8,128)(2,1)S(1)} %copy-done), custom_call_target="tpu_custom_call" | custom-call | flops 1000000000 | bytes 2097152 | tf_op jit(solution)/shard_map/last/pallas_call | solution.py:484
  111.4 5.0 %all-to-all-done.5.rec = bf16[16,32,128]{2,1,0:T(8,128)(2,1)S(1)} async-done(((bf16[16,32,128]{2,1,0:T(8,128)(2,1)}), bf16[16,32,128]{2,1,0:T(8,128)(2,1)S(1)}, u32[]{:S(2)}, u32[]{:S(2)}) %all-to-all-start.5) | async-done | bytes 131104 | tf_op jit(solution)/shard_map/all_to_all | solution.py:406
  116.4 0.0 copy-done.2
  116.4 1.0 unpack.1
Async XLA Ops:
  2.4 19.4 %all-to-all-start = ((bf16[16,144,128]{2,1,0:T(8,128)(2,1)}), bf16[16,144,128]{2,1,0:T(8,128)(2,1)S(1)}, u32[]{:S(2)}, u32[]{:S(2)}) async-start(bf16[16,144,128]{2,1,0:T(8,128)(2,1)} %pack.1), calls=%async_computation | async-start | bytes 1179648 | tf_op jit(solution)/shard_map/all_to_all | solution.py:406
  9.5 1.6 %copy-start.1 = (bf16[8192,128]{1,0:T(8,128)(2,1)S(1)}, bf16[8192,128]{1,0:T(8,128)(2,1)}, u32[]{:S(2)}) copy-start(bf16[8192,128]{1,0:T(8,128)(2,1)} %cent.1) | copy-start | bytes 6291460
  43.0 20.9 %copy-start.3 = (f32[8192]{0:T(1024)S(1)}, f32[8192]{0:T(1024)}, u32[]{:S(2)}) copy-start(f32[8192]{0:T(1024)} %param.6) | copy-start | bytes 98308
  86.9 21.6 %copy-start = (bf16[8192,128]{1,0:T(8,128)(2,1)S(1)}, bf16[8192,128]{1,0:T(8,128)(2,1)}, u32[]{:S(2)}) copy-start(bf16[8192,128]{1,0:T(8,128)(2,1)} %get-tuple-element.79.old) | copy-start | bytes 6291460
  90.6 25.8 %copy-start.2 = (s32[2,128]{1,0:T(2,128)S(1)}, s32[2,128]{1,0:T(2,128)}, u32[]{:S(2)}) copy-start(s32[2,128]{1,0:T(2,128)} %asg.1) | copy-start | bytes 3076
  105.0 11.5 %all-to-all-start.5 = ((bf16[16,32,128]{2,1,0:T(8,128)(2,1)}), bf16[16,32,128]{2,1,0:T(8,128)(2,1)S(1)}, u32[]{:S(2)}, u32[]{:S(2)}) async-start(bf16[16,32,128]{2,1,0:T(8,128)(2,1)} %tail.1), calls=%async_computation.5 | async-start | bytes 262144 | tf_op jit(solution)/shard_map/all_to_all | solution.py:406

commit v9 on v8

--- a/solution.py
+++ b/solution.py
@@ -99,8 +99,7 @@
         out[c, TOK : TOK + 16, :] = jnp.concatenate(parts, axis=0).astype(F32).astype(BF16)
 
 
-def unpack_kernel(asg, rec, mass_out, res_out):
-    masses = []
+def place_kernel(asg, oh_out):
     for it in range(2):
         a = asg[it : it + 1, :]
         owner = a >> 10
@@ -108,21 +107,22 @@
         same = jnp.broadcast_to(own_f, (TOK, TOK)).T == own_f
         before = iota((TOK, TOK), 0) < iota((TOK, TOK), 1)
         rank = jnp.sum(jnp.where(same & before, 1.0, 0.0), axis=0, keepdims=True)
-        place = (owner.astype(F32) * 2.0 + rank) * 1.0
-        shard = a >> 13
-        row = shard.astype(F32) * 16.0 + (owner & 7).astype(F32) * 2.0 + rank
+        row = (a >> 13).astype(F32) * 16.0 + (owner & 7).astype(F32) * 2.0 + rank
         col = column(row)
         lane = iota((TOK, 128), 1).astype(F32)
-        oh = jnp.concatenate(
+        oh_out[it] = jnp.concatenate(
             [jnp.where(col == lane + 128.0 * j, 1.0, 0.0) for j in range(2)], axis=1
         ).astype(BF16)
-        mrows = jnp.concatenate([rec[s, 16:32, :] for s in range(NC)], axis=0)
-        m = mm(oh, mrows)
-        masses.append(m.T[it : it + 1, :])
-        if it == 1:
-            rrows = jnp.concatenate([rec[s, 0:16, :] for s in range(NC)], axis=0)
-            res_out[...] = mm(oh, rrows).astype(BF16)
-    mass_out[...] = jnp.concatenate(masses, axis=0)
+
+
+def unpack_kernel(oh, rec, mass_out, res_out):
+    mrows = jnp.concatenate([rec[s, 16:32, :] for s in range(NC)], axis=0)
+    rrows = jnp.concatenate([rec[s, 0:16, :] for s in range(NC)], axis=0)
+    res_out[...] = mm(oh[1], rrows).astype(BF16)
+    pick = jnp.where(iota((8, 128), 0) == iota((8, 128), 1), 1.0, 0.0).astype(BF16)
+    m = mm(pick, mrows, NT).astype(BF16)
+    mass_out[0:1, :] = mm(m, oh[0], NT)[0:1, :]
+    mass_out[1:2, :] = mm(m, oh[1], NT)[1:2, :]
 
 
 def cent_kernel(cent, out):
@@ -421,6 +421,7 @@
         in_specs=[pl.BlockSpec(memory_space=pltpu.HBM)] * 2,
     )(*(pltpu.with_memory_space_constraint(a, pltpu.HBM) for a in (embeddings, assignments)))
     rec = exchange(pay, "cent")
+    oh = call(place_kernel, shape(2, TOK, SL, dtype=BF16), "places", 10**6, 8)(assignments)
     c0 = call(cent_kernel, shape(KC, D, dtype=BF16), "cents", 10**9, 12)(centroids)
     p, xs, ids, col, cs = call(
         slot_kernel,
@@ -483,7 +484,7 @@
     back = exchange(out, "cent")
     c2 = call(last_kernel, shape(KC, D, dtype=BF16), "last", 10**9, 12)(got, codes, tv, c1)
     mass, res = call(unpack_kernel, (shape(2, TOK), shape(TOK, D, dtype=BF16)), "unpack", 10**6, 8)(
-        assignments, back
+        oh, back
     )
     return c2, mass, res
 

time: 118 us -> 118 us (level)
  no operation moved by 1% of the time
where the time goes in v9:
time: 118 us; the launch traced here: 117 us
  blocking collectives  51.9 us (44%)
  Pallas kernels  40.8 us (35%)
  waiting for transfers between devices  11.6 us (10%)
  starting transfers between devices  10.6 us (9%)
  local copies, waits for them, and re-layouts  1.6 us (1%)
    all_to_all x4, blocking collectives, exchange(): return lax.all_to_all(x, axis, 0, 0, tiled=True)  51.9 us
    pallas_call x1, Pallas kernels, on_device(): call(second_kernel, gshape + (pltpu.HBM((KC, D), BF16), sums, shape(SL, 1...  12.1 us
    all_to_all x2, waiting for transfers between devices, exchange(): return lax.all_to_all(x, axis, 0, 0, tiled=True)  11.6 us
    all_to_all x2, starting transfers between devices, exchange(): return lax.all_to_all(x, axis, 0, 0, tiled=True)  10.6 us
    pallas_call x1, Pallas kernels, on_device(): call(first_kernel, gshape + (pltpu.VMEM((T, 2 * D), BF16), sums), 'first'...  9.17 us
    pallas_call x2, Pallas kernels, columns(): call(body, (shape(ND, 272 if it else 336, 128, dtype=BF16), shape(SL, 128...  7.39 us
    pallas_call x1, Pallas kernels, on_device(): call(cent_kernel, shape(KC, D, dtype=BF16), 'cents', 10 ** 9, 12)(centroids)  3.8 us
    pallas_call x1, Pallas kernels, on_device(): call(last_kernel, shape(KC, D, dtype=BF16), 'last', 10 ** 9, 12)  2.94 us
  transfers between devices with their start and end apart: 2, of which 2 were waited for; matrix products, arithmetic and copies ran while one was open for 0% of the time, Pallas kernels for 6%

profile of v9, /device:TPU:0, one launch (start us, length us, event | category | flops | bytes accessed | tf_op | source)
XLA Modules:
  0.0 117.3 jit_solution(18081281122154607719)
XLA Ops:
  0.6 1.8 %pack.1 = bf16[16,144,128]{2,1,0:T(8,128)(2,1)} custom-call(bf16[128,128]{1,0:T(8,128)(2,1)} %emb_hbm.1, s32[2,128]{1,0:T(2,128)} %asg.1), custom_call_target="tpu_custom_call" | custom-call | flops 1000000 | bytes 2097152 | tf_op jit(solution)/shard_map/pack/pallas_call | solution.py:414
  2.4 7.1 %all-to-all-start = ((bf16[16,144,128]{2,1,0:T(8,128)(2,1)}), bf16[16,144,128]{2,1,0:T(8,128)(2,1)S(1)}, u32[]{:S(2)}, u32[]{:S(2)}) async-start(bf16[16,144,128]{2,1,0:T(8,128)(2,1)} %pack.1), calls=%async_computation | async-start | bytes 1179648 | tf_op jit(solution)/shard_map/all_to_all | solution.py:406
  9.5 0.0 copy-start.1
  9.6 1.6 %copy-done.1 = bf16[8192,128]{1,0:T(8,128)(2,1)S(1)} copy-done((bf16[8192,128]{1,0:T(8,128)(2,1)S(1)}, bf16[8192,128]{1,0:T(8,128)(2,1)}, u32[]{:S(2)}) %copy-start.1) | copy-done | bytes 2097176
  11.1 3.8 %cents.1.old = bf16[8192,128]{1,0:T(8,128)(2,1)S(1)} custom-call(bf16[8192,128]{1,0:T(8,128)(2,1)S(1)} %copy-done.1), custom_call_target="tpu_custom_call" | custom-call | flops 1000000000 | bytes 2097152 | tf_op jit(solution)/shard_map/cents/pallas_call | solution.py:425
  14.9 6.8 %all-to-all-done.rec = bf16[16,144,128]{2,1,0:T(8,128)(2,1)S(1)} async-done(((bf16[16,144,128]{2,1,0:T(8,128)(2,1)}), bf16[16,144,128]{2,1,0:T(8,128)(2,1)S(1)}, u32[]{:S(2)}, u32[]{:S(2)}) %all-to-all-start) | async-done | bytes 589856 | tf_op jit(solution)/shard_map/all_to_all | solution.py:406
  21.8 1.3 %slots.1 = (f32[2,256,128]{2,1,0:T(8,128)S(1)}, bf16[2,256,128]{2,1,0:T(8,128)(2,1)S(1)}, bf16[16,128]{1,0:T(8,128)(2,1)S(1)}, f32[2,256,128]{2,1,0:T(8,128)S(1)}, bf16[256,128]{1,0:T(8,128)(2,1)S(1)}) custom-call(bf16[16,144,128]{2,1,0:T(8,128)(2,1)S(1)} %all-to-all-done.rec, bf16[8192,128]{1,0:T(8,128)(2,1)S(1)} %cents.1.old), custom_call_target="tpu_custom_call" | custom-call | flops 1000000000 | bytes 2097152 | tf_op jit(solution)/shard_map/slots/pallas_call | solution.py:426
  23.1 9.2 %first.1 = (bf16[2048,1024]{1,0:T(8,128)(2,1)S(1)}, bf16[2048,1024]{1,0:T(8,128)(2,1)S(1)}, bf16[2048,1024]{1,0:T(8,128)(2,1)S(1)}, bf16[2048,1024]{1,0:T(8,128)...) custom-call(bf16[16,144,128]{2,1,0:T(8,128)(2,1)S(1)} %all-to-all-do, ...), custom_call_target="tpu_custom_call" | custom-call | flops 10000000000 | bytes 2097152 | tf_op jit(solution)/shard_map/first/pallas_call | solution.py:455
  32.3 10.7 %all_to_all.30.refs_0_ = bf16[16,16,128]{2,1,0:T(8,128)(2,1)S(1)} all-to-all(bf16[16,16,128]{2,1,0:T(8,128)(2,1)S(1)} %get-tuple-element.46), channel_id=1, replica_groups=mesh['dp'=8,'cent'=16] {'cent'}, dimensions={0} | all-to-all | bytes 131072 | tf_op jit(solution)/shard_map/all_to_all | solution.py:406
  43.0 0.0 copy-start.3
  43.0 3.7 %columns0.1 = (bf16[8,336,128]{2,1,0:T(8,128)(2,1)S(1)}, f32[256,128]{1,0:T(8,128)S(1)}) custom-call(bf16[16,16,128]{2,1,0:T(8,128)(2,1)S(1)} %all_to_all.30.refs_0_, f32[2,256,128]{2,1,0:T(8,128)S(1)} %get-tuple-element.47.refs_1_, bf16[2,256,128]{2,1,0:T(8,128)(2,1)S(1)} %get-tuple-element.48.refs_2_.xs_in, ...), custom_call_target="tpu_custom_call" | custom-call | flops 1000000000 | bytes 2097152 | tf_op jit(solution)/shard_map/columns0/pallas_call | solution.py:445
  46.6 17.3 %all_to_all.31.rec = bf16[8,336,128]{2,1,0:T(8,128)(2,1)S(1)} all-to-all(bf16[8,336,128]{2,1,0:T(8,128)(2,1)S(1)} %get-tuple-element.59), channel_id=1, replica_groups=mesh['dp'=8,'cent'=16] {'dp'}, dimensions={0} | all-to-all | bytes 1376256 | tf_op jit(solution)/shard_map/all_to_all | solution.py:406
  63.9 0.0 copy-done.3
  63.9 12.1 %second.1 = (bf16[2048,1024]{1,0:T(8,128)(2,1)S(1)}, bf16[2048,1024]{1,0:T(8,128)(2,1)S(1)}, bf16[2048,1024]{1,0:T(8,128)(2,1)S(1)}, bf16[2048,1024]{1,0:T(8,128...) custom-call(bf16[8,336,128]{2,1,0:T(8,128)(2,1)S(1)} %all_to_all.31., ...), custom_call_target="tpu_custom_call" | custom-call | flops 10000000000 | bytes 2097152 | tf_op jit(solution)/shard_map/second/pallas_call | solution.py:461
  76.1 10.8 %all_to_all.32.refs_0_ = bf16[16,16,128]{2,1,0:T(8,128)(2,1)S(1)} all-to-all(bf16[16,16,128]{2,1,0:T(8,128)(2,1)S(1)} %get-tuple-element.63), channel_id=1, replica_groups=mesh['dp'=8,'cent'=16] {'cent'}, dimensions={0} | all-to-all | bytes 131072 | tf_op jit(solution)/shard_map/all_to_all | solution.py:406
  86.9 0.0 copy-start.2
  86.9 0.0 copy-start
  86.9 3.7 %columns1.1 = (bf16[8,272,128]{2,1,0:T(8,128)(2,1)S(1)}, f32[256,128]{1,0:T(8,128)S(1)}) custom-call(bf16[16,16,128]{2,1,0:T(8,128)(2,1)S(1)} %all_to_all.32.refs_0_, f32[2,256,128]{2,1,0:T(8,128)S(1)} %get-tuple-element.47.refs_1_, bf16[2,256,128]{2,1,0:T(8,128)(2,1)S(1)} %get-tuple-element.48.refs_2_.xs_in, ...), custom_call_target="tpu_custom_call" | custom-call | flops 1000000000 | bytes 2097152 | tf_op jit(solution)/shard_map/columns1/pallas_call | solution.py:445
  90.6 13.1 %all_to_all.33.rec = bf16[8,272,128]{2,1,0:T(8,128)(2,1)S(1)} all-to-all(bf16[8,272,128]{2,1,0:T(8,128)(2,1)S(1)} %get-tuple-element.74), channel_id=1, replica_groups=mesh['dp'=8,'cent'=16] {'dp'}, dimensions={0} | all-to-all | bytes 1114112 | tf_op jit(solution)/shard_map/all_to_all | solution.py:406
  103.7 1.2 %tail.1 = bf16[16,32,128]{2,1,0:T(8,128)(2,1)} custom-call(bf16[8,272,128]{2,1,0:T(8,128)(2,1)S(1)} %all_to_all.33.rec, f32[8,256]{1,0:T(8,128)S(1)} %get-tuple-element.65.refs_4_.codes, f32[8,256]{1,0:T(8,128)S(1)} %get-tuple-element.75.tv, f32[2,256,128]{2,1,0:T(8,128)S(1)} %get-tuple-element.60.col_in, ...), custom_call_target="tpu_custom_call" | custom-call | flops 100000000 | bytes 2097152 | tf_op jit(solution)/shard_map/tail/pallas_call | solution.py:480
  105.0 3.5 %all-to-all-start.5 = ((bf16[16,32,128]{2,1,0:T(8,128)(2,1)}), bf16[16,32,128]{2,1,0:T(8,128)(2,1)S(1)}, u32[]{:S(2)}, u32[]{:S(2)}) async-start(bf16[16,32,128]{2,1,0:T(8,128)(2,1)} %tail.1), calls=%async_computation.5 | async-start | bytes 262144 | tf_op jit(solution)/shard_map/all_to_all | solution.py:406
  108.5 0.0 copy-done.2
  108.5 0.2 places.1.oh
  108.7 0.0 copy-done
  108.7 2.9 %last.1 = bf16[8192,128]{1,0:T(8,128)(2,1)} custom-call(bf16[8,272,128]{2,1,0:T(8,128)(2,1)S(1)} %all_to_all.33.rec, f32[8,256]{1,0:T(8,128)S(1)} %get-tuple-element.65.refs_4_.codes, f32[8,256]{1,0:T(8,128)S(1)} %get-tuple-element.75.tv, bf16[8192,128]{1,0:T(8,128)(2,1)S(1)} %copy-done), custom_call_target="tpu_custom_call" | custom-call | flops 1000000000 | bytes 2097152 | tf_op jit(solution)/shard_map/last/pallas_call | solution.py:485
  111.7 4.8 %all-to-all-done.5.rec = bf16[16,32,128]{2,1,0:T(8,128)(2,1)S(1)} async-done(((bf16[16,32,128]{2,1,0:T(8,128)(2,1)}), bf16[16,32,128]{2,1,0:T(8,128)(2,1)S(1)}, u32[]{:S(2)}, u32[]{:S(2)}) %all-to-all-start.5) | async-done | bytes 131104 | tf_op jit(solution)/shard_map/all_to_all | solution.py:406
  116.4 0.8 unpack.1
Async XLA Ops:
  2.4 19.4 %all-to-all-start = ((bf16[16,144,128]{2,1,0:T(8,128)(2,1)}), bf16[16,144,128]{2,1,0:T(8,128)(2,1)S(1)}, u32[]{:S(2)}, u32[]{:S(2)}) async-start(bf16[16,144,128]{2,1,0:T(8,128)(2,1)} %pack.1), calls=%async_computation | async-start | bytes 1179648 | tf_op jit(solution)/shard_map/all_to_all | solution.py:406
  9.5 1.6 %copy-start.1 = (bf16[8192,128]{1,0:T(8,128)(2,1)S(1)}, bf16[8192,128]{1,0:T(8,128)(2,1)}, u32[]{:S(2)}) copy-start(bf16[8192,128]{1,0:T(8,128)(2,1)} %cent.1) | copy-start | bytes 6291460
  43.0 20.9 %copy-start.3 = (f32[8192]{0:T(1024)S(1)}, f32[8192]{0:T(1024)}, u32[]{:S(2)}) copy-start(f32[8192]{0:T(1024)} %param.6) | copy-start | bytes 98308
  86.9 21.6 %copy-start.2 = (s32[2,128]{1,0:T(2,128)S(1)}, s32[2,128]{1,0:T(2,128)}, u32[]{:S(2)}) copy-start(s32[2,128]{1,0:T(2,128)} %asg.1) | copy-start | bytes 3076
  86.9 21.9 %copy-start = (bf16[8192,128]{1,0:T(8,128)(2,1)S(1)}, bf16[8192,128]{1,0:T(8,128)(2,1)}, u32[]{:S(2)}) copy-start(bf16[8192,128]{1,0:T(8,128)(2,1)} %get-tuple-element.79.old) | copy-start | bytes 6291460
  105.0 11.5 %all-to-all-start.5 = ((bf16[16,32,128]{2,1,0:T(8,128)(2,1)}), bf16[16,32,128]{2,1,0:T(8,128)(2,1)S(1)}, u32[]{:S(2)}, u32[]{:S(2)}) async-start(bf16[16,32,128]{2,1,0:T(8,128)(2,1)} %tail.1), calls=%async_computation.5 | async-start | bytes 262144 | tf_op jit(solution)/shard_map/all_to_all | solution.py:406
